TPU v7x, 32 devices: a whole 2x2x4 slice. The times are simulated.
32 devices in a mesh: groups: 2 (over x), seq: 16 (over z, y, core).
Axes of the slice: x: 2, y: 2, z: 4, core: 2. Of those that a mesh axis runs over, the one named last changes fastest.
Arguments:
- tenant_ids: int32 [8], P('groups'), parts along dimension 0, may hold values from 0 to 15
- timesteps: int32 [8], P('groups'), parts along dimension 0, may hold values from 0 to 999
- counts: int32 [32], P(('groups', 'seq')), parts along dimension 0, may hold values from 1 to 16
- hidden_in: bfloat16 [8, 1024, 3072], P('groups', 'seq'), parts along dimension 0, may hold values from -6 to 6
- frozen_query: bfloat16 [8, 1024, 3072], P('groups', 'seq'), parts along dimension 0, may hold values from -6 to 6
- key_base: bfloat16 [8, 1024, 3072], P('groups', 'seq'), parts along dimension 0, may hold values from -6 to 6
- frozen_value: bfloat16 [8, 1024, 3072], P('groups', 'seq'), parts along dimension 0, may hold values from -6 to 6
- out_grad: bfloat16 [8, 1024, 3072], P('groups', 'seq'), parts along dimension 0, may hold values from -6 to 6
- adapters: float32 [32, 4, 64, 3072], P(('groups', 'seq')), parts along dimension 0, may hold values from -0.625 to 0.625
- first_moment: float32 [32, 4, 64, 3072], P(('groups', 'seq')), parts along dimension 0, may hold values from -4 to 4
- second_moment: float32 [32, 4, 64, 3072], P(('groups', 'seq')), parts along dimension 0, may hold values from 0.01 to 1
Outputs:
- new_adapters: float32 [32, 4, 64, 3072], P(('groups', 'seq')), parts along dimension 0
- new_first: float32 [32, 4, 64, 3072], P(('groups', 'seq')), parts along dimension 0
- new_second: float32 [32, 4, 64, 3072], P(('groups', 'seq')), parts along dimension 0
There are 2 independent parts, one for each index of `groups`. A program takes and returns all parts, laid end to end along the dimension named above; each array names one. Nothing has to cross between parts.
All inputs are finite; a program needn't handle non-finite values.
Results may differ from a plain program's by a relative error of at most 0.0022.
Values may be sent and summed in bfloat16 or wider, within the bound.
No kernel may reach another device: no remote copies, remote signals or barrier semaphores. Data moves between devices by JAX's collectives and lax.ppermute only.
A program may use at most 128 MiB of HBM per device.

v0:
```python
import jax
import jax.numpy as jnp
from jax import lax
from jax.sharding import PartitionSpec as P

HEADS = 24
HD = 128


adapter_scale = 0.5
norm_eps = 1e-06
beta_one = 0.9
beta_two = 0.999
adam_eps = 1e-08
learn_rate = 0.01
adam_step = 100.0
num_steps = 1000.0


def from_root(block, axis, source):
    block = jnp.where(lax.axis_index(axis) == source, block, jnp.zeros_like(block))
    return lax.psum(block, axis)


def head_norm(field_in):
    shaped = field_in.reshape(field_in.shape[:-1] + (HEADS, HD))
    inverse = lax.rsqrt(jnp.mean(shaped * shaped, axis=-1, keepdims=True) + norm_eps)
    return (shaped * inverse, inverse)


def pair_grads(query_n, key_n, value_rows, upstream):
    seq_len = key_n.shape[0]
    row_block = min(512, seq_len)
    block_count = seq_len // row_block
    score_scale = HD ** (-0.5)

    def scan_step(dvalue_acc, operands):
        query_blk, upstream_blk = operands
        scores = jnp.dot(query_blk, key_n.T, preferred_element_type=jnp.float32) * score_scale
        exp_scores = jnp.exp(scores)
        attn_probs = exp_scores / jnp.sum(exp_scores, axis=-1, keepdims=True)
        probs_b = attn_probs.astype(jnp.bfloat16)
        attn_out = jnp.dot(probs_b, value_rows, preferred_element_type=jnp.float32)
        row_delta = jnp.sum(upstream_blk.astype(jnp.float32) * attn_out, axis=-1, keepdims=True)
        dprobs = jnp.dot(upstream_blk, value_rows.T, preferred_element_type=jnp.float32)
        dscores = (attn_probs * (dprobs - row_delta)).astype(jnp.bfloat16)
        dquery_blk = (
            jnp.dot(dscores, key_n, preferred_element_type=jnp.float32) * score_scale
        ).astype(jnp.bfloat16)
        dvalue_acc = dvalue_acc + jnp.einsum(
            "qk,qd->kd", probs_b, upstream_blk, preferred_element_type=jnp.float32
        )
        return (dvalue_acc, dquery_blk)

    dvalue_acc, dquery_n = lax.scan(
        scan_step,
        jnp.zeros((seq_len, key_n.shape[1]), jnp.float32),
        (query_n.reshape(block_count, row_block, -1), upstream.reshape(block_count, row_block, -1)),
    )
    return (dquery_n.reshape(seq_len, -1), dvalue_acc.astype(jnp.bfloat16))


def attend_items(operands):
    results = lax.map(
        lambda item_ops: pair_grads(*item_ops), tuple((member[0] for member in operands))
    )
    return tuple((result_item[None] for result_item in results))


def shards(
    tenant_ids,
    timesteps,
    counts,
    hidden_in,
    frozen_query,
    key_base,
    frozen_value,
    out_grad,
    adapters,
    first_moment,
    second_moment,
):
    image_count, tok_rows, model_dim = hidden_in.shape
    ten_dev = adapters.shape[0]
    seq_devices = lax.axis_size("seq")
    pair_count = image_count * HEADS
    per_device = pair_count // seq_devices
    fetched_list = []
    for picture_index in range(image_count):
        tenant = tenant_ids[picture_index]
        own_adapter = lax.dynamic_index_in_dim(
            adapters, tenant % ten_dev, 0, keepdims=False
        ).astype(jnp.bfloat16)
        fetched_list.append(from_root(own_adapter, "seq", tenant // ten_dev))
    loaded_adapters = jnp.stack(fetched_list)
    query_down_product = jnp.einsum(
        "itd,ird->itr", hidden_in, loaded_adapters[:, 0], preferred_element_type=jnp.float32
    ).astype(jnp.bfloat16)
    value_down_product = jnp.einsum(
        "itd,ird->itr", hidden_in, loaded_adapters[:, 2], preferred_element_type=jnp.float32
    ).astype(jnp.bfloat16)
    query_unscaled = frozen_query.astype(jnp.float32) + adapter_scale * jnp.einsum(
        "itr,ird->itd",
        query_down_product,
        loaded_adapters[:, 1],
        preferred_element_type=jnp.float32,
    )
    normed, inverse = head_norm(query_unscaled)
    query_n = normed.reshape(query_unscaled.shape).astype(jnp.bfloat16)
    key_normed, key_inverse = head_norm(key_base.astype(jnp.float32))
    key_n = key_normed.reshape(key_base.shape).astype(jnp.bfloat16)
    value_complete = (
        frozen_value.astype(jnp.float32)
        + adapter_scale
        * jnp.einsum(
            "itr,ird->itd",
            value_down_product,
            loaded_adapters[:, 3],
            preferred_element_type=jnp.float32,
        )
    ).astype(jnp.bfloat16)
    weight_t = 1.0 / (((timesteps.astype(jnp.float32) + 1.0) / num_steps) ** 2 + 0.25)
    upstream = (weight_t[:, None, None] * out_grad.astype(jnp.float32)).astype(jnp.bfloat16)

    def to_pairs_layout(tokens_major):
        return (
            tokens_major.reshape(image_count, tok_rows, HEADS, HD)
            .transpose(0, 2, 1, 3)
            .reshape(seq_devices, per_device, tok_rows, HD)
        )

    def from_pairs_layout(pairs_major):
        return (
            pairs_major.reshape(image_count, HEADS, tok_rows, HD)
            .transpose(0, 2, 1, 3)
            .reshape(image_count, tok_rows, model_dim)
        )

    dquery_p, dvalue_p = attend_items(
        (
            lax.all_to_all(
                to_pairs_layout(query_n), "seq", split_axis=0, concat_axis=2, tiled=True
            ),
            lax.all_to_all(to_pairs_layout(key_n), "seq", split_axis=0, concat_axis=2, tiled=True),
            lax.all_to_all(
                to_pairs_layout(value_complete), "seq", split_axis=0, concat_axis=2, tiled=True
            ),
            lax.all_to_all(
                to_pairs_layout(upstream), "seq", split_axis=0, concat_axis=2, tiled=True
            ),
        )
    )
    dquery_back, dvalue_back = (
        lax.all_to_all(dquery_p, "seq", split_axis=2, concat_axis=0, tiled=True),
        lax.all_to_all(dvalue_p, "seq", split_axis=2, concat_axis=0, tiled=True),
    )
    dvalue_tok = from_pairs_layout(dvalue_back)
    value_gradient_rows = jnp.einsum(
        "itd,ird->itr", dvalue_tok, loaded_adapters[:, 3], preferred_element_type=jnp.float32
    ).astype(jnp.bfloat16)
    value_up_gradient = adapter_scale * jnp.einsum(
        "itr,itd->ird", value_down_product, dvalue_tok, preferred_element_type=jnp.float32
    )
    dquery_f = (
        from_pairs_layout(dquery_back).astype(jnp.float32).reshape(image_count, tok_rows, HEADS, HD)
    )
    query_gradient = (
        (inverse * (dquery_f - normed * jnp.mean(dquery_f * normed, axis=-1, keepdims=True)))
        .reshape(image_count, tok_rows, model_dim)
        .astype(jnp.bfloat16)
    )
    query_gradient_rows = jnp.einsum(
        "itd,ird->itr", query_gradient, loaded_adapters[:, 1], preferred_element_type=jnp.float32
    ).astype(jnp.bfloat16)
    slots = jnp.stack(
        [
            adapter_scale
            * jnp.einsum(
                "itr,itd->ird", query_gradient_rows, hidden_in, preferred_element_type=jnp.float32
            ),
            adapter_scale
            * jnp.einsum(
                "itr,itd->ird",
                query_down_product,
                query_gradient,
                preferred_element_type=jnp.float32,
            ),
            adapter_scale
            * jnp.einsum(
                "itr,itd->ird", value_gradient_rows, hidden_in, preferred_element_type=jnp.float32
            ),
            value_up_gradient,
        ],
        axis=1,
    )
    summed = lax.psum(slots, "seq")
    owned_ids = lax.axis_index("seq") * ten_dev + jnp.arange(ten_dev, dtype=jnp.int32)
    owners = (tenant_ids[None, :] == owned_ids[:, None]).astype(jnp.float32)
    tenant_sum = jnp.einsum("ti,iabc->tabc", owners, summed, precision=lax.Precision.HIGHEST)
    tenant_grad = tenant_sum / counts.astype(jnp.float32)[:, None, None, None]
    new_first = beta_one * first_moment + (1.0 - beta_one) * tenant_grad
    new_second = beta_two * second_moment + (1.0 - beta_two) * tenant_grad * tenant_grad
    first_corr = 1.0 - beta_one**adam_step
    second_corr = 1.0 - beta_two**adam_step
    new_adapters = adapters - learn_rate * (new_first / first_corr) / (
        jnp.sqrt(new_second / second_corr) + adam_eps
    )
    return (new_adapters, new_first, new_second)


def solution(mesh):
    in_specs = (
        P("groups"),
        P("groups"),
        P(("groups", "seq")),
        P("groups", "seq", None),
        P("groups", "seq", None),
        P("groups", "seq", None),
        P("groups", "seq", None),
        P("groups", "seq", None),
        P(("groups", "seq"), None, None, None),
        P(("groups", "seq"), None, None, None),
        P(("groups", "seq"), None, None, None),
    )
    out_specs = (
        P(("groups", "seq"), None, None, None),
        P(("groups", "seq"), None, None, None),
        P(("groups", "seq"), None, None, None),
    )
    return jax.shard_map(shards, mesh=mesh, in_specs=in_specs, out_specs=out_specs, check_vma=False)
```

profile of v0, /device:TPU:0, one launch (start us, length us, event | category | flops | bytes accessed | tf_op | source)
XLA Modules:
  0.0 869.4 jit_solution(18087278794982869256)
XLA Ops:
  12.9 4.6 mul.140
  22.0 7.5 all-to-all-start.2
  32.7 3.2 broadcast_select_fusion
  36.0 2.3 broadcast_select_fusion.1
  42.9 29.2 %all-to-all-done.2 = bf16[16,6,64,128]{3,2,1,0:T(8,128)(2,1)S(1)} async-done(((bf16[16,6,64,128]{3,2,1,0:T(8,128)(2,1)}), bf16[16,6,64,128]{3,2,1,0:T(8,128)(2,1)S(1)}, u32[]{:S(2)}, u32[]{:S(2)}) %all-to-all-start.2) | async-done | bytes 1572896 | tf_op jit(solution)/shard_map/all_to_all | solution.py:144
  72.1 9.9 %all-to-all-start.1 = ((bf16[16,6,64,128]{3,2,1,0:T(8,128)(2,1)}), bf16[16,6,64,128]{3,2,1,0:T(8,128)(2,1)}, u32[]{:S(2)}, u32[]{:S(2)}) async-start(bf16[16,6,64,128]{3,2,1,0:T(8,128)(2,1)} %bitcast.267), calls=%async_computation.1 | async-start | bytes 3145728 | tf_op jit(solution)/shard_map/all_to_all | solution.py:148
  82.1 149.9 %all-reduce.6.cloned.1.call-done = (bf16[1,4,64,3072]{3,2,0,1:T(8,128)(2,1)}, bf16[1,4,64,3072]{3,2,0,1:T(8,128)(2,1)}, bf16[1,4,64,3072]{3,2,0,1:T(8,128)(2,1)}, bf16[1,4,64,3072]{3,2,0,1:T(8,128)(2,1)}) async-done(((bf16[1,4,64,3072]{3,2,0,1:T(8,128)(2,1)}, bf16[1,4,64,3072]{3,2,0,1:T(8,128)(2,1)}, bf16[1,4,64,3072]{3,2,0,1:T(8,128)(2,1)}, bf16[1,4,64,3072]{3,2,0,1:T(8,128)(2,1)}), ...) | async-done | bytes 6291472 | tf_op jit(solution)/shard_map/psum | solution.py:22
  240.7 4.8 all-to-all-start.3
  254.6 4.5 mul.133
  259.1 4.5 copy_bitcast_fusion.3
  263.6 14.0 %all-to-all-done.3 = bf16[16,6,64,128]{3,2,1,0:T(8,128)(2,1)} async-done(((bf16[16,6,64,128]{3,2,1,0:T(8,128)(2,1)}), bf16[16,6,64,128]{3,2,1,0:T(8,128)(2,1)}, u32[]{:S(2)}, u32[]{:S(2)}) %all-to-all-start.3) | async-done | bytes 1572896 | tf_op jit(solution)/shard_map/all_to_all | solution.py:145
  277.6 9.4 %all-to-all-start = ((bf16[16,6,64,128]{3,2,1,0:T(8,128)(2,1)}), bf16[16,6,64,128]{3,2,1,0:T(8,128)(2,1)}, u32[]{:S(2)}, u32[]{:S(2)}) async-start(bf16[16,6,64,128]{3,2,1,0:T(8,128)(2,1)} %bitcast.275), calls=%async_computation | async-start | bytes 3145728 | tf_op jit(solution)/shard_map/all_to_all | solution.py:141
  288.4 2.7 copy.128
  291.1 2.7 copy.135
  293.8 25.2 %all-to-all-done = bf16[16,6,64,128]{3,2,1,0:T(8,128)(2,1)} async-done(((bf16[16,6,64,128]{3,2,1,0:T(8,128)(2,1)}), bf16[16,6,64,128]{3,2,1,0:T(8,128)(2,1)}, u32[]{:S(2)}, u32[]{:S(2)}) %all-to-all-start) | async-done | bytes 1572896 | tf_op jit(solution)/shard_map/all_to_all | solution.py:141
  319.0 2.8 copy.126
  321.8 140.8 %while.26 = (s32[]{:T(128)}, bf16[6,1024,128]{2,1,0:T(8,128)(2,1)}, bf16[6,1024,128]{2,1,0:T(8,128)(2,1)}, bf16[6,1024,128]{2,1,0:T(8,128)(2,1)}, bf16[6,1024,12...) while((s32[]{:T(128)}, bf16[6,1024,128]{2,1,0:T(8,128)(2,1)}, ...), condition=%wide.region_11.12_spmd, body=%wide.region_6.11_spmd.sunk | while | flops 678624256 | bytes 15086400 | solution.py:64
  326.4 18.0 %while.27 = (s32[]{:T(128)}, f32[1024,128]{1,0:T(8,128)S(1)}, bf16[2,512,128]{2,1,0:T(8,128)(2,1)S(1)}, bf16[2,512,128]{2,1,0:T(8,128)(2,1)S(1)}, bf16[1024,128]...) while((s32[]{:T(128)}, f32[1024,128]{1,0:T(8,128)S(1)}, ...), condition=%wide.region_10.10_spmd.clone, body=%wide.region_7.9_spmd.clone.sunk | while | flops 678493184 | bytes 11677811 | solution.py:55
  330.5 2.6 fusion.102
  339.5 2.6 fusion.102
  349.9 18.0 %while.27 = (s32[]{:T(128)}, f32[1024,128]{1,0:T(8,128)S(1)}, bf16[2,512,128]{2,1,0:T(8,128)(2,1)S(1)}, bf16[2,512,128]{2,1,0:T(8,128)(2,1)S(1)}, bf16[1024,128]...) while((s32[]{:T(128)}, f32[1024,128]{1,0:T(8,128)S(1)}, ...), condition=%wide.region_10.10_spmd.clone, body=%wide.region_7.9_spmd.clone.sunk | while | flops 678493184 | bytes 11677811 | solution.py:55
  354.0 2.6 fusion.102
  363.0 2.6 fusion.102
  373.3 18.0 %while.27 = (s32[]{:T(128)}, f32[1024,128]{1,0:T(8,128)S(1)}, bf16[2,512,128]{2,1,0:T(8,128)(2,1)S(1)}, bf16[2,512,128]{2,1,0:T(8,128)(2,1)S(1)}, bf16[1024,128]...) while((s32[]{:T(128)}, f32[1024,128]{1,0:T(8,128)S(1)}, ...), condition=%wide.region_10.10_spmd.clone, body=%wide.region_7.9_spmd.clone.sunk | while | flops 678493184 | bytes 11677811 | solution.py:55
  377.4 2.6 fusion.102
  386.4 2.6 fusion.102
  396.8 18.0 %while.27 = (s32[]{:T(128)}, f32[1024,128]{1,0:T(8,128)S(1)}, bf16[2,512,128]{2,1,0:T(8,128)(2,1)S(1)}, bf16[2,512,128]{2,1,0:T(8,128)(2,1)S(1)}, bf16[1024,128]...) while((s32[]{:T(128)}, f32[1024,128]{1,0:T(8,128)S(1)}, ...), condition=%wide.region_10.10_spmd.clone, body=%wide.region_7.9_spmd.clone.sunk | while | flops 678493184 | bytes 11677811 | solution.py:55
  400.9 2.6 fusion.102
  409.9 2.6 fusion.102
  420.3 18.0 %while.27 = (s32[]{:T(128)}, f32[1024,128]{1,0:T(8,128)S(1)}, bf16[2,512,128]{2,1,0:T(8,128)(2,1)S(1)}, bf16[2,512,128]{2,1,0:T(8,128)(2,1)S(1)}, bf16[1024,128]...) while((s32[]{:T(128)}, f32[1024,128]{1,0:T(8,128)S(1)}, ...), condition=%wide.region_10.10_spmd.clone, body=%wide.region_7.9_spmd.clone.sunk | while | flops 678493184 | bytes 11677811 | solution.py:55
  424.4 2.6 fusion.102
  433.4 2.6 fusion.102
  435.9 2.3 convolution_add_fusion.2
  443.7 18.0 %while.27 = (s32[]{:T(128)}, f32[1024,128]{1,0:T(8,128)S(1)}, bf16[2,512,128]{2,1,0:T(8,128)(2,1)S(1)}, bf16[2,512,128]{2,1,0:T(8,128)(2,1)S(1)}, bf16[1024,128]...) while((s32[]{:T(128)}, f32[1024,128]{1,0:T(8,128)S(1)}, ...), condition=%wide.region_10.10_spmd.clone, body=%wide.region_7.9_spmd.clone.sunk | while | flops 678493184 | bytes 11677811 | solution.py:55
  447.8 2.6 fusion.102
  456.8 2.6 fusion.102
  462.6 3.8 copy.210
  466.4 9.3 %all-to-all-start.4 = ((bf16[1,6,1024,128]{3,1,0,2:T(8,128)(2,1)}), bf16[1,6,1024,128]{3,1,0,2:T(8,128)(2,1)}, u32[]{:S(2)}, u32[]{:S(2)}) async-start(bf16[1,6,1024,128]{3,1,0,2:T(8,128)(2,1)} %bitcast.263), calls=%async_computation.4 | async-start | bytes 4194304 | tf_op jit(solution)/shard_map/all_to_all | solution.py:154
  475.7 2.5 copy.209
  478.2 38.7 %all-to-all-done.4 = bf16[1,6,1024,128]{3,1,0,2:T(8,128)(2,1)} async-done(((bf16[1,6,1024,128]{3,1,0,2:T(8,128)(2,1)}), bf16[1,6,1024,128]{3,1,0,2:T(8,128)(2,1)}, u32[]{:S(2)}, u32[]{:S(2)}) %all-to-all-start.4) | async-done | bytes 1572896 | tf_op jit(solution)/shard_map/all_to_all | solution.py:154
  516.8 11.3 %all-to-all-start.5 = ((bf16[1,6,1024,128]{3,1,0,2:T(8,128)(2,1)}), bf16[1,6,1024,128]{3,1,0,2:T(8,128)(2,1)}, u32[]{:S(2)}, u32[]{:S(2)}) async-start(bf16[1,6,1024,128]{3,1,0,2:T(8,128)(2,1)} %bitcast.262), calls=%async_computation.5 | async-start | bytes 4194304 | tf_op jit(solution)/shard_map/all_to_all | solution.py:155
  538.3 4.0 fusion.26
  542.4 26.9 %all-to-all-done.5 = bf16[1,6,1024,128]{3,1,0,2:T(8,128)(2,1)} async-done(((bf16[1,6,1024,128]{3,1,0,2:T(8,128)(2,1)}), bf16[1,6,1024,128]{3,1,0,2:T(8,128)(2,1)}, u32[]{:S(2)}, u32[]{:S(2)}) %all-to-all-start.5) | async-done | bytes 1572896 | tf_op jit(solution)/shard_map/all_to_all | solution.py:155
  571.2 4.1 fusion.24
  577.2 7.6 pad_maximum_fusion
  585.5 238.5 %all-reduce.4.cloned.1.call-done = f32[4,4,64,3072]{3,2,0,1:T(8,128)} async-done(((f32[4,4,64,3072]{3,2,0,1:T(8,128)}), f32[4,4,64,3072]{3,2,0,1:T(8,128)}) %all-reduce.4.cloned.1.call-update) | async-done | bytes 12582928 | tf_op jit(solution)/shard_map/psum | solution.py:196
  824.0 33.8 %fusion.21 = f32[1,4,64,3072]{3,0,2,1:T(1,128)S(1)} fusion(f32[4,4,64,3072]{3,2,0,1:T(8,128)} %all-reduce.4.cloned.1.call-done, s32[4]{0:T(128)S(1)} %copy-done.22, s32[]{:T(128)S(6)} %axis_index.8), kind=kOutput, calls=%fused_computation.29 | convolution fusion | flops 37748740 | bytes 15728660 | tf_op jit(solution)/shard_map/ti,iabc->tabc/dot_general | solution.py:199
  857.8 4.6 divide_subtract_fusion
  (199 shorter events, 155.6 us)
Async XLA Ops:
  7.2 228.5 %copy-start = (bf16[4,64,3072]{2,1,0:T(8,128)(2,1)S(1)}, bf16[4,64,3072]{2,1,0:T(8,128)(2,1)}, u32[]{:S(2)}) copy-start(bf16[4,64,3072]{2,1,0:T(8,128)(2,1)} %param.18) | copy-start | bytes 4718596
  12.9 4.6 copy-start.6
  22.0 7.6 copy-start.21
  22.0 50.1 %all-to-all-start.2 = ((bf16[16,6,64,128]{3,2,1,0:T(8,128)(2,1)}), bf16[16,6,64,128]{3,2,1,0:T(8,128)(2,1)S(1)}, u32[]{:S(2)}, u32[]{:S(2)}) async-start(bf16[16,6,64,128]{3,2,1,0:T(8,128)(2,1)} %bitcast.266), calls=%async_computation.2 | async-start | bytes 3145728 | tf_op jit(solution)/shard_map/all_to_all | solution.py:144
  29.6 202.4 %all-reduce.6.cloned.1.call-start = ((), (), s32[]{:S(2)}) async-start(), calls=%async_computation.7 | async-start | bytes 12582912 | tf_op jit(solution)/shard_map/psum | solution.py:22
  38.3 0.7 copy-start.23
  72.1 168.6 %all-to-all-start.1 = ((bf16[16,6,64,128]{3,2,1,0:T(8,128)(2,1)}), bf16[16,6,64,128]{3,2,1,0:T(8,128)(2,1)}, u32[]{:S(2)}, u32[]{:S(2)}) async-start(bf16[16,6,64,128]{3,2,1,0:T(8,128)(2,1)} %bitcast.267), calls=%async_computation.1 | async-start | bytes 3145728 | tf_op jit(solution)/shard_map/all_to_all | solution.py:148
  232.0 1.9 copy-start.12
  233.6 1.5 copy-start.11
  233.9 1.6 copy-start.10
  235.7 3.3 copy-start.5
  235.7 2.6 copy-start.13
  238.2 0.8 copy-start.17
  240.7 36.8 %all-to-all-start.3 = ((bf16[16,6,64,128]{3,2,1,0:T(8,128)(2,1)}), bf16[16,6,64,128]{3,2,1,0:T(8,128)(2,1)}, u32[]{:S(2)}, u32[]{:S(2)}) async-start(bf16[16,6,64,128]{3,2,1,0:T(8,128)(2,1)} %bitcast.268), calls=%async_computation.3 | async-start | bytes 3145728 | tf_op jit(solution)/shard_map/all_to_all | solution.py:145
  245.5 2.1 copy-start.14
  247.6 2.1 copy-start.19
  249.7 1.7 copy-start.1
  252.4 6.7 copy-start.15
  277.6 41.5 %all-to-all-start = ((bf16[16,6,64,128]{3,2,1,0:T(8,128)(2,1)}), bf16[16,6,64,128]{3,2,1,0:T(8,128)(2,1)}, u32[]{:S(2)}, u32[]{:S(2)}) async-start(bf16[16,6,64,128]{3,2,1,0:T(8,128)(2,1)} %bitcast.275), calls=%async_computation | async-start | bytes 3145728 | tf_op jit(solution)/shard_map/all_to_all | solution.py:141
  466.4 9.3 %copy-start.9 = (bf16[6,1024,128]{2,1,0:T(8,128)(2,1)S(1)}, bf16[6,1024,128]{2,1,0:T(8,128)(2,1)}, u32[]{:S(2)}) copy-start(bf16[6,1024,128]{2,1,0:T(8,128)(2,1)} %get-tuple-element.80) | copy-start | bytes 4718596
  466.4 50.4 %all-to-all-start.4 = ((bf16[1,6,1024,128]{3,1,0,2:T(8,128)(2,1)}), bf16[1,6,1024,128]{3,1,0,2:T(8,128)(2,1)}, u32[]{:S(2)}, u32[]{:S(2)}) async-start(bf16[1,6,1024,128]{3,1,0,2:T(8,128)(2,1)} %bitcast.263), calls=%async_computation.4 | async-start | bytes 4194304 | tf_op jit(solution)/shard_map/all_to_all | solution.py:154
  516.8 52.4 %all-to-all-start.5 = ((bf16[1,6,1024,128]{3,1,0,2:T(8,128)(2,1)}), bf16[1,6,1024,128]{3,1,0,2:T(8,128)(2,1)}, u32[]{:S(2)}, u32[]{:S(2)}) async-start(bf16[1,6,1024,128]{3,1,0,2:T(8,128)(2,1)} %bitcast.262), calls=%async_computation.5 | async-start | bytes 4194304 | tf_op jit(solution)/shard_map/all_to_all | solution.py:155
  528.1 295.9 %all-reduce.4.cloned.1.call-start = ((), (), s32[]{:S(2)}) async-start(), calls=%async_computation.6 | async-start | bytes 25165824 | tf_op jit(solution)/shard_map/psum | solution.py:196
  530.4 1.9 copy-start.2
  530.4 1.9 copy-start.16
  534.1 2.0 copy-start.20
  571.2 4.1 copy-start.18
  575.3 1.9 copy-start.4
  584.8 239.2 %copy-start.22 = (s32[4]{0:T(128)S(1)}, s32[4]{0:T(128)}, u32[]{:S(2)}) copy-start(s32[4]{0:T(128)} %param.15) | copy-start | bytes 52
  824.0 33.8 %copy-start.3 = (f32[1,4,64,3072]{3,2,1,0:T(8,128)S(1)}, f32[1,4,64,3072]{3,2,1,0:T(8,128)}, u32[]{:S(2)}) copy-start(f32[1,4,64,3072]{3,2,1,0:T(8,128)} %param.23) | copy-start | bytes 9437188
  824.0 33.8 %copy-start.7 = (f32[1,4,64,3072]{3,2,1,0:T(8,128)S(1)}, f32[1,4,64,3072]{3,2,1,0:T(8,128)}, u32[]{:S(2)}) copy-start(f32[1,4,64,3072]{3,2,1,0:T(8,128)} %param.24) | copy-start | bytes 9437188
  824.0 33.8 %copy-start.8 = (f32[1,4,64,3072]{3,2,1,0:T(8,128)S(1)}, f32[1,4,64,3072]{3,2,1,0:T(8,128)}, u32[]{:S(2)}) copy-start(f32[1,4,64,3072]{3,2,1,0:T(8,128)} %param.25) | copy-start | bytes 9437188
Sparse Core Ops, SparseCore 0:
  38.5 193.4 all-reduce.5
  585.0 238.9 all-reduce.3
where the time goes:
time: 876 us; the launch traced here: 869 us
  waiting for transfers between devices  522 us (60%)
  matrix products  156 us (18%)
  local copies, waits for them, and re-layouts  80.7 us (9%)
  starting transfers between devices  52.3 us (6%)
  other arithmetic  39.4 us (4%)
  between operations  17.9 us (2%)
    psum x1, waiting for transfers between devices, shards(): summed = lax.psum(slots, 'seq')  239 us
    psum x1, waiting for transfers between devices, from_root(): return lax.psum(block, axis)  150 us
    all_to_all x1, waiting for transfers between devices, shards(): lax.all_to_all(dquery_p, 'seq', split_axis=2, concat_axis=0, tiled=True)  38.7 us
    dot_general x1, matrix products, shards(): jnp.einsum('ti,iabc->tabc', owners, summed, precision=lax.Precision.HIGHEST)  33.8 us
    dot_general x12, matrix products, scan_step(): jnp.dot(dscores, key_n, preferred_element_type=jnp.float32) * score_scale  30.8 us
    all_to_all x1, waiting for transfers between devices, shards(): lax.all_to_all(to_pairs_layout(key_n), 'seq', split_axis=0, concat_axis=2...  29.2 us
    dot_general x12, matrix products, scan_step(): jnp.einsum('qk,qd->kd', probs_b, upstream_blk, preferred_element_type=jnp...  27.8 us
    all_to_all x1, waiting for transfers between devices, shards(): lax.all_to_all(dvalue_p, 'seq', split_axis=2, concat_axis=0, tiled=True)  26.9 us
  transfers between devices with their start and end apart: 8, of which 7 were waited for; matrix products, arithmetic and copies ran while one was open for 6% of the time, Pallas kernels for 0%

commit v1 on v0

v1 whole, which is shorter than its diff:
```python
import functools
import math

import jax
import jax.numpy as jnp
from jax import lax
from jax.experimental import pallas as pl
from jax.experimental.pallas import tpu as pltpu
from jax.sharding import PartitionSpec as P

HEADS = 24
HD = 128
RANK = 64

adapter_scale = 0.5
norm_eps = 1e-06
beta_one = 0.9
beta_two = 0.999
adam_eps = 1e-08
learn_rate = 0.01
adam_step = 100.0
num_steps = 1000.0

SCORE_SCALE = HD ** (-0.5)
EXP_SCALE = SCORE_SCALE * math.log2(math.e)
VMEM_LIMIT = 50 << 20

MATS = (0, 2, 1, 3)

F32 = jnp.float32
BF16 = jnp.bfloat16


def dot(left, right):
    return jnp.dot(left, right, preferred_element_type=F32)


def dot_nt(left, right):
    return lax.dot_general(left, right, (((1,), (1,)), ((), ())), preferred_element_type=F32)


def dot_tn(left, right):
    return lax.dot_general(left, right, (((0,), (0,)), ((), ())), preferred_element_type=F32)


def exchange(block, flip, size):
    return lax.ppermute(block, "seq", [(i, i ^ flip) for i in range(size)])


def pack_kernel(chunks, weight_ref, query_ref, key_ref, value_ref, grad_ref, *out_refs):
    weight = weight_ref[pl.program_id(0)]
    head = 0
    for out_ref, count in zip(out_refs, chunks):
        for slot in range(count):
            cols = slice(head * HD, (head + 1) * HD)
            base = slot * 4 * HD
            key = key_ref[0, :, cols].astype(F32)
            inverse = lax.rsqrt(jnp.mean(key * key, axis=-1, keepdims=True) + norm_eps)
            out_ref[0, :, base : base + HD] = query_ref[0, :, cols]
            out_ref[0, :, base + HD : base + 2 * HD] = (key * inverse).astype(BF16)
            out_ref[0, :, base + 2 * HD : base + 3 * HD] = value_ref[0, :, cols]
            out_ref[0, :, base + 3 * HD : base + 4 * HD] = (
                weight * grad_ref[0, :, cols].astype(F32)
            ).astype(BF16)
            head += 1


def pack(weight_t, frozen_query, key_base, frozen_value, out_grad, per, chunks):
    images, rows, width = frozen_query.shape
    cols = width // per
    spec = pl.BlockSpec((1, rows, cols), lambda i, a: (i, 0, a))
    return pl.pallas_call(
        functools.partial(pack_kernel, chunks),
        grid=(images, per),
        in_specs=[pl.BlockSpec(memory_space=pltpu.SMEM)] + [spec] * 4,
        out_specs=[
            pl.BlockSpec((1, rows, n * 4 * HD), lambda i, a: (i * per + a, 0, 0)) for n in chunks
        ],
        out_shape=[jax.ShapeDtypeStruct((images * per, rows, n * 4 * HD), BF16) for n in chunks],
        compiler_params=pltpu.CompilerParams(vmem_limit_bytes=VMEM_LIMIT),
        cost_estimate=pl.CostEstimate(
            flops=0, bytes_accessed=16 * images * rows * width, transcendentals=0
        ),
        name="pack",
    )(weight_t, frozen_query, key_base, frozen_value, out_grad)


def attend_kernel(
    first, row_block, buf_ref, u_ref, bq_ref, bv_ref, *rest
):
    if first:
        gin_ref = None
    else:
        gin_ref, rest = rest[0], rest[1:]
    gout_ref, slot_ref, query_s, value_s, normed_s, inverse_s, dquery_s, dvalue_s, keyt_s = rest
    length = buf_ref.shape[0]

    @pl.when(pl.program_id(0) == 0)
    def _():
        gout_ref[...] = jnp.zeros_like(gout_ref) if first else gin_ref[...]

    query_raw = buf_ref[:, :HD].astype(F32) + adapter_scale * dot(u_ref[:, :RANK], bq_ref[...])
    inverse = lax.rsqrt(jnp.mean(query_raw * query_raw, axis=-1, keepdims=True) + norm_eps)
    normed = query_raw * inverse
    normed_s[...] = normed
    inverse_s[...] = jnp.broadcast_to(inverse, (length, HD))
    query_s[...] = normed.astype(BF16)
    value_s[...] = (
        buf_ref[:, 2 * HD : 3 * HD].astype(F32)
        + adapter_scale * dot(u_ref[:, RANK:], bv_ref[...])
    ).astype(BF16)
    key = buf_ref[:, HD : 2 * HD]
    keyt_s[...] = key.T
    for block in range(length // row_block):
        rows = slice(block * row_block, (block + 1) * row_block)
        upstream = buf_ref[rows, 3 * HD :]
        scores = dot_nt(key, query_s[rows, :])
        exp_scores = jnp.exp2(scores * EXP_SCALE)
        probs = exp_scores * (1.0 / jnp.sum(exp_scores, axis=0, keepdims=True))
        probs_b = probs.astype(BF16)
        dprobs = dot_nt(value_s[...], upstream)
        delta = jnp.sum(probs_b.astype(F32) * dprobs, axis=0, keepdims=True)
        dscores = (probs * (dprobs - delta)).astype(BF16)
        dquery_s[rows, :] = (dot(keyt_s[...], dscores) * SCORE_SCALE).T
        part = dot(probs_b, upstream)
        if block == 0:
            dvalue_s[...] = part
        else:
            dvalue_s[...] += part
    dquery_n = dquery_s[...].astype(BF16).astype(F32)
    normed = normed_s[...]
    dquery = (
        inverse_s[...]
        * (dquery_n - normed * jnp.mean(dquery_n * normed, axis=-1, keepdims=True))
    ).astype(BF16)
    dvalue = dvalue_s[...].astype(BF16)
    gout_ref[:, :RANK] += dot_nt(dquery, bq_ref[...])
    gout_ref[:, RANK:] += dot_nt(dvalue, bv_ref[...])
    slot_ref[:RANK, :] = (adapter_scale * dot_tn(u_ref[:, :RANK], dquery)).astype(slot_ref.dtype)
    slot_ref[RANK:, :] = (adapter_scale * dot_tn(u_ref[:, RANK:], dvalue)).astype(slot_ref.dtype)


def attend(received, u_rows, b_rows, partial_rows, first_head, send_type):
    length = received.shape[0]
    count = received.shape[1] // (4 * HD)
    first = partial_rows is None
    row_block = min(512, length)
    whole = lambda h: (0, 0)
    in_specs = [
        pl.BlockSpec((length, 4 * HD), lambda h: (0, h)),
        pl.BlockSpec((length, 2 * RANK), whole),
        pl.BlockSpec((RANK, HD), lambda h: (0, first_head + h)),
        pl.BlockSpec((RANK, HD), lambda h: (1, first_head + h)),
    ]
    operands = [received, u_rows, b_rows, b_rows]
    if not first:
        in_specs.append(pl.BlockSpec((length, 2 * RANK), whole))
        operands.append(partial_rows)
    return pl.pallas_call(
        functools.partial(attend_kernel, first, row_block),
        grid=(count,),
        in_specs=in_specs,
        out_specs=[
            pl.BlockSpec((length, 2 * RANK), whole),
            pl.BlockSpec((2 * RANK, HD), lambda h: (0, h)),
        ],
        out_shape=[
            jax.ShapeDtypeStruct((length, 2 * RANK), F32),
            jax.ShapeDtypeStruct((2 * RANK, count * HD), send_type),
        ],
        scratch_shapes=[
            pltpu.VMEM((length, HD), BF16),
            pltpu.VMEM((length, HD), BF16),
            pltpu.VMEM((length, HD), F32),
            pltpu.VMEM((length, HD), F32),
            pltpu.VMEM((length, HD), F32),
            pltpu.VMEM((length, HD), F32),
            pltpu.VMEM((HD, length), BF16),
        ],
        compiler_params=pltpu.CompilerParams(vmem_limit_bytes=VMEM_LIMIT),
        cost_estimate=pl.CostEstimate(
            flops=count * length * length * 10000,
            bytes_accessed=2 * received.size,
            transcendentals=count * length * length,
        ),
        name="attend",
    )(*operands)


def adam_kernel(per, where_ref, count_ref, *refs):
    grad_refs = refs[:per]
    adapter_ref, first_ref, second_ref, new_adapter_ref, new_first_ref, new_second_ref = refs[per:]
    first_corr = 1.0 - beta_one**adam_step
    second_corr = 1.0 - beta_two**adam_step
    divisor = count_ref[0].astype(F32)
    for m, grad_ref in enumerate(grad_refs):

        @pl.when(pl.program_id(0) == m)
        def _(grad_ref=grad_ref):
            for place, mat in enumerate(MATS):
                grad = grad_ref[place * RANK : (place + 1) * RANK, :].astype(F32) / divisor
                new_first = beta_one * first_ref[0, mat] + (1.0 - beta_one) * grad
                new_second = beta_two * second_ref[0, mat] + (1.0 - beta_two) * grad * grad
                new_first_ref[0, mat] = new_first
                new_second_ref[0, mat] = new_second
                new_adapter_ref[0, mat] = adapter_ref[0, mat] - learn_rate * (
                    new_first / first_corr
                ) / (jnp.sqrt(new_second / second_corr) + adam_eps)


def adam(place, counts, grads, adapters, first_moment, second_moment):
    per = len(grads)
    rows, cols = grads[0].shape
    state = pl.BlockSpec(
        (1, 4, RANK, cols), lambda m, where_ref, count_ref: (0, 0, 0, jnp.bitwise_xor(m, where_ref[0]))
    )
    grad = pl.BlockSpec((rows, cols), lambda m, where_ref, count_ref: (0, 0))
    return pl.pallas_call(
        functools.partial(adam_kernel, per),
        grid_spec=pltpu.PrefetchScalarGridSpec(
            num_scalar_prefetch=2,
            grid=(per,),
            in_specs=[grad] * per + [state] * 3,
            out_specs=[state] * 3,
        ),
        out_shape=[jax.ShapeDtypeStruct(adapters.shape, F32)] * 3,
        compiler_params=pltpu.CompilerParams(vmem_limit_bytes=VMEM_LIMIT),
        cost_estimate=pl.CostEstimate(
            flops=0, bytes_accessed=24 * adapters.size, transcendentals=0
        ),
        name="adam",
    )(place, counts, *grads, adapters, first_moment, second_moment)


def sum_rows(partial, place, per, size):
    length, width = partial.shape
    kept = partial.reshape((2,) * (per.bit_length() - 1) + (length // per, width))
    bits = per.bit_length() - 1
    for bit in range(bits):
        axis = bits - 1 - bit
        low = lax.index_in_dim(kept, 0, axis, keepdims=False)
        high = lax.index_in_dim(kept, 1, axis, keepdims=False)
        mine = ((place >> bit) & 1) == 1
        sent = jnp.where(mine, low, high)
        kept = jnp.where(mine, high, low) + exchange(sent, 1 << bit, size)
    rows = kept.astype(BF16)
    for bit in reversed(range(bits)):
        axis = bits - 1 - bit
        other = exchange(rows, 1 << bit, size)
        mine = ((place >> bit) & 1) == 1
        rows = jnp.stack(
            [jnp.where(mine, other, rows), jnp.where(mine, rows, other)], axis=axis
        )
    return rows.reshape(length, width)


def fetch_adapter(tenant_ids, adapters, zone, place, per, images, size):
    width = adapters.shape[-1]
    cols = width // per
    own = adapters[0]
    pieces = []
    for m in range(per):
        piece = lax.dynamic_slice_in_dim(own, (place ^ m) * cols, cols, axis=2)
        piece = jnp.stack([piece[mat] for mat in MATS]).reshape(4 * RANK, cols).astype(BF16)
        pieces.append(piece if m == 0 else exchange(piece, m, size))
    blocks = []
    for r in range(images):
        tenant = lax.dynamic_index_in_dim(tenant_ids, zone ^ r, 0, keepdims=False)
        block = jnp.zeros_like(pieces[0])
        for m, piece in enumerate(pieces):
            block = jnp.where(tenant == zone * per + (place ^ m), piece, block)
        blocks.append(block)
    bit = 1
    while len(blocks) > 1:
        sent = jnp.stack(blocks[1::2])
        came = exchange(sent, bit * per, size)
        blocks = [block + came[i] for i, block in enumerate(blocks[0::2])]
        bit *= 2
    return blocks[0]


def gather_images(slots, per, images, size):
    blocks = {0: slots}
    bit = images // 2
    while bit:
        known = sorted(blocks)
        came = exchange(jnp.stack([blocks[r] for r in known]), bit * per, size)
        for i, r in enumerate(known):
            blocks[r ^ bit] = came[i]
        bit //= 2
    return [blocks[r] for r in range(images)]


def shards(
    tenant_ids,
    timesteps,
    counts,
    hidden_in,
    frozen_query,
    key_base,
    frozen_value,
    out_grad,
    adapters,
    first_moment,
    second_moment,
):
    images, rows, width = hidden_in.shape
    size = lax.axis_size("seq")
    per = size // images
    cols = width // per
    heads = HEADS // per
    length = size * rows
    me = lax.axis_index("seq")
    zone, place = me // per, me % per
    chunks = (1,) * heads
    send_type = BF16

    hidden_sent = (
        hidden_in.reshape(images, rows, per, cols).transpose(0, 2, 1, 3).reshape(size, rows, cols)
    )
    hidden = lax.all_to_all(hidden_sent, "seq", 0, 0, tiled=True).reshape(length, cols)

    weight_t = 1.0 / (((timesteps.astype(F32) + 1.0) / num_steps) ** 2 + 0.25)
    packed = pack(weight_t, frozen_query, key_base, frozen_value, out_grad, per, chunks)

    adapter = fetch_adapter(tenant_ids, adapters, zone, place, per, images, size)
    a_rows, b_rows = adapter[: 2 * RANK], adapter[2 * RANK :]
    u_rows = sum_rows(dot_nt(hidden, a_rows), place, per, size)

    history = []
    partial_rows = None
    slots_b = []
    head = 0
    for step, count in enumerate(chunks):
        sent = packed[step]
        if step >= 2:
            sent, history[step - 2] = lax.optimization_barrier((sent, history[step - 2]))
        received = lax.all_to_all(sent, "seq", 0, 0, tiled=True).reshape(length, count * 4 * HD)
        if step >= 2:
            partial_rows = history[step - 1]
        elif step == 1:
            partial_rows = history[0]
        partial_rows, slot = attend(received, u_rows, b_rows, partial_rows, head, send_type)
        history.append(partial_rows)
        slots_b.append(slot)
        head += count

    grad_rows = sum_rows(partial_rows, place, per, size)
    slots_a = (adapter_scale * dot_tn(grad_rows, hidden)).astype(send_type)
    slots = jnp.concatenate([slots_a, jnp.concatenate(slots_b, axis=1)], axis=0)
    gathered = gather_images(slots, per, images, size)
    grads = []
    for m in range(per):
        tenant = zone * per + (place ^ m)
        total = jnp.zeros(slots.shape, F32)
        for r in range(images):
            owner = lax.dynamic_index_in_dim(tenant_ids, zone ^ r, 0, keepdims=False)
            total = total + jnp.where(owner == tenant, gathered[r].astype(F32), 0.0)
        total = total.astype(send_type)
        grads.append(total if m == 0 else exchange(total, m, size))
    return tuple(
        adam(place.reshape(1), counts, grads, adapters, first_moment, second_moment)
    )


def solution(mesh):
    whole = P(("groups", "seq"), None, None, None)
    tokens = P("groups", "seq", None)
    in_specs = (P("groups"), P("groups"), P(("groups", "seq"))) + (tokens,) * 5 + (whole,) * 3
    return jax.shard_map(
        shards, mesh=mesh, in_specs=in_specs, out_specs=(whole,) * 3, check_vma=False
    )
```

time: 876 us -> 349 us (0.40)
  waiting for transfers between devices: 522 us -> 201 us
  matrix products: 156 us -> 0.98 us
  local copies, waits for them, and re-layouts: 80.7 us -> 10.8 us
  Pallas kernels: 0 us -> 42.7 us
  other arithmetic: 39.4 us -> 12.1 us
  starting transfers between devices: 52.3 us -> 66.6 us
    psum x2 -> x0, waiting for transfers between devices: 388 us -> none  [the longest x1 239 us: shards(): summed = lax.psum(slots, 'seq')]
    dot_general x57 -> x2, matrix products: 156 us -> 0.98 us  [the longest x1 0.57 us: dot_nt(): lax.dot_general(left, right, (((1,), (1,)), ((), ())), preferred_element_...]
    ppermute x0 -> x18, waiting for transfers between devices: none -> 107 us  [exchange(): return lax.ppermute(block, 'seq', [(i, i ^ flip) for i in range(size)])]
    pallas_call x0 -> x8, Pallas kernels: none -> 42.7 us  [the longest x6 21.9 us: attend(): pl.pallas_call(functools.partial(attend_kernel, first, row_block), grid=(...]
    all_to_all x6 -> x7, waiting for transfers between devices: 134 us -> 94.2 us  [the longest x6 94.2 us: shards(): lax.all_to_all(sent, 'seq', 0, 0, tiled=True)]
    ppermute x0 -> x18, starting transfers between devices: none -> 21.2 us  [exchange(): return lax.ppermute(block, 'seq', [(i, i ^ flip) for i in range(size)])]
    squeeze x12 -> x0, local copies, waits for them, and re-layouts: 15.9 us -> none  [attend_items(): lax.map(lambda item_ops: pair_grads(*item_ops), tuple((member[0] for memb...]
    mul x4 -> x0, local copies, waits for them, and re-layouts: 13.4 us -> none  [the longest x2 6.76 us: head_norm(): return (shaped * inverse, inverse)]
  transfers between devices with their start and end apart: 8 -> 25, of which waited for: 7 -> 21; matrix products, arithmetic and copies ran while one was open for 6% -> 4% of each run, Pallas kernels for 0% -> 9%
where the time goes in v1:
time: 349 us; the launch traced here: 346 us
  waiting for transfers between devices  201 us (58%)
  starting transfers between devices  66.6 us (19%)
  Pallas kernels  42.7 us (12%)
  other arithmetic  12.1 us (3%)
  between operations  11.6 us (3%)
  local copies, waits for them, and re-layouts  10.8 us (3%)
    ppermute x18, waiting for transfers between devices, exchange(): return lax.ppermute(block, 'seq', [(i, i ^ flip) for i in range(size)])  107 us
    all_to_all x6, waiting for transfers between devices, shards(): lax.all_to_all(sent, 'seq', 0, 0, tiled=True)  94.2 us
    all_to_all x6, starting transfers between devices, shards(): lax.all_to_all(sent, 'seq', 0, 0, tiled=True)  38 us
    pallas_call x6, Pallas kernels, attend(): pl.pallas_call(functools.partial(attend_kernel, first, row_block), grid=(...  21.9 us
    ppermute x18, starting transfers between devices, exchange(): return lax.ppermute(block, 'seq', [(i, i ^ flip) for i in range(size)])  21.2 us
    pallas_call x1, Pallas kernels, pack(): pl.pallas_call(functools.partial(pack_kernel, chunks), grid=(images, per)...  11.8 us
    pallas_call x1, Pallas kernels, adam(): pl.pallas_call(functools.partial(adam_kernel, per), grid_spec=pltpu.Prefe...  8.95 us
    all_to_all x1, starting transfers between devices, shards(): lax.all_to_all(hidden_sent, 'seq', 0, 0, tiled=True).reshape(length, cols)  7.39 us
  transfers between devices with their start and end apart: 25, of which 21 were waited for; matrix products, arithmetic and copies ran while one was open for 4% of the time, Pallas kernels for 9%

profile of v1, /device:TPU:0, one launch (start us, length us, event | category | flops | bytes accessed | tf_op | source)
XLA Modules:
  0.0 345.6 jit_solution(11437896930691539753)
XLA Ops:
  0.6 1.5 fusion.47
  3.4 7.4 %all-to-all-start.1 = ((bf16[16,64,768]{2,1,0:T(8,128)(2,1)}), bf16[16,64,768]{2,1,0:T(8,128)(2,1)S(1)}, u32[]{:S(2)}, u32[]{:S(2)}) async-start(bf16[16,64,768]{2,1,0:T(8,128)(2,1)} %bitcast.234), calls=%async_computation.1 | async-start | bytes 3145728 | tf_op jit(solution)/shard_map/all_to_all | solution.py:321
  10.8 2.1 dynamic-slice_convert_fusion
  15.6 1.6 collective-permute-start
  24.5 1.7 broadcast_select_fusion.3
  26.2 9.9 %collective-permute-done = bf16[256,768]{1,0:T(8,128)(2,1)S(1)} collective-permute-done((bf16[256,768]{1,0:T(8,128)(2,1)}, bf16[256,768]{1,0:T(8,128)(2,1)S(1)}, u32[]{:S(2)}, u32[]{:S(2)}) %collective-permute-start) | collective-permute-done | bytes 393248 | tf_op jit(solution)/shard_map/ppermute | solution.py:47
  36.1 11.5 %collective-permute-done.1 = bf16[256,768]{1,0:T(8,128)(2,1)S(1)} collective-permute-done((bf16[256,768]{1,0:T(8,128)(2,1)}, bf16[256,768]{1,0:T(8,128)(2,1)S(1)}, u32[]{:S(2)}, u32[]{:S(2)}) %collective-permute-start.1) | collective-permute-done | bytes 393248 | tf_op jit(solution)/shard_map/ppermute | solution.py:47
  48.7 1.4 collective-permute-start.3
  53.3 14.9 %collective-permute-done.3 = bf16[2,256,768]{2,1,0:T(8,128)(2,1)} collective-permute-done((bf16[2,256,768]{2,1,0:T(8,128)(2,1)}, bf16[2,256,768]{2,1,0:T(8,128)(2,1)}, u32[]{:S(2)}, u32[]{:S(2)}) %collective-permute-start.3) | collective-permute-done | bytes 786464 | tf_op jit(solution)/shard_map/ppermute | solution.py:47
  68.2 1.8 fusion.30
  70.1 1.9 collective-permute-start.4
  72.0 11.8 %pack.1 = (bf16[16,64,512]{2,1,0:T(8,128)(2,1)}, bf16[16,64,512]{2,1,0:T(8,128)(2,1)}, bf16[16,64,512]{2,1,0:T(8,128)(2,1)}, bf16[16,64,512]{2,1,0:T(8,128)(2,1)...) custom-call(f32[4]{0:T(128)S(1)} %add_divide_fusion.weight_ref, bf16[4,64,3072]{2,1,0:T(8,128)(2,1)} %query_ref.1, ...), custom_call_target="tpu_custom_call" | custom-call | bytes 12582912 | tf_op jit(solution)/shard_map/pack/pallas_call | solution.py:72
  83.9 3.7 %all-to-all-start.2 = ((bf16[16,64,512]{2,1,0:T(8,128)(2,1)}), bf16[16,64,512]{2,1,0:T(8,128)(2,1)S(1)}, u32[]{:S(2)}, u32[]{:S(2)}) async-start(bf16[16,64,512]{2,1,0:T(8,128)(2,1)} %get-tuple-element.28), calls=%async_computation.2 | async-start | bytes 2097152 | tf_op jit(solution)/shard_map/all_to_all | solution.py:338
  89.6 1.3 fusion.32
  92.0 1.4 collective-permute-done.5
  93.5 2.1 collective-permute-start.6
  95.5 14.9 %all-to-all-done.2 = bf16[16,64,512]{2,1,0:T(8,128)(2,1)S(1)} async-done(((bf16[16,64,512]{2,1,0:T(8,128)(2,1)}), bf16[16,64,512]{2,1,0:T(8,128)(2,1)S(1)}, u32[]{:S(2)}, u32[]{:S(2)}) %all-to-all-start.2) | async-done | bytes 1048608 | tf_op jit(solution)/shard_map/all_to_all | solution.py:338
  110.4 6.8 %all-to-all-start = ((bf16[16,64,512]{2,1,0:T(8,128)(2,1)}), bf16[16,64,512]{2,1,0:T(8,128)(2,1)S(1)}, u32[]{:S(2)}, u32[]{:S(2)}) async-start(bf16[16,64,512]{2,1,0:T(8,128)(2,1)} %get-tuple-element.27), calls=%async_computation | async-start | bytes 2097152 | tf_op jit(solution)/shard_map/all_to_all | solution.py:338
  117.3 2.0 collective-permute-start.7
  119.3 9.1 %collective-permute-done.7 = bf16[256,128]{1,0:T(8,128)(2,1)S(1)} collective-permute-done((bf16[256,128]{1,0:T(8,128)(2,1)S(1)}, bf16[256,128]{1,0:T(8,128)(2,1)S(1)}, u32[]{:S(2)}, u32[]{:S(2)}) %collective-permute-start.7) | collective-permute-done | bytes 65568 | tf_op jit(solution)/shard_map/ppermute | solution.py:47
  128.5 1.3 collective-permute-done.8
  129.9 3.7 %attend.6 = (f32[1024,128]{1,0:T(8,128)S(1)}, bf16[128,128]{1,0:T(8,128)(2,1)S(1)}) custom-call(bf16[1024,512]{1,0:T(8,128)(2,1)S(1)} %bitcast.220, bf16[1024,128]{1,0:T(8,128)(2,1)S(1)} %bitcast.226, bf16[128,768]{1,0:T(8,128)(2,1)S(1)} %slice.239.bq_ref.bv_ref, bf16[128,768]{1,0:T(8,128)(2,1)S(1)} %slice.239.bq_ref.bv_ref), custom_call_target="tpu_custom_call" | custom-call | flops 10485760000 | bytes 1048576 | tf_op jit(solution)/shard_map/attend/pallas_call | solution.py:159
  134.4 5.8 %all-to-all-done = bf16[16,64,512]{2,1,0:T(8,128)(2,1)S(1)} async-done(((bf16[16,64,512]{2,1,0:T(8,128)(2,1)}), bf16[16,64,512]{2,1,0:T(8,128)(2,1)S(1)}, u32[]{:S(2)}, u32[]{:S(2)}) %all-to-all-start) | async-done | bytes 1048608 | tf_op jit(solution)/shard_map/all_to_all | solution.py:338
  140.2 6.9 %all-to-all-start.4 = ((bf16[16,64,512]{2,1,0:T(8,128)(2,1)}), bf16[16,64,512]{2,1,0:T(8,128)(2,1)S(1)}, u32[]{:S(2)}, u32[]{:S(2)}) async-start(bf16[16,64,512]{2,1,0:T(8,128)(2,1)} %get-tuple-element.33), calls=%async_computation.4 | async-start | bytes 2097152 | tf_op jit(solution)/shard_map/all_to_all | solution.py:338
  148.2 3.6 %attend.7 = (f32[1024,128]{1,0:T(8,128)S(1)}, bf16[128,128]{1,0:T(8,128)(2,1)S(1)}) custom-call(bf16[1024,512]{1,0:T(8,128)(2,1)S(1)} %bitcast.221, bf16[1024,128]{1,0:T(8,128)(2,1)S(1)} %bitcast.227, bf16[128,768]{1,0:T(8,128)(2,1)S(1)} %slice.239.bq_ref.bv_ref, bf16[128,768]{1,0:T(8,128)(2,1)S(1)} %slice.239.bq_ref.bv_ref, f32[1024,128]{1,0:T(8,128)S(1)} %copy-done.3), custom_call_target="tpu_custom_call" | custom-call | flops 10485760000 | bytes 1048576 | tf_op jit(solution)/shard_map/attend/pallas_call | solution.py:159
  151.8 18.2 %all-to-all-done.4 = bf16[16,64,512]{2,1,0:T(8,128)(2,1)S(1)} async-done(((bf16[16,64,512]{2,1,0:T(8,128)(2,1)}), bf16[16,64,512]{2,1,0:T(8,128)(2,1)S(1)}, u32[]{:S(2)}, u32[]{:S(2)}) %all-to-all-start.4) | async-done | bytes 1048608 | tf_op jit(solution)/shard_map/all_to_all | solution.py:338
  170.1 6.9 %all-to-all-start.3 = ((bf16[16,64,512]{2,1,0:T(8,128)(2,1)}), bf16[16,64,512]{2,1,0:T(8,128)(2,1)S(1)}, u32[]{:S(2)}, u32[]{:S(2)}) async-start(bf16[16,64,512]{2,1,0:T(8,128)(2,1)} %get-tuple-element.31), calls=%async_computation.3 | async-start | bytes 2097152 | tf_op jit(solution)/shard_map/all_to_all | solution.py:338
  176.9 3.6 %attend.8 = (f32[1024,128]{1,0:T(8,128)S(1)}, bf16[128,128]{1,0:T(8,128)(2,1)S(1)}) custom-call(bf16[1024,512]{1,0:T(8,128)(2,1)S(1)} %bitcast.223, bf16[1024,128]{1,0:T(8,128)(2,1)S(1)} %bitcast.228, bf16[128,768]{1,0:T(8,128)(2,1)S(1)} %slice.239.bq_ref.bv_ref, bf16[128,768]{1,0:T(8,128)(2,1)S(1)} %slice.239.bq_ref.bv_ref, ...), custom_call_target="tpu_custom_call" | custom-call | flops 10485760000 | bytes 1048576 | tf_op jit(solution)/shard_map/attend/pallas_call | solution.py:159
  181.4 18.5 %all-to-all-done.3 = bf16[16,64,512]{2,1,0:T(8,128)(2,1)S(1)} async-done(((bf16[16,64,512]{2,1,0:T(8,128)(2,1)}), bf16[16,64,512]{2,1,0:T(8,128)(2,1)S(1)}, u32[]{:S(2)}, u32[]{:S(2)}) %all-to-all-start.3) | async-done | bytes 1048608 | tf_op jit(solution)/shard_map/all_to_all | solution.py:338
  199.9 6.9 %all-to-all-start.6 = ((bf16[16,64,512]{2,1,0:T(8,128)(2,1)}), bf16[16,64,512]{2,1,0:T(8,128)(2,1)S(1)}, u32[]{:S(2)}, u32[]{:S(2)}) async-start(bf16[16,64,512]{2,1,0:T(8,128)(2,1)} %get-tuple-element.38), calls=%async_computation.6 | async-start | bytes 2097152 | tf_op jit(solution)/shard_map/all_to_all | solution.py:338
  207.8 3.6 %attend.9 = (f32[1024,128]{1,0:T(8,128)S(1)}, bf16[128,128]{1,0:T(8,128)(2,1)S(1)}) custom-call(bf16[1024,512]{1,0:T(8,128)(2,1)S(1)} %bitcast.224, bf16[1024,128]{1,0:T(8,128)(2,1)S(1)} %bitcast.229, bf16[128,768]{1,0:T(8,128)(2,1)S(1)} %slice.239.bq_ref.bv_ref, bf16[128,768]{1,0:T(8,128)(2,1)S(1)} %slice.239.bq_ref.bv_ref, f32[1024,128]{1,0:T(8,128)S(1)} %copy-done.1), custom_call_target="tpu_custom_call" | custom-call | flops 10485760000 | bytes 1048576 | tf_op jit(solution)/shard_map/attend/pallas_call | solution.py:159
  211.4 18.3 %all-to-all-done.6 = bf16[16,64,512]{2,1,0:T(8,128)(2,1)S(1)} async-done(((bf16[16,64,512]{2,1,0:T(8,128)(2,1)}), bf16[16,64,512]{2,1,0:T(8,128)(2,1)S(1)}, u32[]{:S(2)}, u32[]{:S(2)}) %all-to-all-start.6) | async-done | bytes 1048608 | tf_op jit(solution)/shard_map/all_to_all | solution.py:338
  229.7 6.9 %all-to-all-start.5 = ((bf16[16,64,512]{2,1,0:T(8,128)(2,1)}), bf16[16,64,512]{2,1,0:T(8,128)(2,1)S(1)}, u32[]{:S(2)}, u32[]{:S(2)}) async-start(bf16[16,64,512]{2,1,0:T(8,128)(2,1)} %get-tuple-element.36), calls=%async_computation.5 | async-start | bytes 2097152 | tf_op jit(solution)/shard_map/all_to_all | solution.py:338
  236.6 3.6 %attend.10 = (f32[1024,128]{1,0:T(8,128)S(1)}, bf16[128,128]{1,0:T(8,128)(2,1)S(1)}) custom-call(bf16[1024,512]{1,0:T(8,128)(2,1)S(1)} %bitcast.222, bf16[1024,128]{1,0:T(8,128)(2,1)S(1)} %bitcast.230, bf16[128,768]{1,0:T(8,128)(2,1)S(1)} %slice.239.bq_ref.bv_ref, bf16[128,768]{1,0:T(8,128)(2,1)S(1)} %slice.239.bq_ref.bv_ref, ...), custom_call_target="tpu_custom_call" | custom-call | flops 10485760000 | bytes 1048576 | tf_op jit(solution)/shard_map/attend/pallas_call | solution.py:159
  241.0 18.5 %all-to-all-done.5 = bf16[16,64,512]{2,1,0:T(8,128)(2,1)S(1)} async-done(((bf16[16,64,512]{2,1,0:T(8,128)(2,1)}), bf16[16,64,512]{2,1,0:T(8,128)(2,1)S(1)}, u32[]{:S(2)}, u32[]{:S(2)}) %all-to-all-start.5) | async-done | bytes 1048608 | tf_op jit(solution)/shard_map/all_to_all | solution.py:338
  260.6 3.6 %attend.11 = (f32[1024,128]{1,0:T(8,128)S(1)}, bf16[128,128]{1,0:T(8,128)(2,1)S(1)}) custom-call(bf16[1024,512]{1,0:T(8,128)(2,1)S(1)} %bitcast.225, bf16[1024,128]{1,0:T(8,128)(2,1)S(1)} %bitcast.231, bf16[128,768]{1,0:T(8,128)(2,1)S(1)} %slice.239.bq_ref.bv_ref, bf16[128,768]{1,0:T(8,128)(2,1)S(1)} %slice.239.bq_ref.bv_ref, f32[1024,128]{1,0:T(8,128)S(1)} %copy-done.5), custom_call_target="tpu_custom_call" | custom-call | flops 10485760000 | bytes 1048576 | tf_op jit(solution)/shard_map/attend/pallas_call | solution.py:159
  266.1 2.0 collective-permute-start.10
  268.2 4.0 %collective-permute-done.10 = f32[256,128]{1,0:T(8,128)S(1)} collective-permute-done((f32[256,128]{1,0:T(8,128)S(1)}, f32[256,128]{1,0:T(8,128)S(1)}, u32[]{:S(2)}, u32[]{:S(2)}) %collective-permute-start.10) | collective-permute-done | bytes 131104 | tf_op jit(solution)/shard_map/ppermute | solution.py:47
  272.2 1.8 collective-permute-start.11
  274.1 2.5 collective-permute-done.11
  276.7 1.3 collective-permute-done.12
  278.6 4.4 %collective-permute-start.13 = (bf16[1,256,768]{2,1,0:T(8,128)(2,1)S(1)}, bf16[1,256,768]{2,1,0:T(8,128)(2,1)S(1)}, u32[]{:S(2)}, u32[]{:S(2)}) collective-permute-start(bf16[1,256,768]{2,1,0:T(8,128)(2,1)S(1)} %fusion.46), channel_id=1, source_target_pairs={{0,8},{1,9},{2,10},{3,11},{4,12},{5,13},{6,14},{7,15},{8,0},{9,1},... | collective-permute-start | bytes 1179656 | tf_op jit(solution)/shard_map/ppermute | solution.py:47
  283.0 17.9 %collective-permute-done.13 = bf16[1,256,768]{2,1,0:T(8,128)(2,1)S(1)} collective-permute-done((bf16[1,256,768]{2,1,0:T(8,128)(2,1)S(1)}, bf16[1,256,768]{2,1,0:T(8,128)(2,1)S(1)}, u32[]{:S(2)}, u32[]{:S(2)}) %collective-permute-start.13) | collective-permute-done | bytes 393248 | tf_op jit(solution)/shard_map/ppermute | solution.py:47
  301.0 19.1 %collective-permute-done.14 = bf16[2,256,768]{2,1,0:T(8,128)(2,1)S(1)} collective-permute-done((bf16[2,256,768]{2,1,0:T(8,128)(2,1)S(1)}, bf16[2,256,768]{2,1,0:T(8,128)(2,1)S(1)}, u32[]{:S(2)}, u32[]{:S(2)}) %collective-permute-start.14) | collective-permute-done | bytes 786464 | tf_op jit(solution)/shard_map/ppermute | solution.py:47
  321.5 1.9 collective-permute-start.15
  324.0 8.7 %collective-permute-done.16.refs_2_ = bf16[256,768]{1,0:T(8,128)(2,1)S(1)} collective-permute-done((bf16[256,768]{1,0:T(8,128)(2,1)S(1)}, bf16[256,768]{1,0:T(8,128)(2,1)S(1)}, u32[]{:S(2)}, u32[]{:S(2)}) %collective-permute-start.16) | collective-permute-done | bytes 393248 | tf_op jit(solution)/shard_map/ppermute | solution.py:47
  332.7 3.9 %collective-permute-done.17.refs_3_ = bf16[256,768]{1,0:T(8,128)(2,1)S(1)} collective-permute-done((bf16[256,768]{1,0:T(8,128)(2,1)S(1)}, bf16[256,768]{1,0:T(8,128)(2,1)S(1)}, u32[]{:S(2)}, u32[]{:S(2)}) %collective-permute-start.17) | collective-permute-done | bytes 393248 | tf_op jit(solution)/shard_map/ppermute | solution.py:47
  336.6 8.9 %adam.1 = (f32[1,4,64,3072]{3,2,1,0:T(8,128)}, f32[1,4,64,3072]{3,2,1,0:T(8,128)}, f32[1,4,64,3072]{3,2,1,0:T(8,128)}) custom-call(s32[1]{0:T(128)} %bitcast.where_ref, s32[1]{0:T(128)S(6)} %copy.38.count_ref, bf16[256,768]{1,0:T(8,128)(2,1)S(1)} %get-tuple-element.54.refs_0_, bf16[256,768]{1,0:T(8,128)(2,1)S(1)} %collective-permute-done.15.refs_1_, ...), custom_call_target="tpu_custom_call" | custom-call | bytes 18874368 | tf_op jit(solution)/shard_map/adam/pallas_call | solution.py:218
  (83 shorter events, 18.7 us)
Async XLA Ops:
  3.4 80.5 %all-to-all-start.1 = ((bf16[16,64,768]{2,1,0:T(8,128)(2,1)}), bf16[16,64,768]{2,1,0:T(8,128)(2,1)S(1)}, u32[]{:S(2)}, u32[]{:S(2)}) async-start(bf16[16,64,768]{2,1,0:T(8,128)(2,1)} %bitcast.234), calls=%async_computation.1 | async-start | bytes 3145728 | tf_op jit(solution)/shard_map/all_to_all | solution.py:321
  14.4 11.8 %collective-permute-start.2 = (bf16[256,768]{1,0:T(8,128)(2,1)}, bf16[256,768]{1,0:T(8,128)(2,1)S(1)}, u32[]{:S(2)}, u32[]{:S(2)}) collective-permute-start(bf16[256,768]{1,0:T(8,128)(2,1)} %bitcast.19), channel_id=1, source_target_pairs={{0,1},{1,0},{2,3},{3,2},{4,5},{5,4},{6,7},{7,6},{8,9},{9,8},{10,11... | collective-permute-start | bytes 1179656 | tf_op jit(solution)/shard_map/ppermute | solution.py:47
  14.8 3.5 copy-start.11
  15.6 20.5 %collective-permute-start = (bf16[256,768]{1,0:T(8,128)(2,1)}, bf16[256,768]{1,0:T(8,128)(2,1)S(1)}, u32[]{:S(2)}, u32[]{:S(2)}) collective-permute-start(bf16[256,768]{1,0:T(8,128)(2,1)} %bitcast.9), channel_id=1, source_target_pairs={{0,3},{1,2},{2,1},{3,0},{4,7},{5,6},{6,5},{7,4},{8,11},{9,10},{10,... | collective-permute-start | bytes 1179656 | tf_op jit(solution)/shard_map/ppermute | solution.py:47
  18.0 29.6 %collective-permute-start.1 = (bf16[256,768]{1,0:T(8,128)(2,1)}, bf16[256,768]{1,0:T(8,128)(2,1)S(1)}, u32[]{:S(2)}, u32[]{:S(2)}) collective-permute-start(bf16[256,768]{1,0:T(8,128)(2,1)} %bitcast.14), channel_id=1, source_target_pairs={{0,2},{1,3},{2,0},{3,1},{4,6},{5,7},{6,4},{7,5},{8,10},{9,11},{10,... | collective-permute-start | bytes 1179656 | tf_op jit(solution)/shard_map/ppermute | solution.py:47
  47.6 36.2 %copy-start.8 = (bf16[256,768]{1,0:T(8,128)(2,1)}, bf16[256,768]{1,0:T(8,128)(2,1)S(1)}, u32[]{:S(2)}) copy-start(bf16[256,768]{1,0:T(8,128)(2,1)S(1)} %collective-permute-done.1) | copy-start | bytes 1179652
  48.7 19.5 %collective-permute-start.3 = (bf16[2,256,768]{2,1,0:T(8,128)(2,1)}, bf16[2,256,768]{2,1,0:T(8,128)(2,1)}, u32[]{:S(2)}, u32[]{:S(2)}) collective-permute-start(bf16[2,256,768]{2,1,0:T(8,128)(2,1)} %pad_maximum_fusion.1), channel_id=1, source_target_pairs={{0,4},{1,5},{2,6},{3,7},{4,0},{5,1},{6,2},{7,3},{8,12},{9,13},{10,... | collective-permute-start | bytes 2359304 | tf_op jit(solution)/shard_map/ppermute | solution.py:47
  52.4 19.7 %copy-start.12 = (s32[4]{0:T(128)S(1)}, s32[4]{0:T(128)}, u32[]{:S(2)}) copy-start(s32[4]{0:T(128)} %param.12) | copy-start | bytes 52
  70.1 19.6 %collective-permute-start.4 = (bf16[1,256,768]{2,1,0:T(8,128)(2,1)}, bf16[1,256,768]{2,1,0:T(8,128)(2,1)}, u32[]{:S(2)}, u32[]{:S(2)}) collective-permute-start(bf16[1,256,768]{2,1,0:T(8,128)(2,1)} %fusion.30), channel_id=1, source_target_pairs={{0,8},{1,9},{2,10},{3,11},{4,12},{5,13},{6,14},{7,15},{8,0},{9,1},... | collective-permute-start | bytes 1179656 | tf_op jit(solution)/shard_map/ppermute | solution.py:47
  83.9 7.1 %copy-start.6 = (bf16[16,64,768]{2,1,0:T(8,128)(2,1)}, bf16[16,64,768]{2,1,0:T(8,128)(2,1)S(1)}, u32[]{:S(2)}) copy-start(bf16[16,64,768]{2,1,0:T(8,128)(2,1)S(1)} %all-to-all-done.1) | copy-start | bytes 4718596
  83.9 26.6 %all-to-all-start.2 = ((bf16[16,64,512]{2,1,0:T(8,128)(2,1)}), bf16[16,64,512]{2,1,0:T(8,128)(2,1)S(1)}, u32[]{:S(2)}, u32[]{:S(2)}) async-start(bf16[16,64,512]{2,1,0:T(8,128)(2,1)} %get-tuple-element.28), calls=%async_computation.2 | async-start | bytes 2097152 | tf_op jit(solution)/shard_map/all_to_all | solution.py:338
  91.0 0.8 copy-start.9
  91.8 1.6 collective-permute-start.5
  93.4 35.0 %copy-start.10 = (bf16[256,768]{1,0:T(8,128)(2,1)S(1)}, bf16[256,768]{1,0:T(8,128)(2,1)}, u32[]{:S(2)}) copy-start(bf16[256,768]{1,0:T(8,128)(2,1)} %copy-done.9) | copy-start | bytes 1179652
  93.5 23.8 %collective-permute-start.6 = (f32[256,128]{1,0:T(8,128)S(1)}, f32[256,128]{1,0:T(8,128)S(1)}, u32[]{:S(2)}, u32[]{:S(2)}) collective-permute-start(f32[256,128]{1,0:T(8,128)S(1)} %select_bitcast_fusion.7), channel_id=1, source_target_pairs={{0,2},{1,3},{2,0},{3,1},{4,6},{5,7},{6,4},{7,5},{8,10},{9,11},{10,... | collective-permute-start | bytes 393224 | tf_op jit(solution)/shard_map/ppermute | solution.py:47
  110.4 29.8 %all-to-all-start = ((bf16[16,64,512]{2,1,0:T(8,128)(2,1)}), bf16[16,64,512]{2,1,0:T(8,128)(2,1)S(1)}, u32[]{:S(2)}, u32[]{:S(2)}) async-start(bf16[16,64,512]{2,1,0:T(8,128)(2,1)} %get-tuple-element.27), calls=%async_computation | async-start | bytes 2097152 | tf_op jit(solution)/shard_map/all_to_all | solution.py:338
  117.3 11.0 %collective-permute-start.7 = (bf16[256,128]{1,0:T(8,128)(2,1)S(1)}, bf16[256,128]{1,0:T(8,128)(2,1)S(1)}, u32[]{:S(2)}, u32[]{:S(2)}) collective-permute-start(bf16[256,128]{1,0:T(8,128)(2,1)S(1)} %fusion.45), channel_id=1, source_target_pairs={{0,2},{1,3},{2,0},{3,1},{4,6},{5,7},{6,4},{7,5},{8,10},{9,11},{10,... | collective-permute-start | bytes 196616 | tf_op jit(solution)/shard_map/ppermute | solution.py:47
  128.4 1.4 collective-permute-start.8
  133.6 0.8 copy-start.2
  140.2 29.9 %all-to-all-start.4 = ((bf16[16,64,512]{2,1,0:T(8,128)(2,1)}), bf16[16,64,512]{2,1,0:T(8,128)(2,1)S(1)}, u32[]{:S(2)}, u32[]{:S(2)}) async-start(bf16[16,64,512]{2,1,0:T(8,128)(2,1)} %get-tuple-element.33), calls=%async_computation.4 | async-start | bytes 2097152 | tf_op jit(solution)/shard_map/all_to_all | solution.py:338
  147.1 1.0 copy-start.3
  170.1 29.8 %all-to-all-start.3 = ((bf16[16,64,512]{2,1,0:T(8,128)(2,1)}), bf16[16,64,512]{2,1,0:T(8,128)(2,1)S(1)}, u32[]{:S(2)}, u32[]{:S(2)}) async-start(bf16[16,64,512]{2,1,0:T(8,128)(2,1)} %get-tuple-element.31), calls=%async_computation.3 | async-start | bytes 2097152 | tf_op jit(solution)/shard_map/all_to_all | solution.py:338
  180.6 0.8 copy-start
  199.9 29.8 %all-to-all-start.6 = ((bf16[16,64,512]{2,1,0:T(8,128)(2,1)}), bf16[16,64,512]{2,1,0:T(8,128)(2,1)S(1)}, u32[]{:S(2)}, u32[]{:S(2)}) async-start(bf16[16,64,512]{2,1,0:T(8,128)(2,1)} %get-tuple-element.38), calls=%async_computation.6 | async-start | bytes 2097152 | tf_op jit(solution)/shard_map/all_to_all | solution.py:338
  206.8 1.0 copy-start.1
  229.7 29.8 %all-to-all-start.5 = ((bf16[16,64,512]{2,1,0:T(8,128)(2,1)}), bf16[16,64,512]{2,1,0:T(8,128)(2,1)S(1)}, u32[]{:S(2)}, u32[]{:S(2)}) async-start(bf16[16,64,512]{2,1,0:T(8,128)(2,1)} %get-tuple-element.36), calls=%async_computation.5 | async-start | bytes 2097152 | tf_op jit(solution)/shard_map/all_to_all | solution.py:338
  240.2 0.8 copy-start.4
  259.5 1.0 copy-start.5
  264.2 1.8 collective-permute-start.9
  266.1 12.0 %copy-start.7 = (bf16[16,64,768]{2,1,0:T(8,128)(2,1)S(1)}, bf16[16,64,768]{2,1,0:T(8,128)(2,1)}, u32[]{:S(2)}) copy-start(bf16[16,64,768]{2,1,0:T(8,128)(2,1)} %copy-done.6) | copy-start | bytes 4718596
  266.1 6.1 %collective-permute-start.10 = (f32[256,128]{1,0:T(8,128)S(1)}, f32[256,128]{1,0:T(8,128)S(1)}, u32[]{:S(2)}, u32[]{:S(2)}) collective-permute-start(f32[256,128]{1,0:T(8,128)S(1)} %select_bitcast_fusion.4), channel_id=1, source_target_pairs={{0,2},{1,3},{2,0},{3,1},{4,6},{5,7},{6,4},{7,5},{8,10},{9,11},{10,... | collective-permute-start | bytes 393224 | tf_op jit(solution)/shard_map/ppermute | solution.py:47
  272.2 4.3 %collective-permute-start.11 = (bf16[256,128]{1,0:T(8,128)(2,1)S(1)}, bf16[256,128]{1,0:T(8,128)(2,1)S(1)}, u32[]{:S(2)}, u32[]{:S(2)}) collective-permute-start(bf16[256,128]{1,0:T(8,128)(2,1)S(1)} %fusion.44), channel_id=1, source_target_pairs={{0,2},{1,3},{2,0},{3,1},{4,6},{5,7},{6,4},{7,5},{8,10},{9,11},{10,... | collective-permute-start | bytes 196616 | tf_op jit(solution)/shard_map/ppermute | solution.py:47
  276.6 1.4 collective-permute-start.12
  278.6 22.3 %collective-permute-start.13 = (bf16[1,256,768]{2,1,0:T(8,128)(2,1)S(1)}, bf16[1,256,768]{2,1,0:T(8,128)(2,1)S(1)}, u32[]{:S(2)}, u32[]{:S(2)}) collective-permute-start(bf16[1,256,768]{2,1,0:T(8,128)(2,1)S(1)} %fusion.46), channel_id=1, source_target_pairs={{0,8},{1,9},{2,10},{3,11},{4,12},{5,13},{6,14},{7,15},{8,0},{9,1},... | collective-permute-start | bytes 1179656 | tf_op jit(solution)/shard_map/ppermute | solution.py:47
  300.9 19.1 %collective-permute-start.14 = (bf16[2,256,768]{2,1,0:T(8,128)(2,1)S(1)}, bf16[2,256,768]{2,1,0:T(8,128)(2,1)S(1)}, u32[]{:S(2)}, u32[]{:S(2)}) collective-permute-start(bf16[2,256,768]{2,1,0:T(8,128)(2,1)S(1)} %pad_maximum_fusion.2), channel_id=1, source_target_pairs={{0,4},{1,5},{2,6},{3,7},{4,0},{5,1},{6,2},{7,3},{8,12},{9,13},{10,... | collective-permute-start | bytes 2359304 | tf_op jit(solution)/shard_map/ppermute | solution.py:47
  320.6 12.1 %collective-permute-start.16 = (bf16[256,768]{1,0:T(8,128)(2,1)S(1)}, bf16[256,768]{1,0:T(8,128)(2,1)S(1)}, u32[]{:S(2)}, u32[]{:S(2)}) collective-permute-start(bf16[256,768]{1,0:T(8,128)(2,1)S(1)} %get-tuple-element.53), channel_id=1, source_target_pairs={{0,2},{1,3},{2,0},{3,1},{4,6},{5,7},{6,4},{7,5},{8,10},{9,11},{10,... | collective-permute-start | bytes 1179656 | tf_op jit(solution)/shard_map/ppermute | solution.py:47
  321.4 15.2 %collective-permute-start.17 = (bf16[256,768]{1,0:T(8,128)(2,1)S(1)}, bf16[256,768]{1,0:T(8,128)(2,1)S(1)}, u32[]{:S(2)}, u32[]{:S(2)}) collective-permute-start(bf16[256,768]{1,0:T(8,128)(2,1)S(1)} %get-tuple-element.51), channel_id=1, source_target_pairs={{0,3},{1,2},{2,1},{3,0},{4,7},{5,6},{6,5},{7,4},{8,11},{9,10},{10,... | collective-permute-start | bytes 1179656 | tf_op jit(solution)/shard_map/ppermute | solution.py:47
  321.5 15.1 %collective-permute-start.15 = (bf16[256,768]{1,0:T(8,128)(2,1)S(1)}, bf16[256,768]{1,0:T(8,128)(2,1)S(1)}, u32[]{:S(2)}, u32[]{:S(2)}) collective-permute-start(bf16[256,768]{1,0:T(8,128)(2,1)S(1)} %get-tuple-element.52), channel_id=1, source_target_pairs={{0,1},{1,0},{2,3},{3,2},{4,5},{5,4},{6,7},{7,6},{8,9},{9,8},{10,11... | collective-permute-start | bytes 1179656 | tf_op jit(solution)/shard_map/ppermute | solution.py:47

commit v2 on v1

v2 whole, which is shorter than its diff:
```python
import functools
import math

import jax
import jax.numpy as jnp
from jax import lax
from jax.experimental import pallas as pl
from jax.experimental.pallas import tpu as pltpu
from jax.sharding import PartitionSpec as P

HEADS = 24
HD = 128
RANK = 64

adapter_scale = 0.5
norm_eps = 1e-06
beta_one = 0.9
beta_two = 0.999
adam_eps = 1e-08
learn_rate = 0.01
adam_step = 100.0
num_steps = 1000.0

SCORE_SCALE = HD ** (-0.5)
EXP_SCALE = SCORE_SCALE * math.log2(math.e)
VMEM_LIMIT = 24 << 20

F32 = jnp.float32
BF16 = jnp.bfloat16


def dot(left, right):
    return jnp.dot(left, right, preferred_element_type=F32)


def dot_nt(left, right):
    return lax.dot_general(left, right, (((1,), (1,)), ((), ())), preferred_element_type=F32)


def dot_tn(left, right):
    return lax.dot_general(left, right, (((0,), (0,)), ((), ())), preferred_element_type=F32)


def exchange(block, flip, size):
    return lax.ppermute(block, "seq", [(i, i ^ flip) for i in range(size)])


def pack_kernel(chunks, per, steps_ref, query_ref, key_ref, value_ref, grad_ref, *out_refs):
    step = jnp.full((query_ref.shape[1], HD), steps_ref[pl.program_id(0)], jnp.int32)
    weight = 1.0 / (((step.astype(F32) + 1.0) / num_steps) ** 2 + 0.25)
    head = 0
    for dest in range(per):
        for out_ref, count in zip(out_refs, chunks):
            for slot in range(count):
                cols = slice(head * HD, (head + 1) * HD)
                base = slot * 4 * HD
                key = key_ref[0, :, cols].astype(F32)
                inverse = lax.rsqrt(jnp.mean(key * key, axis=-1, keepdims=True) + norm_eps)
                out_ref[dest, :, base : base + HD] = query_ref[0, :, cols]
                out_ref[dest, :, base + HD : base + 2 * HD] = (key * inverse).astype(BF16)
                out_ref[dest, :, base + 2 * HD : base + 3 * HD] = value_ref[0, :, cols]
                out_ref[dest, :, base + 3 * HD : base + 4 * HD] = (
                    weight * grad_ref[0, :, cols].astype(F32)
                ).astype(BF16)
                head += 1


def pack(timesteps, frozen_query, key_base, frozen_value, out_grad, per, chunks):
    images, rows, width = frozen_query.shape
    spec = pl.BlockSpec((1, rows, width), lambda i: (i, 0, 0))
    return pl.pallas_call(
        functools.partial(pack_kernel, chunks, per),
        grid=(images,),
        in_specs=[pl.BlockSpec(memory_space=pltpu.SMEM)] + [spec] * 4,
        out_specs=[pl.BlockSpec((per, rows, n * 4 * HD), lambda i: (i, 0, 0)) for n in chunks],
        out_shape=[jax.ShapeDtypeStruct((images * per, rows, n * 4 * HD), BF16) for n in chunks],
        compiler_params=pltpu.CompilerParams(vmem_limit_bytes=50 << 20),
        cost_estimate=pl.CostEstimate(
            flops=0, bytes_accessed=16 * images * rows * width, transcendentals=0
        ),
        name="pack",
    )(timesteps, frozen_query, key_base, frozen_value, out_grad)


def attend_kernel(
    first, row_block, buf_ref, u_ref, bq_ref, bv_ref, *rest
):
    if first:
        gin_ref = None
    else:
        gin_ref, rest = rest[0], rest[1:]
    gout_ref, slot_ref, query_s, value_s, normed_s, inverse_s, dquery_s, dvalue_s, keyt_s = rest
    length = buf_ref.shape[0]

    @pl.when(pl.program_id(0) == 0)
    def _():
        gout_ref[...] = jnp.zeros_like(gout_ref) if first else gin_ref[...]

    query_raw = buf_ref[:, :HD].astype(F32) + adapter_scale * dot(u_ref[:, :RANK], bq_ref[...])
    inverse = lax.rsqrt(jnp.mean(query_raw * query_raw, axis=-1, keepdims=True) + norm_eps)
    normed = query_raw * inverse
    normed_s[...] = normed
    inverse_s[...] = jnp.broadcast_to(inverse, (length, HD))
    query_s[...] = normed.astype(BF16)
    value_s[...] = (
        buf_ref[:, 2 * HD : 3 * HD].astype(F32)
        + adapter_scale * dot(u_ref[:, RANK:], bv_ref[...])
    ).astype(BF16)
    key = buf_ref[:, HD : 2 * HD]
    keyt_s[...] = key.T
    for block in range(length // row_block):
        rows = slice(block * row_block, (block + 1) * row_block)
        upstream = buf_ref[rows, 3 * HD :]
        scores = dot_nt(key, query_s[rows, :])
        exp_scores = jnp.exp2(scores * EXP_SCALE)
        probs = exp_scores * (1.0 / jnp.sum(exp_scores, axis=0, keepdims=True))
        probs_b = probs.astype(BF16)
        dprobs = dot_nt(value_s[...], upstream)
        delta = jnp.sum(probs_b.astype(F32) * dprobs, axis=0, keepdims=True)
        dscores = (probs * (dprobs - delta)).astype(BF16)
        dquery_s[rows, :] = (dot(keyt_s[...], dscores) * SCORE_SCALE).T
        part = dot(probs_b, upstream)
        if block == 0:
            dvalue_s[...] = part
        else:
            dvalue_s[...] += part
    dquery_n = dquery_s[...].astype(BF16).astype(F32)
    normed = normed_s[...]
    dquery = (
        inverse_s[...]
        * (dquery_n - normed * jnp.mean(dquery_n * normed, axis=-1, keepdims=True))
    ).astype(BF16)
    dvalue = dvalue_s[...].astype(BF16)
    gout_ref[:, :RANK] += dot_nt(dquery, bq_ref[...])
    gout_ref[:, RANK:] += dot_nt(dvalue, bv_ref[...])
    slot_ref[:RANK, :] = (adapter_scale * dot_tn(u_ref[:, :RANK], dquery)).astype(slot_ref.dtype)
    slot_ref[RANK:, :] = (adapter_scale * dot_tn(u_ref[:, RANK:], dvalue)).astype(slot_ref.dtype)


def attend(received, u_rows, b_rows, partial_rows, first_head, send_type):
    length = received.shape[0]
    count = received.shape[1] // (4 * HD)
    first = partial_rows is None
    row_block = min(512, length)
    whole = lambda h: (0, 0)
    in_specs = [
        pl.BlockSpec((length, 4 * HD), lambda h: (0, h)),
        pl.BlockSpec((length, 2 * RANK), whole),
        pl.BlockSpec((RANK, HD), lambda h: (0, first_head + h)),
        pl.BlockSpec((RANK, HD), lambda h: (1, first_head + h)),
    ]
    operands = [received, u_rows, b_rows, b_rows]
    if not first:
        in_specs.append(pl.BlockSpec((length, 2 * RANK), whole))
        operands.append(partial_rows)
    return pl.pallas_call(
        functools.partial(attend_kernel, first, row_block),
        grid=(count,),
        in_specs=in_specs,
        out_specs=[
            pl.BlockSpec((length, 2 * RANK), whole),
            pl.BlockSpec((2 * RANK, HD), lambda h: (0, h)),
        ],
        out_shape=[
            jax.ShapeDtypeStruct((length, 2 * RANK), F32),
            jax.ShapeDtypeStruct((2 * RANK, count * HD), send_type),
        ],
        scratch_shapes=[
            pltpu.VMEM((length, HD), BF16),
            pltpu.VMEM((length, HD), BF16),
            pltpu.VMEM((length, HD), F32),
            pltpu.VMEM((length, HD), F32),
            pltpu.VMEM((length, HD), F32),
            pltpu.VMEM((length, HD), F32),
            pltpu.VMEM((HD, length), BF16),
        ],
        compiler_params=pltpu.CompilerParams(vmem_limit_bytes=VMEM_LIMIT),
        cost_estimate=pl.CostEstimate(
            flops=count * length * length * 10000,
            bytes_accessed=2 * received.size,
            transcendentals=count * length * length,
        ),
        name="attend",
    )(*operands)


def adam_kernel(per, where_ref, count_ref, *refs):
    early_refs, late_refs, refs = refs[:per], refs[per : 2 * per], refs[2 * per :]
    adapter_ref, first_ref, second_ref, new_adapter_ref, new_first_ref, new_second_ref = refs
    cols = adapter_ref.shape[-1]
    early = early_refs[0].shape[-1]
    first_corr = 1.0 - beta_one**adam_step
    second_corr = 1.0 - beta_two**adam_step
    share = 1.0 / count_ref[0].astype(F32)

    def step(mat, where, grad):
        grad = grad.astype(F32) * share
        new_first = beta_one * first_ref[0, mat, :, where] + (1.0 - beta_one) * grad
        new_second = beta_two * second_ref[0, mat, :, where] + (1.0 - beta_two) * grad * grad
        new_first_ref[0, mat, :, where] = new_first
        new_second_ref[0, mat, :, where] = new_second
        corrected = new_second * (1.0 / second_corr)
        root = corrected * lax.rsqrt(corrected)
        new_adapter_ref[0, mat, :, where] = adapter_ref[0, mat, :, where] - (
            learn_rate / first_corr
        ) * new_first / (root + adam_eps)

    for m in range(per):

        @pl.when(pl.program_id(0) == m)
        def _(m=m):
            step(0, slice(0, cols), late_refs[m][:, :cols])
            step(1, slice(0, early), early_refs[m][...])
            step(1, slice(early, cols), late_refs[m][:, cols:])


def adam(place, counts, early, late, adapters, first_moment, second_moment):
    per = len(early)
    cols = adapters.shape[-1] // per
    state = pl.BlockSpec(
        (1, 2, RANK, cols),
        lambda m, p, where_ref, count_ref: (0, p, 0, jnp.bitwise_xor(m, where_ref[0])),
    )
    grads = [
        pl.BlockSpec((RANK, grad.shape[1]), lambda m, p, where_ref, count_ref: (p, 0))
        for grad in (*early, *late)
    ]
    return pl.pallas_call(
        functools.partial(adam_kernel, per),
        grid_spec=pltpu.PrefetchScalarGridSpec(
            num_scalar_prefetch=2,
            grid=(per, 2),
            in_specs=grads + [state] * 3,
            out_specs=[state] * 3,
        ),
        out_shape=[jax.ShapeDtypeStruct(adapters.shape, F32)] * 3,
        compiler_params=pltpu.CompilerParams(vmem_limit_bytes=VMEM_LIMIT),
        cost_estimate=pl.CostEstimate(
            flops=0, bytes_accessed=24 * adapters.size, transcendentals=0
        ),
        name="adam",
    )(place, counts, *early, *late, adapters, first_moment, second_moment)


def reduce_scatter_rows(partial, place, per, size):
    rows = partial.shape[0] // per
    total = lax.dynamic_slice_in_dim(partial, place * rows, rows, axis=0)
    came = [
        exchange(lax.dynamic_slice_in_dim(partial, (place ^ m) * rows, rows, axis=0), m, size)
        for m in range(1, per)
    ]
    for block in came:
        total = total + block
    return total.astype(BF16)


def gather_rows(total, per, size):
    return [total] + [exchange(total, m, size) for m in range(1, per)]


def in_order(blocks, place):
    bit = 1
    while bit < len(blocks):
        flip = (place & bit) != 0
        blocks = [
            jnp.where(flip, blocks[i ^ bit], blocks[i]) for i in range(len(blocks))
        ]
        bit *= 2
    return jnp.concatenate(blocks, axis=0)


def slot_kernel(per, where_ref, *refs):
    row_refs, (hidden_ref, last_ref, out_ref, total_s) = refs[:per], refs[per:]
    cols = hidden_ref.shape[1]
    for m, row_ref in enumerate(row_refs):

        @pl.when(pl.program_id(0) == m)
        def _(row_ref=row_ref, m=m):
            part = dot_tn(row_ref[...], hidden_ref[...])
            if m:
                part = part + total_s[...]
            if m < per - 1:
                total_s[...] = part
            else:
                out_ref[:, :cols] = (adapter_scale * part).astype(out_ref.dtype)
                out_ref[:, cols:] = last_ref[...]


def slots_of_hidden(place, blocks, hidden, last):
    per = len(blocks)
    rows, width = blocks[0].shape
    cols = hidden.shape[1]
    whole = lambda m, where_ref: (0, 0)
    return pl.pallas_call(
        functools.partial(slot_kernel, per),
        grid_spec=pltpu.PrefetchScalarGridSpec(
            num_scalar_prefetch=1,
            grid=(per,),
            in_specs=[pl.BlockSpec((rows, width), whole)] * per
            + [
                pl.BlockSpec((rows, cols), lambda m, where_ref: (jnp.bitwise_xor(m, where_ref[0]), 0)),
                pl.BlockSpec(last.shape, whole),
            ],
            out_specs=pl.BlockSpec((width, cols + last.shape[1]), whole),
            scratch_shapes=[pltpu.VMEM((width, cols), F32)],
        ),
        out_shape=jax.ShapeDtypeStruct((width, cols + last.shape[1]), last.dtype),
        compiler_params=pltpu.CompilerParams(vmem_limit_bytes=VMEM_LIMIT),
        cost_estimate=pl.CostEstimate(
            flops=2 * rows * per * width * cols, bytes_accessed=2 * hidden.size, transcendentals=0
        ),
        name="slots",
    )(place, *blocks, hidden, last)


def tie(values, *others):
    return lax.optimization_barrier((values, others))[0]


def pieces_kernel(per, where_ref, adapter_ref, *out_refs):
    for m in range(per):

        @pl.when(pl.program_id(0) == m)
        def _(m=m):
            for half in range(2):
                for row, mat in enumerate((half, half + 2)):
                    out_refs[half * per + m][row * RANK : (row + 1) * RANK, :] = adapter_ref[
                        0, mat
                    ].astype(BF16)


def column_pieces(place, adapters, per):
    cols = adapters.shape[-1] // per
    pieces = pl.pallas_call(
        functools.partial(pieces_kernel, per),
        grid_spec=pltpu.PrefetchScalarGridSpec(
            num_scalar_prefetch=1,
            grid=(per,),
            in_specs=[
                pl.BlockSpec(
                    (1, 4, RANK, cols),
                    lambda m, where_ref: (0, 0, 0, jnp.bitwise_xor(m, where_ref[0])),
                )
            ],
            out_specs=[pl.BlockSpec((2 * RANK, cols), lambda m, where_ref: (0, 0))] * (2 * per),
        ),
        out_shape=[jax.ShapeDtypeStruct((2 * RANK, cols), BF16)] * (2 * per),
        compiler_params=pltpu.CompilerParams(vmem_limit_bytes=VMEM_LIMIT),
        cost_estimate=pl.CostEstimate(
            flops=0, bytes_accessed=6 * adapters.size, transcendentals=0
        ),
        name="pieces",
    )(place, adapters)
    return pieces[:per], pieces[per:]


def spread(pieces, size):
    return [piece if m == 0 else exchange(piece, m, size) for m, piece in enumerate(pieces)]


def for_images_kernel(per, images, where_ref, ids_ref, *refs):
    piece_refs, (kept_ref, sent_ref) = refs[:per], refs[per:]
    zone, place = where_ref[0], where_ref[1]
    for r in range(images):
        tenant = ids_ref[jnp.bitwise_xor(zone, r)]
        block = jnp.zeros(piece_refs[0].shape, BF16)
        for m, piece_ref in enumerate(piece_refs):
            owner = zone * per + jnp.bitwise_xor(place, m)
            block = jnp.where(tenant == owner, piece_ref[...], block)
        if r % 2:
            sent_ref[r // 2] = block
        else:
            kept_ref[r // 2] = block


def for_images(where, tenant_ids, pieces):
    images = tenant_ids.shape[0]
    shape = (images // 2,) + pieces[0].shape
    smem = pl.BlockSpec(memory_space=pltpu.SMEM)
    return pl.pallas_call(
        functools.partial(for_images_kernel, len(pieces), images),
        in_specs=[smem, smem] + [pl.BlockSpec(memory_space=pltpu.VMEM)] * len(pieces),
        out_specs=[pl.BlockSpec(memory_space=pltpu.VMEM)] * 2,
        out_shape=[jax.ShapeDtypeStruct(shape, BF16)] * 2,
        compiler_params=pltpu.CompilerParams(vmem_limit_bytes=VMEM_LIMIT),
        cost_estimate=pl.CostEstimate(
            flops=0, bytes_accessed=8 * images * pieces[0].size, transcendentals=0
        ),
        name="for_images",
    )(where, tenant_ids, *pieces)


def halve_all(kept, came, per, size):
    blocks = [kept[i] + came[i] for i in range(kept.shape[0])]
    bit = 2
    while len(blocks) > 1:
        came = exchange(jnp.stack(blocks[1::2]), bit * per, size)
        blocks = [block + came[i] for i, block in enumerate(blocks[0::2])]
        bit *= 2
    return blocks[0]


def direct_images(slots, per, images, size):
    return [slots] + [exchange(slots, r * per, size) for r in range(1, images)]


def owner_kernel(per, images, where_ref, ids_ref, *refs):
    image_refs, sum_refs = refs[:images], refs[images:]
    zone, place = where_ref[0], where_ref[1]
    for m, sum_ref in enumerate(sum_refs):
        owner = zone * per + jnp.bitwise_xor(place, m)
        total = jnp.zeros(sum_ref.shape, F32)
        for r, image_ref in enumerate(image_refs):
            mine = ids_ref[jnp.bitwise_xor(zone, r)] == owner
            total = total + jnp.where(mine, image_ref[...].astype(F32), 0.0)
        sum_ref[...] = total.astype(sum_ref.dtype)


def owner_sums(where, tenant_ids, gathered, per, size):
    images = len(gathered)
    smem = pl.BlockSpec(memory_space=pltpu.SMEM)
    vmem = pl.BlockSpec(memory_space=pltpu.VMEM)
    sums = pl.pallas_call(
        functools.partial(owner_kernel, per, images),
        in_specs=[smem, smem] + [vmem] * images,
        out_specs=[vmem] * per,
        out_shape=[jax.ShapeDtypeStruct(gathered[0].shape, gathered[0].dtype)] * per,
        compiler_params=pltpu.CompilerParams(vmem_limit_bytes=VMEM_LIMIT),
        cost_estimate=pl.CostEstimate(
            flops=0, bytes_accessed=4 * images * gathered[0].size, transcendentals=0
        ),
        name="owner_sums",
    )(where, tenant_ids, *gathered)
    return [total if m == 0 else exchange(total, m, size) for m, total in enumerate(sums)]


def shards(
    tenant_ids,
    timesteps,
    counts,
    hidden_in,
    frozen_query,
    key_base,
    frozen_value,
    out_grad,
    adapters,
    first_moment,
    second_moment,
):
    images, rows, width = hidden_in.shape
    size = lax.axis_size("seq")
    per = size // images
    cols = width // per
    heads = HEADS // per
    length = size * rows
    me = lax.axis_index("seq")
    zone, place = me // per, me % per
    chunks = (heads - 1, 1)
    send_type = BF16

    hidden_sent = (
        hidden_in.reshape(images, rows, per, cols).transpose(0, 2, 1, 3).reshape(size, rows, cols)
    )
    pieces_a, pieces_b = column_pieces(place.reshape(1), adapters, per)
    pieces_a = spread(pieces_a, size)
    hidden_sent = tie(hidden_sent, pieces_a[1])
    hidden = lax.all_to_all(hidden_sent, "seq", 0, 0, tiled=True).reshape(length, cols)

    packed = pack(timesteps, frozen_query, key_base, frozen_value, out_grad, per, chunks)

    where = jnp.stack([zone, place])
    pieces_a = tie(pieces_a, packed)
    a_kept, a_sent = for_images(where, tenant_ids, pieces_a)
    a_came = exchange(a_sent, per, size)
    b_kept, b_sent = for_images(where, tenant_ids, spread(pieces_b, size))
    a_rows = halve_all(a_kept, a_came, per, size)
    b_rows = halve_all(b_kept, exchange(b_sent, per, size), per, size)

    packed = tie(packed, a_rows)
    u_total = reduce_scatter_rows(dot_nt(hidden, a_rows), place, per, size)

    u_rows = in_order(gather_rows(u_total, per, size), place)

    partial_rows = None
    head = 0
    slots_b = []
    for sent, count in zip(packed, chunks):
        received = lax.all_to_all(sent, "seq", 0, 0, tiled=True).reshape(length, count * 4 * HD)
        partial_rows, slot = attend(received, u_rows, b_rows, partial_rows, head, send_type)
        slots_b.append(slot)
        head += count
    early = {0: slots_b[0]}
    early[images // 2] = exchange(early[0], images // 2 * per, size)
    partial_rows = tie(partial_rows, early[images // 2])

    grad_total = reduce_scatter_rows(partial_rows, place, per, size)
    grad_rows = gather_rows(grad_total, per, size)
    bit = images // 4
    while bit:
        known = sorted(early)
        came = exchange(jnp.stack([early[r] for r in known]), bit * per, size)
        for i, r in enumerate(known):
            early[r ^ bit] = came[i]
        bit //= 2
    late = slots_of_hidden(place.reshape(1), grad_rows, hidden, slots_b[1])
    late = direct_images(late, per, images, size)
    early = owner_sums(where, tenant_ids, [early[r] for r in range(images)], per, size)
    late = [late[0]] + tie(late[1:], early)
    late = owner_sums(where, tenant_ids, late, per, size)
    return tuple(
        adam(place.reshape(1), counts, early, late, adapters, first_moment, second_moment)
    )


def solution(mesh):
    whole = P(("groups", "seq"), None, None, None)
    tokens = P("groups", "seq", None)
    in_specs = (P("groups"), P("groups"), P(("groups", "seq"))) + (tokens,) * 5 + (whole,) * 3
    return jax.shard_map(
        shards, mesh=mesh, in_specs=in_specs, out_specs=(whole,) * 3, check_vma=False
    )
```

time: 349 us -> 292 us (0.84)
  waiting for transfers between devices: 201 us -> 181 us
  other arithmetic: 12.1 us -> 1.58 us
  between operations: 11.6 us -> 1.67 us
  starting transfers between devices: 66.6 us -> 57.1 us
  local copies, waits for them, and re-layouts: 10.8 us -> 5.75 us
    all_to_all x6 -> x2, waiting for transfers between devices: 94.2 us -> 0.01 us  [shards(): lax.all_to_all(sent, 'seq', 0, 0, tiled=True)]
    ppermute x18 -> x33, waiting for transfers between devices: 107 us -> 155 us  [exchange(): return lax.ppermute(block, 'seq', [(i, i ^ flip) for i in range(size)])]
    all_to_all x1, waiting for transfers between devices: 0.01 us -> 25.9 us  [shards(): lax.all_to_all(hidden_sent, 'seq', 0, 0, tiled=True).reshape(length, cols)]
    all_to_all x6 -> x2, starting transfers between devices: 38 us -> 13.1 us  [shards(): lax.all_to_all(sent, 'seq', 0, 0, tiled=True)]
    ppermute x18 -> x33, starting transfers between devices: 21.2 us -> 36.4 us  [exchange(): return lax.ppermute(block, 'seq', [(i, i ^ flip) for i in range(size)])]
    another operation x15 -> x2, other arithmetic: 5.45 us -> 0.11 us  [the longest x1 0.07 us: shards(): where = jnp.stack([zone, place])]
    pallas_call x6 -> x2, Pallas kernels: 21.9 us -> 23.3 us  [attend(): pl.pallas_call(functools.partial(attend_kernel, first, row_block), grid=(...]
    pallas_call x1 -> x7, Pallas kernels: 11.8 us -> 11.3 us  [the longest x1 6.06 us: pack(): pl.pallas_call(functools.partial(pack_kernel, chunks, per), grid=(images,...]
  transfers between devices with their start and end apart: 25 -> 36, of which waited for: 21 -> 18; matrix products, arithmetic and copies ran while one was open for 4% -> 1% of each run, Pallas kernels for 9% -> 11%
where the time goes in v2:
time: 292 us; the launch traced here: 290 us
  waiting for transfers between devices  181 us (62%)
  starting transfers between devices  57.1 us (20%)
  Pallas kernels  40.8 us (14%)
  local copies, waits for them, and re-layouts  5.75 us (2%)
    ppermute x33, waiting for transfers between devices, exchange(): return lax.ppermute(block, 'seq', [(i, i ^ flip) for i in range(size)])  155 us
    ppermute x33, starting transfers between devices, exchange(): return lax.ppermute(block, 'seq', [(i, i ^ flip) for i in range(size)])  36.4 us
    all_to_all x1, waiting for transfers between devices, shards(): lax.all_to_all(hidden_sent, 'seq', 0, 0, tiled=True).reshape(length, cols)  25.9 us
    pallas_call x2, Pallas kernels, attend(): pl.pallas_call(functools.partial(attend_kernel, first, row_block), grid=(...  23.3 us
    all_to_all x2, starting transfers between devices, shards(): lax.all_to_all(sent, 'seq', 0, 0, tiled=True)  13.1 us
    all_to_all x1, starting transfers between devices, shards(): lax.all_to_all(hidden_sent, 'seq', 0, 0, tiled=True).reshape(length, cols)  7.52 us
    pallas_call x1, Pallas kernels, adam(): pl.pallas_call(functools.partial(adam_kernel, per), grid_spec=pltpu.Prefe...  6.18 us
    pallas_call x1, Pallas kernels, pack(): pl.pallas_call(functools.partial(pack_kernel, chunks, per), grid=(images,...  6.06 us
  transfers between devices with their start and end apart: 36, of which 18 were waited for; matrix products, arithmetic and copies ran while one was open for 1% of the time, Pallas kernels for 11%

profile of v2, /device:TPU:0, one launch (start us, length us, event | category | flops | bytes accessed | tf_op | source)
XLA Modules:
  0.0 289.7 jit_solution(7592996965945131564)
XLA Ops:
  0.7 1.9 copy-done
  4.1 1.2 pad_maximum_fusion
  6.1 7.5 %all-to-all-start.1 = ((bf16[16,64,768]{2,1,0:T(8,128)(2,1)}), bf16[16,64,768]{2,1,0:T(8,128)(2,1)S(1)}, u32[]{:S(2)}, u32[]{:S(2)}) async-start(bf16[16,64,768]{2,1,0:T(8,128)(2,1)} %bitcast.23), calls=%async_computation.1 | async-start | bytes 3145728 | tf_op jit(solution)/shard_map/all_to_all | solution.py:467
  13.6 6.1 %pack.1 = (bf16[16,64,2560]{2,1,0:T(8,128)(2,1)}, bf16[16,64,512]{2,1,0:T(8,128)(2,1)}) custom-call(s32[4]{0:T(128)S(1)} %copy-done.8, bf16[4,64,3072]{2,1,0:T(8,128)(2,1)S(1)} %copy-done.4, bf16[4,64,3072]{2,1,0:T(8,128)(2,1)} %key_ref.1, bf16[4,64,3072]{2,1,0:T(8,128)(2,1)} %value_ref.1, bf16[4,64,3072]{2,1,0:T(8,128)(2,1)} %grad_ref.1), custom_call_target="tpu_custom_call" | custom-call | bytes 12582912 | tf_op jit(solution)/shard_map/pack/pallas_call | solution.py:71
  19.7 25.9 %all-to-all-done.1 = bf16[16,64,768]{2,1,0:T(8,128)(2,1)S(1)} async-done(((bf16[16,64,768]{2,1,0:T(8,128)(2,1)}), bf16[16,64,768]{2,1,0:T(8,128)(2,1)S(1)}, u32[]{:S(2)}, u32[]{:S(2)}) %all-to-all-start.1) | async-done | bytes 1572896 | tf_op jit(solution)/shard_map/all_to_all | solution.py:467
  45.6 9.3 %all-to-all-start = ((bf16[16,64,2560]{2,1,0:T(8,128)(2,1)}), bf16[16,64,2560]{2,1,0:T(8,128)(2,1)}, u32[]{:S(2)}, u32[]{:S(2)}) async-start(bf16[16,64,2560]{2,1,0:T(8,128)(2,1)} %get-tuple-element.38), calls=%async_computation | async-start | bytes 10485760 | tf_op jit(solution)/shard_map/all_to_all | solution.py:488
  54.9 1.9 collective-permute-start.1
  56.9 34.8 %collective-permute-done.1.refs_2_ = bf16[128,768]{1,0:T(8,128)(2,1)S(1)} collective-permute-done((bf16[128,768]{1,0:T(8,128)(2,1)S(1)}, bf16[128,768]{1,0:T(8,128)(2,1)S(1)}, u32[]{:S(2)}, u32[]{:S(2)}) %collective-permute-start.1) | collective-permute-done | bytes 196640 | tf_op jit(solution)/shard_map/ppermute | solution.py:45
  91.8 3.6 %collective-permute-done.2.refs_3_ = bf16[128,768]{1,0:T(8,128)(2,1)S(1)} collective-permute-done((bf16[128,768]{1,0:T(8,128)(2,1)S(1)}, bf16[128,768]{1,0:T(8,128)(2,1)S(1)}, u32[]{:S(2)}, u32[]{:S(2)}) %collective-permute-start.2) | collective-permute-done | bytes 196640 | tf_op jit(solution)/shard_map/ppermute | solution.py:45
  96.2 8.3 %collective-permute-start.11 = (bf16[128,768]{1,0:T(8,128)(2,1)}, bf16[128,768]{1,0:T(8,128)(2,1)S(1)}, u32[]{:S(2)}, u32[]{:S(2)}) collective-permute-start(bf16[128,768]{1,0:T(8,128)(2,1)} %copy-done.12), channel_id=1, source_target_pairs={{0,1},{1,0},{2,3},{3,2},{4,5},{5,4},{6,7},{7,6},{8,9},{9,8},{10,11... | collective-permute-start | bytes 589832 | tf_op jit(solution)/shard_map/ppermute | solution.py:45
  104.4 1.4 collective-permute-start.13
  105.9 43.0 %collective-permute-done.3 = bf16[2,128,768]{2,1,0:T(8,128)(2,1)S(1)} collective-permute-done((bf16[2,128,768]{2,1,0:T(8,128)(2,1)S(1)}, bf16[2,128,768]{2,1,0:T(8,128)(2,1)S(1)}, u32[]{:S(2)}, u32[]{:S(2)}) %collective-permute-start.3) | collective-permute-done | bytes 393248 | tf_op jit(solution)/shard_map/ppermute | solution.py:45
  149.7 4.5 %collective-permute-start.4 = (bf16[1,128,768]{2,1,0:T(8,128)(2,1)S(1)}, bf16[1,128,768]{2,1,0:T(8,128)(2,1)}, u32[]{:S(2)}, u32[]{:S(2)}) collective-permute-start(bf16[1,128,768]{2,1,0:T(8,128)(2,1)S(1)} %slice_add_fusion.2), channel_id=1, source_target_pairs={{0,8},{1,9},{2,10},{3,11},{4,12},{5,13},{6,14},{7,15},{8,0},{9,1},... | collective-permute-start | bytes 589832 | tf_op jit(solution)/shard_map/ppermute | solution.py:45
  155.0 24.9 %collective-permute-done.4 = bf16[1,128,768]{2,1,0:T(8,128)(2,1)} collective-permute-done((bf16[1,128,768]{2,1,0:T(8,128)(2,1)S(1)}, bf16[1,128,768]{2,1,0:T(8,128)(2,1)}, u32[]{:S(2)}, u32[]{:S(2)}) %collective-permute-start.4) | collective-permute-done | bytes 196640 | tf_op jit(solution)/shard_map/ppermute | solution.py:45
  179.9 1.6 fusion.4
  181.6 0.9 collective-permute-start.7
  182.4 0.8 collective-permute-start.6
  183.6 3.7 %collective-permute-done.7 = f32[256,128]{1,0:T(8,128)S(1)} collective-permute-done((f32[256,128]{1,0:T(8,128)S(1)}, f32[256,128]{1,0:T(8,128)S(1)}, u32[]{:S(2)}, u32[]{:S(2)}) %collective-permute-start.7) | collective-permute-done | bytes 131104 | tf_op jit(solution)/shard_map/ppermute | solution.py:45
  187.3 2.9 %collective-permute-done.6 = f32[256,128]{1,0:T(8,128)S(1)} collective-permute-done((f32[256,128]{1,0:T(8,128)S(1)}, f32[256,128]{1,0:T(8,128)S(1)}, u32[]{:S(2)}, u32[]{:S(2)}) %collective-permute-start.6) | collective-permute-done | bytes 131104 | tf_op jit(solution)/shard_map/ppermute | solution.py:45
  190.3 1.2 collective-permute-start.8
  192.2 2.3 collective-permute-done.15
  194.6 1.6 collective-permute-done.9
  196.2 3.8 %all-to-all-start.2 = ((bf16[16,64,512]{2,1,0:T(8,128)(2,1)}), bf16[16,64,512]{2,1,0:T(8,128)(2,1)S(1)}, u32[]{:S(2)}, u32[]{:S(2)}) async-start(bf16[16,64,512]{2,1,0:T(8,128)(2,1)} %get-tuple-element.61), calls=%async_computation.2 | async-start | bytes 2097152 | tf_op jit(solution)/shard_map/all_to_all | solution.py:488
  200.1 19.6 %attend.2 = (f32[1024,128]{1,0:T(8,128)S(1)}, bf16[128,640]{1,0:T(8,128)(2,1)S(1)}) custom-call(bf16[1024,2560]{1,0:T(8,128)(2,1)} %bitcast.2.buf_ref, bf16[1024,128]{1,0:T(8,128)(2,1)S(1)} %pad_maximum_fusion.2.u_ref, bf16[128,768]{1,0:T(8,128)(2,1)S(1)} %fusion.1.bq_ref.bv_ref, bf16[128,768]{1,0:T(8,128)(2,1)S(1)} %fusion.1.bq_ref.bv_ref), custom_call_target="tpu_custom_call" | custom-call | flops 52428800000 | bytes 5242880 | tf_op jit(solution)/shard_map/attend/pallas_call | solution.py:156
  219.7 0.8 copy-done.17
  220.5 2.6 collective-permute-start.16
  223.1 1.0 copy-done.18
  224.1 3.6 %attend.3 = (f32[1024,128]{1,0:T(8,128)S(1)}, bf16[128,128]{1,0:T(8,128)(2,1)S(1)}) custom-call(bf16[1024,512]{1,0:T(8,128)(2,1)S(1)} %bitcast.20, bf16[1024,128]{1,0:T(8,128)(2,1)S(1)} %pad_maximum_fusion.2.u_ref, bf16[128,768]{1,0:T(8,128)(2,1)S(1)} %fusion.1.bq_ref.bv_ref, bf16[128,768]{1,0:T(8,128)(2,1)S(1)} %fusion.1.bq_ref.bv_ref, ...), custom_call_target="tpu_custom_call" | custom-call | flops 10485760000 | bytes 1048576 | tf_op jit(solution)/shard_map/attend/pallas_call | solution.py:156
  227.8 5.6 %collective-permute-done.16.refs_2_ = bf16[128,640]{1,0:T(8,128)(2,1)S(1)} collective-permute-done((bf16[128,640]{1,0:T(8,128)(2,1)S(1)}, bf16[128,640]{1,0:T(8,128)(2,1)S(1)}, u32[]{:S(2)}, u32[]{:S(2)}) %collective-permute-start.16) | collective-permute-done | bytes 163872 | tf_op jit(solution)/shard_map/ppermute | solution.py:45
  233.4 0.8 collective-permute-start.23
  234.2 0.8 collective-permute-start.22
  235.4 1.6 collective-permute-start.17
  237.0 2.2 collective-permute-done.23
  239.2 2.9 collective-permute-done.22
  242.3 1.4 collective-permute-start.25
  244.1 2.8 collective-permute-done.25.refs_2_
  246.9 1.1 collective-permute-done.26.refs_3_
  248.0 1.0 slots.1.refs_0_
  249.0 1.4 collective-permute-start.27
  251.0 2.5 collective-permute-start.29
  253.5 1.1 owner_sums.2
  255.4 5.0 %collective-permute-done.27.refs_1_ = bf16[128,896]{1,0:T(8,128)(2,1)S(1)} collective-permute-done((bf16[128,896]{1,0:T(8,128)(2,1)S(1)}, bf16[128,896]{1,0:T(8,128)(2,1)S(1)}, u32[]{:S(2)}, u32[]{:S(2)}) %collective-permute-start.27) | collective-permute-done | bytes 229408 | tf_op jit(solution)/shard_map/ppermute | solution.py:45
  260.8 8.8 %collective-permute-done.28.refs_2_ = bf16[128,896]{1,0:T(8,128)(2,1)S(1)} collective-permute-done((bf16[128,896]{1,0:T(8,128)(2,1)S(1)}, bf16[128,896]{1,0:T(8,128)(2,1)S(1)}, u32[]{:S(2)}, u32[]{:S(2)}) %collective-permute-start.28) | collective-permute-done | bytes 229408 | tf_op jit(solution)/shard_map/ppermute | solution.py:45
  269.7 1.2 owner_sums.3
  271.0 1.2 collective-permute-start.31
  273.5 5.9 %collective-permute-done.31.refs_6_ = bf16[128,896]{1,0:T(8,128)(2,1)S(1)} collective-permute-done((bf16[128,896]{1,0:T(8,128)(2,1)S(1)}, bf16[128,896]{1,0:T(8,128)(2,1)S(1)}, u32[]{:S(2)}, u32[]{:S(2)}) %collective-permute-start.31) | collective-permute-done | bytes 229408 | tf_op jit(solution)/shard_map/ppermute | solution.py:45
  279.5 4.0 %collective-permute-done.32.refs_7_ = bf16[128,896]{1,0:T(8,128)(2,1)S(1)} collective-permute-done((bf16[128,896]{1,0:T(8,128)(2,1)S(1)}, bf16[128,896]{1,0:T(8,128)(2,1)S(1)}, u32[]{:S(2)}, u32[]{:S(2)}) %collective-permute-start.32) | collective-permute-done | bytes 229408 | tf_op jit(solution)/shard_map/ppermute | solution.py:45
  283.5 6.2 %adam.1 = (f32[1,4,64,3072]{3,2,1,0:T(8,128)}, f32[1,4,64,3072]{3,2,1,0:T(8,128)}, f32[1,4,64,3072]{3,2,1,0:T(8,128)}) custom-call(s32[1]{0:T(128)} %bitcast.where_ref, s32[1]{0:T(128)S(6)} %copy.14.count_ref, bf16[128,640]{1,0:T(8,128)(2,1)S(1)} %get-tuple-element.57.refs_0_, bf16[128,640]{1,0:T(8,128)(2,1)S(1)} %collective-permute-done.18.refs_1_, ...), custom_call_target="tpu_custom_call" | custom-call | bytes 18874368 | tf_op jit(solution)/shard_map/adam/pallas_call | solution.py:228
  (91 shorter events, 9.5 us)
Async XLA Ops:
  3.1 2.3 copy-start.11
  3.1 2.3 copy-start.12
  3.1 2.3 collective-permute-start
  6.1 7.5 %copy-start.4 = (bf16[4,64,3072]{2,1,0:T(8,128)(2,1)S(1)}, bf16[4,64,3072]{2,1,0:T(8,128)(2,1)}, u32[]{:S(2)}) copy-start(bf16[4,64,3072]{2,1,0:T(8,128)(2,1)} %query_ref.1) | copy-start | bytes 4718596
  6.1 7.5 %copy-start.8 = (s32[4]{0:T(128)S(1)}, s32[4]{0:T(128)}, u32[]{:S(2)}) copy-start(s32[4]{0:T(128)} %steps_ref.1) | copy-start | bytes 52
  6.1 39.5 %all-to-all-start.1 = ((bf16[16,64,768]{2,1,0:T(8,128)(2,1)}), bf16[16,64,768]{2,1,0:T(8,128)(2,1)S(1)}, u32[]{:S(2)}, u32[]{:S(2)}) async-start(bf16[16,64,768]{2,1,0:T(8,128)(2,1)} %bitcast.23), calls=%async_computation.1 | async-start | bytes 3145728 | tf_op jit(solution)/shard_map/all_to_all | solution.py:467
  45.6 9.3 %copy-start.16 = (bf16[128,768]{1,0:T(8,128)(2,1)S(1)}, bf16[128,768]{1,0:T(8,128)(2,1)}, u32[]{:S(2)}) copy-start(bf16[128,768]{1,0:T(8,128)(2,1)} %copy-done.15) | copy-start | bytes 589828
  45.6 11.3 %copy-start.14 = (bf16[128,768]{1,0:T(8,128)(2,1)S(1)}, bf16[128,768]{1,0:T(8,128)(2,1)}, u32[]{:S(2)}) copy-start(bf16[128,768]{1,0:T(8,128)(2,1)} %copy-done.13) | copy-start | bytes 589828
  45.6 49.8 %copy-start.6 = (bf16[128,768]{1,0:T(8,128)(2,1)S(1)}, bf16[128,768]{1,0:T(8,128)(2,1)}, u32[]{:S(2)}) copy-start(bf16[128,768]{1,0:T(8,128)(2,1)} %copy-done.5) | copy-start | bytes 589828
  45.6 49.8 %copy-start.7 = (s32[4]{0:T(128)S(1)}, s32[4]{0:T(128)}, u32[]{:S(2)}) copy-start(s32[4]{0:T(128)} %ids_ref.7) | copy-start | bytes 52
  45.6 58.8 %copy-start.10 = (bf16[128,768]{1,0:T(8,128)(2,1)S(1)}, bf16[128,768]{1,0:T(8,128)(2,1)}, u32[]{:S(2)}) copy-start(bf16[128,768]{1,0:T(8,128)(2,1)} %copy-done.9) | copy-start | bytes 589828
  45.6 150.6 %all-to-all-start = ((bf16[16,64,2560]{2,1,0:T(8,128)(2,1)}), bf16[16,64,2560]{2,1,0:T(8,128)(2,1)}, u32[]{:S(2)}, u32[]{:S(2)}) async-start(bf16[16,64,2560]{2,1,0:T(8,128)(2,1)} %get-tuple-element.38), calls=%async_computation | async-start | bytes 10485760 | tf_op jit(solution)/shard_map/all_to_all | solution.py:488
  54.9 36.9 %collective-permute-start.1 = (bf16[128,768]{1,0:T(8,128)(2,1)S(1)}, bf16[128,768]{1,0:T(8,128)(2,1)S(1)}, u32[]{:S(2)}, u32[]{:S(2)}) collective-permute-start(bf16[128,768]{1,0:T(8,128)(2,1)S(1)} %copy-done.16), channel_id=1, source_target_pairs={{0,2},{1,3},{2,0},{3,1},{4,6},{5,7},{6,4},{7,5},{8,10},{9,11},{10,... | collective-permute-start | bytes 589832 | tf_op jit(solution)/shard_map/ppermute | solution.py:45
  56.9 38.5 %collective-permute-start.2 = (bf16[128,768]{1,0:T(8,128)(2,1)S(1)}, bf16[128,768]{1,0:T(8,128)(2,1)S(1)}, u32[]{:S(2)}, u32[]{:S(2)}) collective-permute-start(bf16[128,768]{1,0:T(8,128)(2,1)S(1)} %copy-done.14), channel_id=1, source_target_pairs={{0,3},{1,2},{2,1},{3,0},{4,7},{5,6},{6,5},{7,4},{8,11},{9,10},{10,... | collective-permute-start | bytes 589832 | tf_op jit(solution)/shard_map/ppermute | solution.py:45
  96.1 52.8 %collective-permute-start.3 = (bf16[2,128,768]{2,1,0:T(8,128)(2,1)S(1)}, bf16[2,128,768]{2,1,0:T(8,128)(2,1)S(1)}, u32[]{:S(2)}, u32[]{:S(2)}) collective-permute-start(bf16[2,128,768]{2,1,0:T(8,128)(2,1)S(1)} %get-tuple-element.49), channel_id=1, source_target_pairs={{0,4},{1,5},{2,6},{3,7},{4,0},{5,1},{6,2},{7,3},{8,12},{9,13},{10,... | collective-permute-start | bytes 1179656 | tf_op jit(solution)/shard_map/ppermute | solution.py:45
  96.2 58.0 %collective-permute-start.11 = (bf16[128,768]{1,0:T(8,128)(2,1)}, bf16[128,768]{1,0:T(8,128)(2,1)S(1)}, u32[]{:S(2)}, u32[]{:S(2)}) collective-permute-start(bf16[128,768]{1,0:T(8,128)(2,1)} %copy-done.12), channel_id=1, source_target_pairs={{0,1},{1,0},{2,3},{3,2},{4,5},{5,4},{6,7},{7,6},{8,9},{9,8},{10,11... | collective-permute-start | bytes 589832 | tf_op jit(solution)/shard_map/ppermute | solution.py:45
  104.4 49.7 %collective-permute-start.12 = (bf16[128,768]{1,0:T(8,128)(2,1)}, bf16[128,768]{1,0:T(8,128)(2,1)S(1)}, u32[]{:S(2)}, u32[]{:S(2)}) collective-permute-start(bf16[128,768]{1,0:T(8,128)(2,1)} %copy-done.11), channel_id=1, source_target_pairs={{0,2},{1,3},{2,0},{3,1},{4,6},{5,7},{6,4},{7,5},{8,10},{9,11},{10,... | collective-permute-start | bytes 589832 | tf_op jit(solution)/shard_map/ppermute | solution.py:45
  104.4 49.7 %collective-permute-start.13 = (bf16[128,768]{1,0:T(8,128)(2,1)S(1)}, bf16[128,768]{1,0:T(8,128)(2,1)S(1)}, u32[]{:S(2)}, u32[]{:S(2)}) collective-permute-start(bf16[128,768]{1,0:T(8,128)(2,1)S(1)} %copy-done.10), channel_id=1, source_target_pairs={{0,3},{1,2},{2,1},{3,0},{4,7},{5,6},{6,5},{7,4},{8,11},{9,10},{10,... | collective-permute-start | bytes 589832 | tf_op jit(solution)/shard_map/ppermute | solution.py:45
  149.7 30.3 %collective-permute-start.4 = (bf16[1,128,768]{2,1,0:T(8,128)(2,1)S(1)}, bf16[1,128,768]{2,1,0:T(8,128)(2,1)}, u32[]{:S(2)}, u32[]{:S(2)}) collective-permute-start(bf16[1,128,768]{2,1,0:T(8,128)(2,1)S(1)} %slice_add_fusion.2), channel_id=1, source_target_pairs={{0,8},{1,9},{2,10},{3,11},{4,12},{5,13},{6,14},{7,15},{8,0},{9,1},... | collective-permute-start | bytes 589832 | tf_op jit(solution)/shard_map/ppermute | solution.py:45
  154.9 28.6 %collective-permute-start.14 = (bf16[2,128,768]{2,1,0:T(8,128)(2,1)S(1)}, bf16[2,128,768]{2,1,0:T(8,128)(2,1)S(1)}, u32[]{:S(2)}, u32[]{:S(2)}) collective-permute-start(bf16[2,128,768]{2,1,0:T(8,128)(2,1)S(1)} %get-tuple-element.55), channel_id=1, source_target_pairs={{0,4},{1,5},{2,6},{3,7},{4,0},{5,1},{6,2},{7,3},{8,12},{9,13},{10,... | collective-permute-start | bytes 1179656 | tf_op jit(solution)/shard_map/ppermute | solution.py:45
  181.6 5.8 %collective-permute-start.7 = (f32[256,128]{1,0:T(8,128)S(1)}, f32[256,128]{1,0:T(8,128)S(1)}, u32[]{:S(2)}, u32[]{:S(2)}) collective-permute-start(f32[256,128]{1,0:T(8,128)S(1)} %get-tuple-element.81), channel_id=1, source_target_pairs={{0,3},{1,2},{2,1},{3,0},{4,7},{5,6},{6,5},{7,4},{8,11},{9,10},{10,... | collective-permute-start | bytes 393224 | tf_op jit(solution)/shard_map/ppermute | solution.py:45
  182.4 7.8 %collective-permute-start.6 = (f32[256,128]{1,0:T(8,128)S(1)}, f32[256,128]{1,0:T(8,128)S(1)}, u32[]{:S(2)}, u32[]{:S(2)}) collective-permute-start(f32[256,128]{1,0:T(8,128)S(1)} %get-tuple-element.82), channel_id=1, source_target_pairs={{0,2},{1,3},{2,0},{3,1},{4,6},{5,7},{6,4},{7,5},{8,10},{9,11},{10,... | collective-permute-start | bytes 393224 | tf_op jit(solution)/shard_map/ppermute | solution.py:45
  183.3 7.0 %collective-permute-start.5 = (f32[256,128]{1,0:T(8,128)S(1)}, f32[256,128]{1,0:T(8,128)S(1)}, u32[]{:S(2)}, u32[]{:S(2)}) collective-permute-start(f32[256,128]{1,0:T(8,128)S(1)} %get-tuple-element.80), channel_id=1, source_target_pairs={{0,1},{1,0},{2,3},{3,2},{4,5},{5,4},{6,7},{7,6},{8,9},{9,8},{10,11... | collective-permute-start | bytes 393224 | tf_op jit(solution)/shard_map/ppermute | solution.py:45
  183.5 11.0 %collective-permute-start.15 = (bf16[1,128,768]{2,1,0:T(8,128)(2,1)S(1)}, bf16[1,128,768]{2,1,0:T(8,128)(2,1)S(1)}, u32[]{:S(2)}, u32[]{:S(2)}) collective-permute-start(bf16[1,128,768]{2,1,0:T(8,128)(2,1)S(1)} %slice_add_fusion), channel_id=1, source_target_pairs={{0,8},{1,9},{2,10},{3,11},{4,12},{5,13},{6,14},{7,15},{8,0},{9,1},... | collective-permute-start | bytes 589832 | tf_op jit(solution)/shard_map/ppermute | solution.py:45
  190.3 4.3 %collective-permute-start.8 = (bf16[256,128]{1,0:T(8,128)(2,1)S(1)}, bf16[256,128]{1,0:T(8,128)(2,1)S(1)}, u32[]{:S(2)}, u32[]{:S(2)}) collective-permute-start(bf16[256,128]{1,0:T(8,128)(2,1)S(1)} %add_convert_fusion.1), channel_id=1, source_target_pairs={{0,3},{1,2},{2,1},{3,0},{4,7},{5,6},{6,5},{7,4},{8,11},{9,10},{10,... | collective-permute-start | bytes 196616 | tf_op jit(solution)/shard_map/ppermute | solution.py:45
  191.4 4.7 %collective-permute-start.9 = (bf16[256,128]{1,0:T(8,128)(2,1)S(1)}, bf16[256,128]{1,0:T(8,128)(2,1)S(1)}, u32[]{:S(2)}, u32[]{:S(2)}) collective-permute-start(bf16[256,128]{1,0:T(8,128)(2,1)S(1)} %add_convert_fusion.1), channel_id=1, source_target_pairs={{0,2},{1,3},{2,0},{3,1},{4,6},{5,7},{6,4},{7,5},{8,10},{9,11},{10,... | collective-permute-start | bytes 196616 | tf_op jit(solution)/shard_map/ppermute | solution.py:45
  192.0 4.2 %collective-permute-start.10 = (bf16[256,128]{1,0:T(8,128)(2,1)S(1)}, bf16[256,128]{1,0:T(8,128)(2,1)S(1)}, u32[]{:S(2)}, u32[]{:S(2)}) collective-permute-start(bf16[256,128]{1,0:T(8,128)(2,1)S(1)} %add_convert_fusion.1), channel_id=1, source_target_pairs={{0,1},{1,0},{2,3},{3,2},{4,5},{5,4},{6,7},{7,6},{8,9},{9,8},{10,11... | collective-permute-start | bytes 196616 | tf_op jit(solution)/shard_map/ppermute | solution.py:45
  196.2 26.8 %all-to-all-start.2 = ((bf16[16,64,512]{2,1,0:T(8,128)(2,1)}), bf16[16,64,512]{2,1,0:T(8,128)(2,1)S(1)}, u32[]{:S(2)}, u32[]{:S(2)}) async-start(bf16[16,64,512]{2,1,0:T(8,128)(2,1)} %get-tuple-element.61), calls=%async_computation.2 | async-start | bytes 2097152 | tf_op jit(solution)/shard_map/all_to_all | solution.py:488
  220.5 12.9 %collective-permute-start.16 = (bf16[128,640]{1,0:T(8,128)(2,1)S(1)}, bf16[128,640]{1,0:T(8,128)(2,1)S(1)}, u32[]{:S(2)}, u32[]{:S(2)}) collective-permute-start(bf16[128,640]{1,0:T(8,128)(2,1)S(1)} %get-tuple-element.56.refs_0_), channel_id=1, source_target_pairs={{0,8},{1,9},{2,10},{3,11},{4,12},{5,13},{6,14},{7,15},{8,0},{9,1},... | collective-permute-start | bytes 491528 | tf_op jit(solution)/shard_map/ppermute | solution.py:45
  224.1 59.4 %copy-start.3 = (f32[1,4,64,3072]{3,2,1,0:T(8,128)S(1)}, f32[1,4,64,3072]{3,2,1,0:T(8,128)}, u32[]{:S(2)}) copy-start(f32[1,4,64,3072]{3,2,1,0:T(8,128)} %refs_10_.1) | copy-start | bytes 9437188
  233.4 50.1 %copy-start.2 = (f32[1,4,64,3072]{3,2,1,0:T(8,128)S(1)}, f32[1,4,64,3072]{3,2,1,0:T(8,128)}, u32[]{:S(2)}) copy-start(f32[1,4,64,3072]{3,2,1,0:T(8,128)} %refs_9_.1) | copy-start | bytes 9437188
  233.4 5.8 %collective-permute-start.23 = (f32[256,128]{1,0:T(8,128)S(1)}, f32[256,128]{1,0:T(8,128)S(1)}, u32[]{:S(2)}, u32[]{:S(2)}) collective-permute-start(f32[256,128]{1,0:T(8,128)S(1)} %get-tuple-element.78), channel_id=1, source_target_pairs={{0,3},{1,2},{2,1},{3,0},{4,7},{5,6},{6,5},{7,4},{8,11},{9,10},{10,... | collective-permute-start | bytes 393224 | tf_op jit(solution)/shard_map/ppermute | solution.py:45
  234.2 7.9 %collective-permute-start.22 = (f32[256,128]{1,0:T(8,128)S(1)}, f32[256,128]{1,0:T(8,128)S(1)}, u32[]{:S(2)}, u32[]{:S(2)}) collective-permute-start(f32[256,128]{1,0:T(8,128)S(1)} %get-tuple-element.79), channel_id=1, source_target_pairs={{0,2},{1,3},{2,0},{3,1},{4,6},{5,7},{6,4},{7,5},{8,10},{9,11},{10,... | collective-permute-start | bytes 393224 | tf_op jit(solution)/shard_map/ppermute | solution.py:45
  235.1 7.0 %collective-permute-start.21 = (f32[256,128]{1,0:T(8,128)S(1)}, f32[256,128]{1,0:T(8,128)S(1)}, u32[]{:S(2)}, u32[]{:S(2)}) collective-permute-start(f32[256,128]{1,0:T(8,128)S(1)} %get-tuple-element.77), channel_id=1, source_target_pairs={{0,1},{1,0},{2,3},{3,2},{4,5},{5,4},{6,7},{7,6},{8,9},{9,8},{10,11... | collective-permute-start | bytes 393224 | tf_op jit(solution)/shard_map/ppermute | solution.py:45
  235.4 18.1 %collective-permute-start.17 = (bf16[2,128,640]{2,1,0:T(8,128)(2,1)S(1)}, bf16[2,128,640]{2,1,0:T(8,128)(2,1)S(1)}, u32[]{:S(2)}, u32[]{:S(2)}) collective-permute-start(bf16[2,128,640]{2,1,0:T(8,128)(2,1)S(1)} %pad_maximum_fusion.1), channel_id=1, source_target_pairs={{0,4},{1,5},{2,6},{3,7},{4,0},{5,1},{6,2},{7,3},{8,12},{9,13},{10,... | collective-permute-start | bytes 983048 | tf_op jit(solution)/shard_map/ppermute | solution.py:45
  242.1 1.9 collective-permute-start.24
  242.3 4.6 %collective-permute-start.25 = (bf16[256,128]{1,0:T(8,128)(2,1)S(1)}, bf16[256,128]{1,0:T(8,128)(2,1)S(1)}, u32[]{:S(2)}, u32[]{:S(2)}) collective-permute-start(bf16[256,128]{1,0:T(8,128)(2,1)S(1)} %add_convert_fusion.refs_0_), channel_id=1, source_target_pairs={{0,2},{1,3},{2,0},{3,1},{4,6},{5,7},{6,4},{7,5},{8,10},{9,11},{10,... | collective-permute-start | bytes 196616 | tf_op jit(solution)/shard_map/ppermute | solution.py:45
  243.6 4.4 %collective-permute-start.26 = (bf16[256,128]{1,0:T(8,128)(2,1)S(1)}, bf16[256,128]{1,0:T(8,128)(2,1)S(1)}, u32[]{:S(2)}, u32[]{:S(2)}) collective-permute-start(bf16[256,128]{1,0:T(8,128)(2,1)S(1)} %add_convert_fusion.refs_0_), channel_id=1, source_target_pairs={{0,3},{1,2},{2,1},{3,0},{4,7},{5,6},{6,5},{7,4},{8,11},{9,10},{10,... | collective-permute-start | bytes 196616 | tf_op jit(solution)/shard_map/ppermute | solution.py:45
  248.0 35.5 %copy-start.1 = (f32[1,4,64,3072]{3,2,1,0:T(8,128)S(1)}, f32[1,4,64,3072]{3,2,1,0:T(8,128)}, u32[]{:S(2)}) copy-start(f32[1,4,64,3072]{3,2,1,0:T(8,128)} %refs_8_.1) | copy-start | bytes 9437188
  249.0 11.4 %collective-permute-start.27 = (bf16[128,896]{1,0:T(8,128)(2,1)S(1)}, bf16[128,896]{1,0:T(8,128)(2,1)S(1)}, u32[]{:S(2)}, u32[]{:S(2)}) collective-permute-start(bf16[128,896]{1,0:T(8,128)(2,1)S(1)} %slots.1.refs_0_), channel_id=1, source_target_pairs={{0,4},{1,5},{2,6},{3,7},{4,0},{5,1},{6,2},{7,3},{8,12},{9,13},{10,... | collective-permute-start | bytes 688136 | tf_op jit(solution)/shard_map/ppermute | solution.py:45
  250.4 19.2 %collective-permute-start.28 = (bf16[128,896]{1,0:T(8,128)(2,1)S(1)}, bf16[128,896]{1,0:T(8,128)(2,1)S(1)}, u32[]{:S(2)}, u32[]{:S(2)}) collective-permute-start(bf16[128,896]{1,0:T(8,128)(2,1)S(1)} %slots.1.refs_0_), channel_id=1, source_target_pairs={{0,8},{1,9},{2,10},{3,11},{4,12},{5,13},{6,14},{7,15},{8,0},{9,1},... | collective-permute-start | bytes 688136 | tf_op jit(solution)/shard_map/ppermute | solution.py:45
  251.0 18.7 %collective-permute-start.29 = (bf16[128,896]{1,0:T(8,128)(2,1)S(1)}, bf16[128,896]{1,0:T(8,128)(2,1)S(1)}, u32[]{:S(2)}, u32[]{:S(2)}) collective-permute-start(bf16[128,896]{1,0:T(8,128)(2,1)S(1)} %slots.1.refs_0_), channel_id=1, source_target_pairs={{0,12},{1,13},{2,14},{3,15},{4,8},{5,9},{6,10},{7,11},{8,4},{9,5},... | collective-permute-start | bytes 688136 | tf_op jit(solution)/shard_map/ppermute | solution.py:45
  254.6 15.1 %collective-permute-start.18 = (bf16[128,640]{1,0:T(8,128)(2,1)S(1)}, bf16[128,640]{1,0:T(8,128)(2,1)S(1)}, u32[]{:S(2)}, u32[]{:S(2)}) collective-permute-start(bf16[128,640]{1,0:T(8,128)(2,1)S(1)} %get-tuple-element.58), channel_id=1, source_target_pairs={{0,1},{1,0},{2,3},{3,2},{4,5},{5,4},{6,7},{7,6},{8,9},{9,8},{10,11... | collective-permute-start | bytes 491528 | tf_op jit(solution)/shard_map/ppermute | solution.py:45
  254.7 15.0 %collective-permute-start.19 = (bf16[128,640]{1,0:T(8,128)(2,1)S(1)}, bf16[128,640]{1,0:T(8,128)(2,1)S(1)}, u32[]{:S(2)}, u32[]{:S(2)}) collective-permute-start(bf16[128,640]{1,0:T(8,128)(2,1)S(1)} %get-tuple-element.59), channel_id=1, source_target_pairs={{0,2},{1,3},{2,0},{3,1},{4,6},{5,7},{6,4},{7,5},{8,10},{9,11},{10,... | collective-permute-start | bytes 491528 | tf_op jit(solution)/shard_map/ppermute | solution.py:45
  260.4 9.2 %collective-permute-start.20 = (bf16[128,640]{1,0:T(8,128)(2,1)S(1)}, bf16[128,640]{1,0:T(8,128)(2,1)S(1)}, u32[]{:S(2)}, u32[]{:S(2)}) collective-permute-start(bf16[128,640]{1,0:T(8,128)(2,1)S(1)} %get-tuple-element.60), channel_id=1, source_target_pairs={{0,3},{1,2},{2,1},{3,0},{4,7},{5,6},{6,5},{7,4},{8,11},{9,10},{10,... | collective-permute-start | bytes 491528 | tf_op jit(solution)/shard_map/ppermute | solution.py:45
  270.9 2.6 collective-permute-start.30
  271.0 8.5 %collective-permute-start.31 = (bf16[128,896]{1,0:T(8,128)(2,1)S(1)}, bf16[128,896]{1,0:T(8,128)(2,1)S(1)}, u32[]{:S(2)}, u32[]{:S(2)}) collective-permute-start(bf16[128,896]{1,0:T(8,128)(2,1)S(1)} %get-tuple-element.71), channel_id=1, source_target_pairs={{0,2},{1,3},{2,0},{3,1},{4,6},{5,7},{6,4},{7,5},{8,10},{9,11},{10,... | collective-permute-start | bytes 688136 | tf_op jit(solution)/shard_map/ppermute | solution.py:45
  272.2 11.2 %collective-permute-start.32 = (bf16[128,896]{1,0:T(8,128)(2,1)S(1)}, bf16[128,896]{1,0:T(8,128)(2,1)S(1)}, u32[]{:S(2)}, u32[]{:S(2)}) collective-permute-start(bf16[128,896]{1,0:T(8,128)(2,1)S(1)} %get-tuple-element.72), channel_id=1, source_target_pairs={{0,3},{1,2},{2,1},{3,0},{4,7},{5,6},{6,5},{7,4},{8,11},{9,10},{10,... | collective-permute-start | bytes 688136 | tf_op jit(solution)/shard_map/ppermute | solution.py:45
  (9 other events, 9.7 us)

commit v3 on v2

--- a/solution.py
+++ b/solution.py
@@ -176,7 +176,7 @@
         ],
         compiler_params=pltpu.CompilerParams(vmem_limit_bytes=VMEM_LIMIT),
         cost_estimate=pl.CostEstimate(
-            flops=count * length * length * 10000,
+            flops=count * length * length * 10 * HD,
             bytes_accessed=2 * received.size,
             transcendentals=count * length * length,
         ),
@@ -187,49 +187,49 @@
 def adam_kernel(per, where_ref, count_ref, *refs):
     early_refs, late_refs, refs = refs[:per], refs[per : 2 * per], refs[2 * per :]
     adapter_ref, first_ref, second_ref, new_adapter_ref, new_first_ref, new_second_ref = refs
-    cols = adapter_ref.shape[-1]
-    early = early_refs[0].shape[-1]
     first_corr = 1.0 - beta_one**adam_step
     second_corr = 1.0 - beta_two**adam_step
     share = 1.0 / count_ref[0].astype(F32)
 
-    def step(mat, where, grad):
+    def step(mat, grad_ref):
+        row = mat // 2 * RANK
+        grad = grad_ref[row : row + RANK, :]
         grad = grad.astype(F32) * share
-        new_first = beta_one * first_ref[0, mat, :, where] + (1.0 - beta_one) * grad
-        new_second = beta_two * second_ref[0, mat, :, where] + (1.0 - beta_two) * grad * grad
-        new_first_ref[0, mat, :, where] = new_first
-        new_second_ref[0, mat, :, where] = new_second
+        new_first = beta_one * first_ref[0, mat] + (1.0 - beta_one) * grad
+        new_second = beta_two * second_ref[0, mat] + (1.0 - beta_two) * grad * grad
+        new_first_ref[0, mat] = new_first
+        new_second_ref[0, mat] = new_second
         corrected = new_second * (1.0 / second_corr)
         root = corrected * lax.rsqrt(corrected)
-        new_adapter_ref[0, mat, :, where] = adapter_ref[0, mat, :, where] - (
-            learn_rate / first_corr
-        ) * new_first / (root + adam_eps)
+        new_adapter_ref[0, mat] = adapter_ref[0, mat] - (learn_rate / first_corr) * new_first / (
+            root + adam_eps
+        )
 
     for m in range(per):
 
         @pl.when(pl.program_id(0) == m)
         def _(m=m):
-            step(0, slice(0, cols), late_refs[m][:, :cols])
-            step(1, slice(0, early), early_refs[m][...])
-            step(1, slice(early, cols), late_refs[m][:, cols:])
+            for half in range(2):
+                step(2 * half, late_refs[m])
+                step(2 * half + 1, early_refs[m])
 
 
 def adam(place, counts, early, late, adapters, first_moment, second_moment):
     per = len(early)
     cols = adapters.shape[-1] // per
     state = pl.BlockSpec(
-        (1, 2, RANK, cols),
-        lambda m, p, where_ref, count_ref: (0, p, 0, jnp.bitwise_xor(m, where_ref[0])),
+        (1, 4, RANK, cols),
+        lambda m, where_ref, count_ref: (0, 0, 0, jnp.bitwise_xor(m, where_ref[0])),
     )
     grads = [
-        pl.BlockSpec((RANK, grad.shape[1]), lambda m, p, where_ref, count_ref: (p, 0))
+        pl.BlockSpec(grad.shape, lambda m, where_ref, count_ref: (0, 0))
         for grad in (*early, *late)
     ]
     return pl.pallas_call(
         functools.partial(adam_kernel, per),
         grid_spec=pltpu.PrefetchScalarGridSpec(
             num_scalar_prefetch=2,
-            grid=(per, 2),
+            grid=(per,),
             in_specs=grads + [state] * 3,
             out_specs=[state] * 3,
         ),
@@ -270,8 +270,7 @@
 
 
 def slot_kernel(per, where_ref, *refs):
-    row_refs, (hidden_ref, last_ref, out_ref, total_s) = refs[:per], refs[per:]
-    cols = hidden_ref.shape[1]
+    row_refs, (hidden_ref, out_ref, total_s) = refs[:per], refs[per:]
     for m, row_ref in enumerate(row_refs):
 
         @pl.when(pl.program_id(0) == m)
@@ -282,11 +281,10 @@
             if m < per - 1:
                 total_s[...] = part
             else:
-                out_ref[:, :cols] = (adapter_scale * part).astype(out_ref.dtype)
-                out_ref[:, cols:] = last_ref[...]
-
-
-def slots_of_hidden(place, blocks, hidden, last):
+                out_ref[...] = (adapter_scale * part).astype(out_ref.dtype)
+
+
+def slots_of_hidden(place, blocks, hidden, send_type):
     per = len(blocks)
     rows, width = blocks[0].shape
     cols = hidden.shape[1]
@@ -297,24 +295,21 @@
             num_scalar_prefetch=1,
             grid=(per,),
             in_specs=[pl.BlockSpec((rows, width), whole)] * per
-            + [
-                pl.BlockSpec((rows, cols), lambda m, where_ref: (jnp.bitwise_xor(m, where_ref[0]), 0)),
-                pl.BlockSpec(last.shape, whole),
-            ],
-            out_specs=pl.BlockSpec((width, cols + last.shape[1]), whole),
+            + [pl.BlockSpec((rows, cols), lambda m, where_ref: (jnp.bitwise_xor(m, where_ref[0]), 0))],
+            out_specs=pl.BlockSpec((width, cols), whole),
             scratch_shapes=[pltpu.VMEM((width, cols), F32)],
         ),
-        out_shape=jax.ShapeDtypeStruct((width, cols + last.shape[1]), last.dtype),
+        out_shape=jax.ShapeDtypeStruct((width, cols), send_type),
         compiler_params=pltpu.CompilerParams(vmem_limit_bytes=VMEM_LIMIT),
         cost_estimate=pl.CostEstimate(
             flops=2 * rows * per * width * cols, bytes_accessed=2 * hidden.size, transcendentals=0
         ),
         name="slots",
-    )(place, *blocks, hidden, last)
-
-
-def tie(values, *others):
-    return lax.optimization_barrier((values, others))[0]
+    )(place, *blocks, hidden)
+
+
+def tie(*values):
+    return lax.optimization_barrier(values)
 
 
 def pieces_kernel(per, where_ref, adapter_ref, *out_refs):
@@ -461,25 +456,28 @@
     hidden_sent = (
         hidden_in.reshape(images, rows, per, cols).transpose(0, 2, 1, 3).reshape(size, rows, cols)
     )
-    pieces_a, pieces_b = column_pieces(place.reshape(1), adapters, per)
+    hidden_sent, spread_from = tie(hidden_sent, adapters)
+    pieces_a, pieces_b = column_pieces(place.reshape(1), spread_from, per)
     pieces_a = spread(pieces_a, size)
-    hidden_sent = tie(hidden_sent, pieces_a[1])
     hidden = lax.all_to_all(hidden_sent, "seq", 0, 0, tiled=True).reshape(length, cols)
 
     packed = pack(timesteps, frozen_query, key_base, frozen_value, out_grad, per, chunks)
 
     where = jnp.stack([zone, place])
-    pieces_a = tie(pieces_a, packed)
+    pieces_a, packed = tie(pieces_a, packed)
     a_kept, a_sent = for_images(where, tenant_ids, pieces_a)
     a_came = exchange(a_sent, per, size)
     b_kept, b_sent = for_images(where, tenant_ids, spread(pieces_b, size))
     a_rows = halve_all(a_kept, a_came, per, size)
     b_rows = halve_all(b_kept, exchange(b_sent, per, size), per, size)
 
-    packed = tie(packed, a_rows)
+    packed, a_rows = tie(packed, a_rows)
     u_total = reduce_scatter_rows(dot_nt(hidden, a_rows), place, per, size)
 
     u_rows = in_order(gather_rows(u_total, per, size), place)
+
+    packed = list(packed)
+    packed[-1], u_rows, b_rows = tie(packed[-1], u_rows, b_rows)
 
     partial_rows = None
     head = 0
@@ -489,23 +487,22 @@
         partial_rows, slot = attend(received, u_rows, b_rows, partial_rows, head, send_type)
         slots_b.append(slot)
         head += count
-    early = {0: slots_b[0]}
-    early[images // 2] = exchange(early[0], images // 2 * per, size)
-    partial_rows = tie(partial_rows, early[images // 2])
+    early = {0: jnp.concatenate(slots_b, axis=1)}
+    bits = [1 << n for n in range(images.bit_length() - 1)]
+    for bit in reversed(bits):
+        early[bit] = exchange(early[0], bit * per, size)
 
     grad_total = reduce_scatter_rows(partial_rows, place, per, size)
     grad_rows = gather_rows(grad_total, per, size)
-    bit = images // 4
-    while bit:
-        known = sorted(early)
-        came = exchange(jnp.stack([early[r] for r in known]), bit * per, size)
-        for i, r in enumerate(known):
-            early[r ^ bit] = came[i]
-        bit //= 2
-    late = slots_of_hidden(place.reshape(1), grad_rows, hidden, slots_b[1])
+    late = slots_of_hidden(place.reshape(1), grad_rows, hidden, send_type)
+    late, early[images // 2] = tie(late, early[images // 2])
+    for r in range(1, images):
+        if r not in early:
+            low = r & -r
+            early[r] = exchange(early[r ^ low], low * per, size)
     late = direct_images(late, per, images, size)
     early = owner_sums(where, tenant_ids, [early[r] for r in range(images)], per, size)
-    late = [late[0]] + tie(late[1:], early)
+    early, late = tie(early, late)
     late = owner_sums(where, tenant_ids, late, per, size)
     return tuple(
         adam(place.reshape(1), counts, early, late, adapters, first_moment, second_moment)

time: 292 us -> 284 us (0.973)
  waiting for transfers between devices: 181 us -> 166 us
  starting transfers between devices: 57.1 us -> 62.9 us
    all_to_all x1, waiting for transfers between devices: 25.9 us -> 0.01 us  [shards(): lax.all_to_all(hidden_sent, 'seq', 0, 0, tiled=True).reshape(length, cols)]
    ppermute x33 -> x34, starting transfers between devices: 36.4 us -> 46.8 us  [exchange(): return lax.ppermute(block, 'seq', [(i, i ^ flip) for i in range(size)])]
    ppermute x33 -> x34, waiting for transfers between devices: 155 us -> 164 us  [exchange(): return lax.ppermute(block, 'seq', [(i, i ^ flip) for i in range(size)])]
    all_to_all x2, starting transfers between devices: 13.1 us -> 8.74 us  [shards(): lax.all_to_all(sent, 'seq', 0, 0, tiled=True)]
  transfers between devices with their start and end apart: 36 -> 37, of which waited for: 18 -> 16; matrix products, arithmetic and copies ran while one was open for 1% -> 0% of each run, Pallas kernels for 11% -> 11%
where the time goes in v3:
time: 284 us; the launch traced here: 282 us
  waiting for transfers between devices  166 us (58%)
  starting transfers between devices  62.9 us (22%)
  Pallas kernels  41.2 us (15%)
  local copies, waits for them, and re-layouts  7.34 us (3%)
    ppermute x34, waiting for transfers between devices, exchange(): return lax.ppermute(block, 'seq', [(i, i ^ flip) for i in range(size)])  164 us
    ppermute x34, starting transfers between devices, exchange(): return lax.ppermute(block, 'seq', [(i, i ^ flip) for i in range(size)])  46.8 us
    pallas_call x2, Pallas kernels, attend(): pl.pallas_call(functools.partial(attend_kernel, first, row_block), grid=(...  23.3 us
    all_to_all x2, starting transfers between devices, shards(): lax.all_to_all(sent, 'seq', 0, 0, tiled=True)  8.74 us
    all_to_all x1, starting transfers between devices, shards(): lax.all_to_all(hidden_sent, 'seq', 0, 0, tiled=True).reshape(length, cols)  7.39 us
    pallas_call x1, Pallas kernels, pack(): pl.pallas_call(functools.partial(pack_kernel, chunks, per), grid=(images,...  6.1 us
    unnamed x31, local copies, waits for them, and re-layouts  5.79 us
  transfers between devices with their start and end apart: 37, of which 16 were waited for; matrix products, arithmetic and copies ran while one was open for 0% of the time, Pallas kernels for 11%

profile of v3, /device:TPU:0, one launch (start us, length us, event | category | flops | bytes accessed | tf_op | source)
XLA Modules:
  0.0 281.5 jit_solution(17974757921129768784)
XLA Ops:
  0.6 1.5 fusion.4
  2.1 1.2 pad_maximum_fusion
  3.3 7.4 %all-to-all-start.1 = ((bf16[16,64,768]{2,1,0:T(8,128)(2,1)}), bf16[16,64,768]{2,1,0:T(8,128)(2,1)S(1)}, u32[]{:S(2)}, u32[]{:S(2)}) async-start(bf16[16,64,768]{2,1,0:T(8,128)(2,1)} %bitcast.2), calls=%async_computation.1 | async-start | bytes 3145728 | tf_op jit(solution)/shard_map/all_to_all | solution.py:462
  10.8 1.9 copy-done
  12.7 1.3 pieces.1
  16.4 1.7 collective-permute-start.1
  18.1 6.1 %pack.1 = (bf16[16,64,2560]{2,1,0:T(8,128)(2,1)}, bf16[16,64,512]{2,1,0:T(8,128)(2,1)}) custom-call(s32[4]{0:T(128)S(1)} %copy-done.6, bf16[4,64,3072]{2,1,0:T(8,128)(2,1)S(1)} %copy-done.4, bf16[4,64,3072]{2,1,0:T(8,128)(2,1)} %key_ref.1, bf16[4,64,3072]{2,1,0:T(8,128)(2,1)} %value_ref.1, bf16[4,64,3072]{2,1,0:T(8,128)(2,1)} %grad_ref.1), custom_call_target="tpu_custom_call" | custom-call | bytes 12582912 | tf_op jit(solution)/shard_map/pack/pallas_call | solution.py:71
  24.3 6.8 %collective-permute-done.1.refs_2_ = bf16[128,768]{1,0:T(8,128)(2,1)} collective-permute-done((bf16[128,768]{1,0:T(8,128)(2,1)}, bf16[128,768]{1,0:T(8,128)(2,1)}, u32[]{:S(2)}, u32[]{:S(2)}) %collective-permute-start.1) | collective-permute-done | bytes 196640 | tf_op jit(solution)/shard_map/ppermute | solution.py:45
  31.0 5.0 %collective-permute-done.2.refs_3_ = bf16[128,768]{1,0:T(8,128)(2,1)} collective-permute-done((bf16[128,768]{1,0:T(8,128)(2,1)}, bf16[128,768]{1,0:T(8,128)(2,1)}, u32[]{:S(2)}, u32[]{:S(2)}) %collective-permute-start.2) | collective-permute-done | bytes 196640 | tf_op jit(solution)/shard_map/ppermute | solution.py:45
  36.1 1.3 for_images.2
  37.5 14.9 %collective-permute-done.3 = bf16[2,128,768]{2,1,0:T(8,128)(2,1)S(1)} collective-permute-done((bf16[2,128,768]{2,1,0:T(8,128)(2,1)S(1)}, bf16[2,128,768]{2,1,0:T(8,128)(2,1)S(1)}, u32[]{:S(2)}, u32[]{:S(2)}) %collective-permute-start.3) | collective-permute-done | bytes 393248 | tf_op jit(solution)/shard_map/ppermute | solution.py:45
  52.4 2.6 collective-permute-start.4
  55.0 9.0 %collective-permute-done.4 = bf16[1,128,768]{2,1,0:T(8,128)(2,1)S(1)} collective-permute-done((bf16[1,128,768]{2,1,0:T(8,128)(2,1)S(1)}, bf16[1,128,768]{2,1,0:T(8,128)(2,1)S(1)}, u32[]{:S(2)}, u32[]{:S(2)}) %collective-permute-start.4) | collective-permute-done | bytes 196640 | tf_op jit(solution)/shard_map/ppermute | solution.py:45
  64.1 4.9 %all-to-all-start = ((bf16[16,64,2560]{2,1,0:T(8,128)(2,1)}), bf16[16,64,2560]{2,1,0:T(8,128)(2,1)}, u32[]{:S(2)}, u32[]{:S(2)}) async-start(bf16[16,64,2560]{2,1,0:T(8,128)(2,1)} %get-tuple-element.68), calls=%async_computation | async-start | bytes 10485760 | tf_op jit(solution)/shard_map/all_to_all | solution.py:486
  69.4 1.7 collective-permute-start.12
  71.1 34.7 %collective-permute-done.12.refs_2_ = bf16[128,768]{1,0:T(8,128)(2,1)S(1)} collective-permute-done((bf16[128,768]{1,0:T(8,128)(2,1)S(1)}, bf16[128,768]{1,0:T(8,128)(2,1)S(1)}, u32[]{:S(2)}, u32[]{:S(2)}) %collective-permute-start.12) | collective-permute-done | bytes 196640 | tf_op jit(solution)/shard_map/ppermute | solution.py:45
  105.8 3.6 %collective-permute-done.13.refs_3_ = bf16[128,768]{1,0:T(8,128)(2,1)S(1)} collective-permute-done((bf16[128,768]{1,0:T(8,128)(2,1)S(1)}, bf16[128,768]{1,0:T(8,128)(2,1)S(1)}, u32[]{:S(2)}, u32[]{:S(2)}) %collective-permute-start.13) | collective-permute-done | bytes 196640 | tf_op jit(solution)/shard_map/ppermute | solution.py:45
  110.8 8.3 %collective-permute-start.5 = (f32[256,128]{1,0:T(8,128)S(1)}, f32[256,128]{1,0:T(8,128)S(1)}, u32[]{:S(2)}, u32[]{:S(2)}) collective-permute-start(f32[256,128]{1,0:T(8,128)S(1)} %get-tuple-element.110), channel_id=1, source_target_pairs={{0,1},{1,0},{2,3},{3,2},{4,5},{5,4},{6,7},{7,6},{8,9},{9,8},{10,11... | collective-permute-start | bytes 393224 | tf_op jit(solution)/shard_map/ppermute | solution.py:45
  119.1 1.7 collective-permute-start.6
  120.8 42.1 %collective-permute-done.14 = bf16[2,128,768]{2,1,0:T(8,128)(2,1)S(1)} collective-permute-done((bf16[2,128,768]{2,1,0:T(8,128)(2,1)S(1)}, bf16[2,128,768]{2,1,0:T(8,128)(2,1)S(1)}, u32[]{:S(2)}, u32[]{:S(2)}) %collective-permute-start.14) | collective-permute-done | bytes 393248 | tf_op jit(solution)/shard_map/ppermute | solution.py:45
  163.0 4.5 %collective-permute-start.15 = (bf16[1,128,768]{2,1,0:T(8,128)(2,1)S(1)}, bf16[1,128,768]{2,1,0:T(8,128)(2,1)S(1)}, u32[]{:S(2)}, u32[]{:S(2)}) collective-permute-start(bf16[1,128,768]{2,1,0:T(8,128)(2,1)S(1)} %slice_add_fusion), channel_id=1, source_target_pairs={{0,8},{1,9},{2,10},{3,11},{4,12},{5,13},{6,14},{7,15},{8,0},{9,1},... | collective-permute-start | bytes 589832 | tf_op jit(solution)/shard_map/ppermute | solution.py:45
  167.6 1.6 collective-permute-start.9
  169.5 24.4 %collective-permute-done.15 = bf16[1,128,768]{2,1,0:T(8,128)(2,1)S(1)} collective-permute-done((bf16[1,128,768]{2,1,0:T(8,128)(2,1)S(1)}, bf16[1,128,768]{2,1,0:T(8,128)(2,1)S(1)}, u32[]{:S(2)}, u32[]{:S(2)}) %collective-permute-start.15) | collective-permute-done | bytes 196640 | tf_op jit(solution)/shard_map/ppermute | solution.py:45
  194.0 3.9 %all-to-all-start.2 = ((bf16[16,64,512]{2,1,0:T(8,128)(2,1)}), bf16[16,64,512]{2,1,0:T(8,128)(2,1)S(1)}, u32[]{:S(2)}, u32[]{:S(2)}) async-start(bf16[16,64,512]{2,1,0:T(8,128)(2,1)} %get-tuple-element.81), calls=%async_computation.2 | async-start | bytes 2097152 | tf_op jit(solution)/shard_map/all_to_all | solution.py:486
  197.9 19.6 %attend.2 = (f32[1024,128]{1,0:T(8,128)S(1)}, bf16[128,640]{1,0:T(8,128)(2,1)S(1)}) custom-call(bf16[1024,2560]{1,0:T(8,128)(2,1)} %bitcast.4.buf_ref, bf16[1024,128]{1,0:T(8,128)(2,1)S(1)} %pad_maximum_fusion.1.u_ref, bf16[128,768]{1,0:T(8,128)(2,1)S(1)} %fusion.1.bq_ref.bv_ref, bf16[128,768]{1,0:T(8,128)(2,1)S(1)} %fusion.1.bq_ref.bv_ref), custom_call_target="tpu_custom_call" | custom-call | flops 6710886400 | bytes 5242880 | tf_op jit(solution)/shard_map/attend/pallas_call | solution.py:156
  218.4 2.3 all-to-all-done.2
  220.7 1.0 copy-done.14
  221.7 3.7 %attend.3 = (f32[1024,128]{1,0:T(8,128)S(1)}, bf16[128,128]{1,0:T(8,128)(2,1)S(1)}) custom-call(bf16[1024,512]{1,0:T(8,128)(2,1)S(1)} %bitcast.14, bf16[1024,128]{1,0:T(8,128)(2,1)S(1)} %pad_maximum_fusion.1.u_ref, bf16[128,768]{1,0:T(8,128)(2,1)S(1)} %fusion.1.bq_ref.bv_ref, bf16[128,768]{1,0:T(8,128)(2,1)S(1)} %fusion.1.bq_ref.bv_ref, ...), custom_call_target="tpu_custom_call" | custom-call | flops 1342177280 | bytes 1048576 | tf_op jit(solution)/shard_map/attend/pallas_call | solution.py:156
  226.1 1.7 collective-permute-start.19
  228.2 4.7 %collective-permute-start.23 = (bf16[128,768]{1,0:T(8,128)(2,1)S(1)}, bf16[128,768]{1,0:T(8,128)(2,1)S(1)}, u32[]{:S(2)}, u32[]{:S(2)}) collective-permute-start(bf16[128,768]{1,0:T(8,128)(2,1)S(1)} %constant_dynamic-update-slice_fusion.refs_0_), channel_id=1, source_target_pairs={{0,8},{1,9},{2,10},{3,11},{4,12},{5,13},{6,14},{7,15},{8,0},{9,1},... | collective-permute-start | bytes 589832 | tf_op jit(solution)/shard_map/ppermute | solution.py:45
  232.8 1.9 collective-permute-done.18
  234.8 1.5 collective-permute-start.22
  236.9 3.1 %collective-permute-start.16 = (bf16[128,768]{1,0:T(8,128)(2,1)S(1)}, bf16[128,768]{1,0:T(8,128)(2,1)S(1)}, u32[]{:S(2)}, u32[]{:S(2)}) collective-permute-start(bf16[128,768]{1,0:T(8,128)(2,1)S(1)} %constant_dynamic-update-slice_fusion.refs_0_), channel_id=1, source_target_pairs={{0,4},{1,5},{2,6},{3,7},{4,0},{5,1},{6,2},{7,3},{8,12},{9,13},{10,... | collective-permute-start | bytes 589832 | tf_op jit(solution)/shard_map/ppermute | solution.py:45
  240.1 0.8 collective-permute-done.21.refs_2_
  240.9 1.0 slots.1.refs_0_
  242.0 3.1 %collective-permute-start.24 = (bf16[128,768]{1,0:T(8,128)(2,1)S(1)}, bf16[128,768]{1,0:T(8,128)(2,1)S(1)}, u32[]{:S(2)}, u32[]{:S(2)}) collective-permute-start(bf16[128,768]{1,0:T(8,128)(2,1)S(1)} %collective-permute-done.23.refs_2_), channel_id=1, source_target_pairs={{0,4},{1,5},{2,6},{3,7},{4,0},{5,1},{6,2},{7,3},{8,12},{9,13},{10,... | collective-permute-start | bytes 589832 | tf_op jit(solution)/shard_map/ppermute | solution.py:45
  245.1 2.1 collective-permute-start.30
  247.2 2.3 collective-permute-start.28
  249.5 1.7 collective-permute-done.24.refs_3_
  251.3 1.1 owner_sums.2
  252.5 1.2 collective-permute-start.26
  253.7 3.5 %collective-permute-done.30.refs_3_ = bf16[128,768]{1,0:T(8,128)(2,1)S(1)} collective-permute-done((bf16[128,768]{1,0:T(8,128)(2,1)S(1)}, bf16[128,768]{1,0:T(8,128)(2,1)S(1)}, u32[]{:S(2)}, u32[]{:S(2)}) %collective-permute-start.30) | collective-permute-done | bytes 196640 | tf_op jit(solution)/shard_map/ppermute | solution.py:45
  257.2 6.9 %collective-permute-done.29.refs_2_ = bf16[128,768]{1,0:T(8,128)(2,1)S(1)} collective-permute-done((bf16[128,768]{1,0:T(8,128)(2,1)S(1)}, bf16[128,768]{1,0:T(8,128)(2,1)S(1)}, u32[]{:S(2)}, u32[]{:S(2)}) %collective-permute-start.29) | collective-permute-done | bytes 196640 | tf_op jit(solution)/shard_map/ppermute | solution.py:45
  264.1 1.1 owner_sums.3
  265.3 1.7 collective-permute-start.32
  267.8 5.2 %collective-permute-done.32.refs_6_ = bf16[128,768]{1,0:T(8,128)(2,1)S(1)} collective-permute-done((bf16[128,768]{1,0:T(8,128)(2,1)S(1)}, bf16[128,768]{1,0:T(8,128)(2,1)S(1)}, u32[]{:S(2)}, u32[]{:S(2)}) %collective-permute-start.32) | collective-permute-done | bytes 196640 | tf_op jit(solution)/shard_map/ppermute | solution.py:45
  273.1 3.3 %collective-permute-done.33.refs_7_ = bf16[128,768]{1,0:T(8,128)(2,1)S(1)} collective-permute-done((bf16[128,768]{1,0:T(8,128)(2,1)S(1)}, bf16[128,768]{1,0:T(8,128)(2,1)S(1)}, u32[]{:S(2)}, u32[]{:S(2)}) %collective-permute-start.33) | collective-permute-done | bytes 196640 | tf_op jit(solution)/shard_map/ppermute | solution.py:45
  276.4 5.1 %adam.1 = (f32[1,4,64,3072]{3,2,1,0:T(8,128)}, f32[1,4,64,3072]{3,2,1,0:T(8,128)}, f32[1,4,64,3072]{3,2,1,0:T(8,128)}) custom-call(s32[1]{0:T(128)} %bitcast.where_ref, s32[1]{0:T(128)S(6)} %copy.15.count_ref, bf16[128,768]{1,0:T(8,128)(2,1)S(1)} %get-tuple-element.91.refs_0_, bf16[128,768]{1,0:T(8,128)(2,1)S(1)} %collective-permute-done.25.refs_1_, ...), custom_call_target="tpu_custom_call" | custom-call | bytes 18874368 | tf_op jit(solution)/shard_map/adam/pallas_call | solution.py:228
  (82 shorter events, 7.9 us)
Async XLA Ops:
  3.3 60.7 %all-to-all-start.1 = ((bf16[16,64,768]{2,1,0:T(8,128)(2,1)}), bf16[16,64,768]{2,1,0:T(8,128)(2,1)S(1)}, u32[]{:S(2)}, u32[]{:S(2)}) async-start(bf16[16,64,768]{2,1,0:T(8,128)(2,1)} %bitcast.2), calls=%async_computation.1 | async-start | bytes 3145728 | tf_op jit(solution)/shard_map/all_to_all | solution.py:462
  10.8 1.9 copy-start
  12.6 5.4 %copy-start.4 = (bf16[4,64,3072]{2,1,0:T(8,128)(2,1)S(1)}, bf16[4,64,3072]{2,1,0:T(8,128)(2,1)}, u32[]{:S(2)}) copy-start(bf16[4,64,3072]{2,1,0:T(8,128)(2,1)} %query_ref.1) | copy-start | bytes 4718596
  12.6 5.4 %copy-start.6 = (s32[4]{0:T(128)S(1)}, s32[4]{0:T(128)}, u32[]{:S(2)}) copy-start(s32[4]{0:T(128)} %steps_ref.1) | copy-start | bytes 52
  16.0 8.3 %collective-permute-start = (bf16[128,768]{1,0:T(8,128)(2,1)}, bf16[128,768]{1,0:T(8,128)(2,1)}, u32[]{:S(2)}, u32[]{:S(2)}) collective-permute-start(bf16[128,768]{1,0:T(8,128)(2,1)} %get-tuple-element.55), channel_id=1, source_target_pairs={{0,1},{1,0},{2,3},{3,2},{4,5},{5,4},{6,7},{7,6},{8,9},{9,8},{10,11... | collective-permute-start | bytes 589832 | tf_op jit(solution)/shard_map/ppermute | solution.py:45
  16.4 14.6 %collective-permute-start.1 = (bf16[128,768]{1,0:T(8,128)(2,1)}, bf16[128,768]{1,0:T(8,128)(2,1)}, u32[]{:S(2)}, u32[]{:S(2)}) collective-permute-start(bf16[128,768]{1,0:T(8,128)(2,1)} %get-tuple-element.56), channel_id=1, source_target_pairs={{0,2},{1,3},{2,0},{3,1},{4,6},{5,7},{6,4},{7,5},{8,10},{9,11},{10,... | collective-permute-start | bytes 589832 | tf_op jit(solution)/shard_map/ppermute | solution.py:45
  18.1 18.0 %collective-permute-start.2 = (bf16[128,768]{1,0:T(8,128)(2,1)}, bf16[128,768]{1,0:T(8,128)(2,1)}, u32[]{:S(2)}, u32[]{:S(2)}) collective-permute-start(bf16[128,768]{1,0:T(8,128)(2,1)} %get-tuple-element.57), channel_id=1, source_target_pairs={{0,3},{1,2},{2,1},{3,0},{4,7},{5,6},{6,5},{7,4},{8,11},{9,10},{10,... | collective-permute-start | bytes 589832 | tf_op jit(solution)/shard_map/ppermute | solution.py:45
  18.1 18.0 %copy-start.5 = (s32[4]{0:T(128)S(1)}, s32[4]{0:T(128)}, u32[]{:S(2)}) copy-start(s32[4]{0:T(128)} %ids_ref.7) | copy-start | bytes 52
  37.4 15.0 %collective-permute-start.3 = (bf16[2,128,768]{2,1,0:T(8,128)(2,1)S(1)}, bf16[2,128,768]{2,1,0:T(8,128)(2,1)S(1)}, u32[]{:S(2)}, u32[]{:S(2)}) collective-permute-start(bf16[2,128,768]{2,1,0:T(8,128)(2,1)S(1)} %get-tuple-element.67), channel_id=1, source_target_pairs={{0,4},{1,5},{2,6},{3,7},{4,0},{5,1},{6,2},{7,3},{8,12},{9,13},{10,... | collective-permute-start | bytes 1179656 | tf_op jit(solution)/shard_map/ppermute | solution.py:45
  52.4 11.6 %collective-permute-start.4 = (bf16[1,128,768]{2,1,0:T(8,128)(2,1)S(1)}, bf16[1,128,768]{2,1,0:T(8,128)(2,1)S(1)}, u32[]{:S(2)}, u32[]{:S(2)}) collective-permute-start(bf16[1,128,768]{2,1,0:T(8,128)(2,1)S(1)} %slice_add_fusion.2), channel_id=1, source_target_pairs={{0,8},{1,9},{2,10},{3,11},{4,12},{5,13},{6,14},{7,15},{8,0},{9,1},... | collective-permute-start | bytes 589832 | tf_op jit(solution)/shard_map/ppermute | solution.py:45
  64.1 4.9 %copy-start.12 = (bf16[128,768]{1,0:T(8,128)(2,1)S(1)}, bf16[128,768]{1,0:T(8,128)(2,1)}, u32[]{:S(2)}) copy-start(bf16[128,768]{1,0:T(8,128)(2,1)} %copy-done.11) | copy-start | bytes 589828
  64.1 5.4 %copy-start.10 = (bf16[128,768]{1,0:T(8,128)(2,1)S(1)}, bf16[128,768]{1,0:T(8,128)(2,1)}, u32[]{:S(2)}) copy-start(bf16[128,768]{1,0:T(8,128)(2,1)} %copy-done.9) | copy-start | bytes 589828
  64.1 7.0 %copy-start.8 = (bf16[128,768]{1,0:T(8,128)(2,1)S(1)}, bf16[128,768]{1,0:T(8,128)(2,1)}, u32[]{:S(2)}) copy-start(bf16[128,768]{1,0:T(8,128)(2,1)} %copy-done.7) | copy-start | bytes 589828
  64.1 129.9 %all-to-all-start = ((bf16[16,64,2560]{2,1,0:T(8,128)(2,1)}), bf16[16,64,2560]{2,1,0:T(8,128)(2,1)}, u32[]{:S(2)}, u32[]{:S(2)}) async-start(bf16[16,64,2560]{2,1,0:T(8,128)(2,1)} %get-tuple-element.68), calls=%async_computation | async-start | bytes 10485760 | tf_op jit(solution)/shard_map/all_to_all | solution.py:486
  69.0 2.1 collective-permute-start.11
  69.4 36.4 %collective-permute-start.12 = (bf16[128,768]{1,0:T(8,128)(2,1)S(1)}, bf16[128,768]{1,0:T(8,128)(2,1)S(1)}, u32[]{:S(2)}, u32[]{:S(2)}) collective-permute-start(bf16[128,768]{1,0:T(8,128)(2,1)S(1)} %copy-done.10), channel_id=1, source_target_pairs={{0,2},{1,3},{2,0},{3,1},{4,6},{5,7},{6,4},{7,5},{8,10},{9,11},{10,... | collective-permute-start | bytes 589832 | tf_op jit(solution)/shard_map/ppermute | solution.py:45
  71.1 38.3 %collective-permute-start.13 = (bf16[128,768]{1,0:T(8,128)(2,1)S(1)}, bf16[128,768]{1,0:T(8,128)(2,1)S(1)}, u32[]{:S(2)}, u32[]{:S(2)}) collective-permute-start(bf16[128,768]{1,0:T(8,128)(2,1)S(1)} %copy-done.8), channel_id=1, source_target_pairs={{0,3},{1,2},{2,1},{3,0},{4,7},{5,6},{6,5},{7,4},{8,11},{9,10},{10,... | collective-permute-start | bytes 589832 | tf_op jit(solution)/shard_map/ppermute | solution.py:45
  110.1 52.8 %collective-permute-start.14 = (bf16[2,128,768]{2,1,0:T(8,128)(2,1)S(1)}, bf16[2,128,768]{2,1,0:T(8,128)(2,1)S(1)}, u32[]{:S(2)}, u32[]{:S(2)}) collective-permute-start(bf16[2,128,768]{2,1,0:T(8,128)(2,1)S(1)} %get-tuple-element.77), channel_id=1, source_target_pairs={{0,4},{1,5},{2,6},{3,7},{4,0},{5,1},{6,2},{7,3},{8,12},{9,13},{10,... | collective-permute-start | bytes 1179656 | tf_op jit(solution)/shard_map/ppermute | solution.py:45
  110.8 56.7 %collective-permute-start.5 = (f32[256,128]{1,0:T(8,128)S(1)}, f32[256,128]{1,0:T(8,128)S(1)}, u32[]{:S(2)}, u32[]{:S(2)}) collective-permute-start(f32[256,128]{1,0:T(8,128)S(1)} %get-tuple-element.110), channel_id=1, source_target_pairs={{0,1},{1,0},{2,3},{3,2},{4,5},{5,4},{6,7},{7,6},{8,9},{9,8},{10,11... | collective-permute-start | bytes 393224 | tf_op jit(solution)/shard_map/ppermute | solution.py:45
  119.1 48.4 %collective-permute-start.7 = (f32[256,128]{1,0:T(8,128)S(1)}, f32[256,128]{1,0:T(8,128)S(1)}, u32[]{:S(2)}, u32[]{:S(2)}) collective-permute-start(f32[256,128]{1,0:T(8,128)S(1)} %get-tuple-element.111), channel_id=1, source_target_pairs={{0,3},{1,2},{2,1},{3,0},{4,7},{5,6},{6,5},{7,4},{8,11},{9,10},{10,... | collective-permute-start | bytes 393224 | tf_op jit(solution)/shard_map/ppermute | solution.py:45
  119.1 48.4 %collective-permute-start.6 = (f32[256,128]{1,0:T(8,128)S(1)}, f32[256,128]{1,0:T(8,128)S(1)}, u32[]{:S(2)}, u32[]{:S(2)}) collective-permute-start(f32[256,128]{1,0:T(8,128)S(1)} %get-tuple-element.112), channel_id=1, source_target_pairs={{0,2},{1,3},{2,0},{3,1},{4,6},{5,7},{6,4},{7,5},{8,10},{9,11},{10,... | collective-permute-start | bytes 393224 | tf_op jit(solution)/shard_map/ppermute | solution.py:45
  163.0 30.9 %collective-permute-start.15 = (bf16[1,128,768]{2,1,0:T(8,128)(2,1)S(1)}, bf16[1,128,768]{2,1,0:T(8,128)(2,1)S(1)}, u32[]{:S(2)}, u32[]{:S(2)}) collective-permute-start(bf16[1,128,768]{2,1,0:T(8,128)(2,1)S(1)} %slice_add_fusion), channel_id=1, source_target_pairs={{0,8},{1,9},{2,10},{3,11},{4,12},{5,13},{6,14},{7,15},{8,0},{9,1},... | collective-permute-start | bytes 589832 | tf_op jit(solution)/shard_map/ppermute | solution.py:45
  167.6 26.4 %collective-permute-start.10 = (bf16[256,128]{1,0:T(8,128)(2,1)S(1)}, bf16[256,128]{1,0:T(8,128)(2,1)S(1)}, u32[]{:S(2)}, u32[]{:S(2)}) collective-permute-start(bf16[256,128]{1,0:T(8,128)(2,1)S(1)} %add_convert_fusion.1), channel_id=1, source_target_pairs={{0,1},{1,0},{2,3},{3,2},{4,5},{5,4},{6,7},{7,6},{8,9},{9,8},{10,11... | collective-permute-start | bytes 196616 | tf_op jit(solution)/shard_map/ppermute | solution.py:45
  167.6 26.3 %collective-permute-start.9 = (bf16[256,128]{1,0:T(8,128)(2,1)S(1)}, bf16[256,128]{1,0:T(8,128)(2,1)S(1)}, u32[]{:S(2)}, u32[]{:S(2)}) collective-permute-start(bf16[256,128]{1,0:T(8,128)(2,1)S(1)} %add_convert_fusion.1), channel_id=1, source_target_pairs={{0,2},{1,3},{2,0},{3,1},{4,6},{5,7},{6,4},{7,5},{8,10},{9,11},{10,... | collective-permute-start | bytes 196616 | tf_op jit(solution)/shard_map/ppermute | solution.py:45
  169.3 24.7 %collective-permute-start.8 = (bf16[256,128]{1,0:T(8,128)(2,1)S(1)}, bf16[256,128]{1,0:T(8,128)(2,1)S(1)}, u32[]{:S(2)}, u32[]{:S(2)}) collective-permute-start(bf16[256,128]{1,0:T(8,128)(2,1)S(1)} %add_convert_fusion.1), channel_id=1, source_target_pairs={{0,3},{1,2},{2,1},{3,0},{4,7},{5,6},{6,5},{7,4},{8,11},{9,10},{10,... | collective-permute-start | bytes 196616 | tf_op jit(solution)/shard_map/ppermute | solution.py:45
  194.0 26.7 %all-to-all-start.2 = ((bf16[16,64,512]{2,1,0:T(8,128)(2,1)}), bf16[16,64,512]{2,1,0:T(8,128)(2,1)S(1)}, u32[]{:S(2)}, u32[]{:S(2)}) async-start(bf16[16,64,512]{2,1,0:T(8,128)(2,1)} %get-tuple-element.81), calls=%async_computation.2 | async-start | bytes 2097152 | tf_op jit(solution)/shard_map/all_to_all | solution.py:486
  220.7 1.0 copy-start.14
  221.7 54.6 %copy-start.2 = (f32[1,4,64,3072]{3,2,1,0:T(8,128)S(1)}, f32[1,4,64,3072]{3,2,1,0:T(8,128)}, u32[]{:S(2)}) copy-start(f32[1,4,64,3072]{3,2,1,0:T(8,128)} %refs_9_.1) | copy-start | bytes 9437188
  221.7 54.6 %copy-start.3 = (f32[1,4,64,3072]{3,2,1,0:T(8,128)S(1)}, f32[1,4,64,3072]{3,2,1,0:T(8,128)}, u32[]{:S(2)}) copy-start(f32[1,4,64,3072]{3,2,1,0:T(8,128)} %refs_10_.1) | copy-start | bytes 9437188
  225.4 7.4 %collective-permute-start.17 = (f32[256,128]{1,0:T(8,128)S(1)}, f32[256,128]{1,0:T(8,128)S(1)}, u32[]{:S(2)}, u32[]{:S(2)}) collective-permute-start(f32[256,128]{1,0:T(8,128)S(1)} %get-tuple-element.107), channel_id=1, source_target_pairs={{0,1},{1,0},{2,3},{3,2},{4,5},{5,4},{6,7},{7,6},{8,9},{9,8},{10,11... | collective-permute-start | bytes 393224 | tf_op jit(solution)/shard_map/ppermute | solution.py:45
  226.1 6.7 %collective-permute-start.19 = (f32[256,128]{1,0:T(8,128)S(1)}, f32[256,128]{1,0:T(8,128)S(1)}, u32[]{:S(2)}, u32[]{:S(2)}) collective-permute-start(f32[256,128]{1,0:T(8,128)S(1)} %get-tuple-element.108), channel_id=1, source_target_pairs={{0,3},{1,2},{2,1},{3,0},{4,7},{5,6},{6,5},{7,4},{8,11},{9,10},{10,... | collective-permute-start | bytes 393224 | tf_op jit(solution)/shard_map/ppermute | solution.py:45
  227.8 7.0 %collective-permute-start.18 = (f32[256,128]{1,0:T(8,128)S(1)}, f32[256,128]{1,0:T(8,128)S(1)}, u32[]{:S(2)}, u32[]{:S(2)}) collective-permute-start(f32[256,128]{1,0:T(8,128)S(1)} %get-tuple-element.109), channel_id=1, source_target_pairs={{0,2},{1,3},{2,0},{3,1},{4,6},{5,7},{6,4},{7,5},{8,10},{9,11},{10,... | collective-permute-start | bytes 393224 | tf_op jit(solution)/shard_map/ppermute | solution.py:45
  228.2 13.8 %collective-permute-start.23 = (bf16[128,768]{1,0:T(8,128)(2,1)S(1)}, bf16[128,768]{1,0:T(8,128)(2,1)S(1)}, u32[]{:S(2)}, u32[]{:S(2)}) collective-permute-start(bf16[128,768]{1,0:T(8,128)(2,1)S(1)} %constant_dynamic-update-slice_fusion.refs_0_), channel_id=1, source_target_pairs={{0,8},{1,9},{2,10},{3,11},{4,12},{5,13},{6,14},{7,15},{8,0},{9,1},... | collective-permute-start | bytes 589832 | tf_op jit(solution)/shard_map/ppermute | solution.py:45
  234.8 41.6 %copy-start.1 = (f32[1,4,64,3072]{3,2,1,0:T(8,128)S(1)}, f32[1,4,64,3072]{3,2,1,0:T(8,128)}, u32[]{:S(2)}) copy-start(f32[1,4,64,3072]{3,2,1,0:T(8,128)} %refs_8_.1) | copy-start | bytes 9437188
  234.8 5.3 %collective-permute-start.22 = (bf16[256,128]{1,0:T(8,128)(2,1)S(1)}, bf16[256,128]{1,0:T(8,128)(2,1)S(1)}, u32[]{:S(2)}, u32[]{:S(2)}) collective-permute-start(bf16[256,128]{1,0:T(8,128)(2,1)S(1)} %add_convert_fusion.refs_0_), channel_id=1, source_target_pairs={{0,3},{1,2},{2,1},{3,0},{4,7},{5,6},{6,5},{7,4},{8,11},{9,10},{10,... | collective-permute-start | bytes 196616 | tf_op jit(solution)/shard_map/ppermute | solution.py:45
  236.3 4.7 %collective-permute-start.21 = (bf16[256,128]{1,0:T(8,128)(2,1)S(1)}, bf16[256,128]{1,0:T(8,128)(2,1)S(1)}, u32[]{:S(2)}, u32[]{:S(2)}) collective-permute-start(bf16[256,128]{1,0:T(8,128)(2,1)S(1)} %add_convert_fusion.refs_0_), channel_id=1, source_target_pairs={{0,2},{1,3},{2,0},{3,1},{4,6},{5,7},{6,4},{7,5},{8,10},{9,11},{10,... | collective-permute-start | bytes 196616 | tf_op jit(solution)/shard_map/ppermute | solution.py:45
  236.9 4.0 %collective-permute-start.20 = (bf16[256,128]{1,0:T(8,128)(2,1)S(1)}, bf16[256,128]{1,0:T(8,128)(2,1)S(1)}, u32[]{:S(2)}, u32[]{:S(2)}) collective-permute-start(bf16[256,128]{1,0:T(8,128)(2,1)S(1)} %add_convert_fusion.refs_0_), channel_id=1, source_target_pairs={{0,1},{1,0},{2,3},{3,2},{4,5},{5,4},{6,7},{7,6},{8,9},{9,8},{10,11... | collective-permute-start | bytes 196616 | tf_op jit(solution)/shard_map/ppermute | solution.py:45
  236.9 12.6 %collective-permute-start.16 = (bf16[128,768]{1,0:T(8,128)(2,1)S(1)}, bf16[128,768]{1,0:T(8,128)(2,1)S(1)}, u32[]{:S(2)}, u32[]{:S(2)}) collective-permute-start(bf16[128,768]{1,0:T(8,128)(2,1)S(1)} %constant_dynamic-update-slice_fusion.refs_0_), channel_id=1, source_target_pairs={{0,4},{1,5},{2,6},{3,7},{4,0},{5,1},{6,2},{7,3},{8,12},{9,13},{10,... | collective-permute-start | bytes 589832 | tf_op jit(solution)/shard_map/ppermute | solution.py:45
  242.0 9.3 %collective-permute-start.24 = (bf16[128,768]{1,0:T(8,128)(2,1)S(1)}, bf16[128,768]{1,0:T(8,128)(2,1)S(1)}, u32[]{:S(2)}, u32[]{:S(2)}) collective-permute-start(bf16[128,768]{1,0:T(8,128)(2,1)S(1)} %collective-permute-done.23.refs_2_), channel_id=1, source_target_pairs={{0,4},{1,5},{2,6},{3,7},{4,0},{5,1},{6,2},{7,3},{8,12},{9,13},{10,... | collective-permute-start | bytes 589832 | tf_op jit(solution)/shard_map/ppermute | solution.py:45
  245.1 12.1 %collective-permute-start.30 = (bf16[128,768]{1,0:T(8,128)(2,1)S(1)}, bf16[128,768]{1,0:T(8,128)(2,1)S(1)}, u32[]{:S(2)}, u32[]{:S(2)}) collective-permute-start(bf16[128,768]{1,0:T(8,128)(2,1)S(1)} %slots.1.refs_0_), channel_id=1, source_target_pairs={{0,12},{1,13},{2,14},{3,15},{4,8},{5,9},{6,10},{7,11},{8,4},{9,5},... | collective-permute-start | bytes 589832 | tf_op jit(solution)/shard_map/ppermute | solution.py:45
  247.2 16.9 %collective-permute-start.29 = (bf16[128,768]{1,0:T(8,128)(2,1)S(1)}, bf16[128,768]{1,0:T(8,128)(2,1)S(1)}, u32[]{:S(2)}, u32[]{:S(2)}) collective-permute-start(bf16[128,768]{1,0:T(8,128)(2,1)S(1)} %slots.1.refs_0_), channel_id=1, source_target_pairs={{0,8},{1,9},{2,10},{3,11},{4,12},{5,13},{6,14},{7,15},{8,0},{9,1},... | collective-permute-start | bytes 589832 | tf_op jit(solution)/shard_map/ppermute | solution.py:45
  247.2 16.9 %collective-permute-start.28 = (bf16[128,768]{1,0:T(8,128)(2,1)S(1)}, bf16[128,768]{1,0:T(8,128)(2,1)S(1)}, u32[]{:S(2)}, u32[]{:S(2)}) collective-permute-start(bf16[128,768]{1,0:T(8,128)(2,1)S(1)} %slots.1.refs_0_), channel_id=1, source_target_pairs={{0,4},{1,5},{2,6},{3,7},{4,0},{5,1},{6,2},{7,3},{8,12},{9,13},{10,... | collective-permute-start | bytes 589832 | tf_op jit(solution)/shard_map/ppermute | solution.py:45
  252.4 11.7 %collective-permute-start.25 = (bf16[128,768]{1,0:T(8,128)(2,1)S(1)}, bf16[128,768]{1,0:T(8,128)(2,1)S(1)}, u32[]{:S(2)}, u32[]{:S(2)}) collective-permute-start(bf16[128,768]{1,0:T(8,128)(2,1)S(1)} %get-tuple-element.87), channel_id=1, source_target_pairs={{0,1},{1,0},{2,3},{3,2},{4,5},{5,4},{6,7},{7,6},{8,9},{9,8},{10,11... | collective-permute-start | bytes 589832 | tf_op jit(solution)/shard_map/ppermute | solution.py:45
  252.5 11.6 %collective-permute-start.26 = (bf16[128,768]{1,0:T(8,128)(2,1)S(1)}, bf16[128,768]{1,0:T(8,128)(2,1)S(1)}, u32[]{:S(2)}, u32[]{:S(2)}) collective-permute-start(bf16[128,768]{1,0:T(8,128)(2,1)S(1)} %get-tuple-element.88), channel_id=1, source_target_pairs={{0,2},{1,3},{2,0},{3,1},{4,6},{5,7},{6,4},{7,5},{8,10},{9,11},{10,... | collective-permute-start | bytes 589832 | tf_op jit(solution)/shard_map/ppermute | solution.py:45
  257.2 6.9 %collective-permute-start.27 = (bf16[128,768]{1,0:T(8,128)(2,1)S(1)}, bf16[128,768]{1,0:T(8,128)(2,1)S(1)}, u32[]{:S(2)}, u32[]{:S(2)}) collective-permute-start(bf16[128,768]{1,0:T(8,128)(2,1)S(1)} %get-tuple-element.89), channel_id=1, source_target_pairs={{0,3},{1,2},{2,1},{3,0},{4,7},{5,6},{6,5},{7,4},{8,11},{9,10},{10,... | collective-permute-start | bytes 589832 | tf_op jit(solution)/shard_map/ppermute | solution.py:45
  265.2 2.6 collective-permute-start.31
  265.3 7.8 %collective-permute-start.32 = (bf16[128,768]{1,0:T(8,128)(2,1)S(1)}, bf16[128,768]{1,0:T(8,128)(2,1)S(1)}, u32[]{:S(2)}, u32[]{:S(2)}) collective-permute-start(bf16[128,768]{1,0:T(8,128)(2,1)S(1)} %get-tuple-element.101), channel_id=1, source_target_pairs={{0,2},{1,3},{2,0},{3,1},{4,6},{5,7},{6,4},{7,5},{8,10},{9,11},{10,... | collective-permute-start | bytes 589832 | tf_op jit(solution)/shard_map/ppermute | solution.py:45
  267.0 9.4 %collective-permute-start.33 = (bf16[128,768]{1,0:T(8,128)(2,1)S(1)}, bf16[128,768]{1,0:T(8,128)(2,1)S(1)}, u32[]{:S(2)}, u32[]{:S(2)}) collective-permute-start(bf16[128,768]{1,0:T(8,128)(2,1)S(1)} %get-tuple-element.102), channel_id=1, source_target_pairs={{0,3},{1,2},{2,1},{3,0},{4,7},{5,6},{6,5},{7,4},{8,11},{9,10},{10,... | collective-permute-start | bytes 589832 | tf_op jit(solution)/shard_map/ppermute | solution.py:45
  (4 other events, 2.8 us)

commit v4 on v3

--- a/solution.py
+++ b/solution.py
@@ -502,7 +502,7 @@
             early[r] = exchange(early[r ^ low], low * per, size)
     late = direct_images(late, per, images, size)
     early = owner_sums(where, tenant_ids, [early[r] for r in range(images)], per, size)
-    early, late = tie(early, late)
+    early[1], late = tie(early[1], late)
     late = owner_sums(where, tenant_ids, late, per, size)
     return tuple(
         adam(place.reshape(1), counts, early, late, adapters, first_moment, second_moment)

time: 284 us -> 282 us (level)
  transfers between devices with their start and end apart: 37 -> 37, of which waited for: 16 -> 16; matrix products, arithmetic and copies ran while one was open for 0% -> 0% of each run, Pallas kernels for 11% -> 12%
where the time goes in v4:
time: 282 us; the launch traced here: 281 us
  waiting for transfers between devices  166 us (59%)
  starting transfers between devices  62.9 us (22%)
  Pallas kernels  41.2 us (15%)
  local copies, waits for them, and re-layouts  7.34 us (3%)
    ppermute x34, waiting for transfers between devices, exchange(): return lax.ppermute(block, 'seq', [(i, i ^ flip) for i in range(size)])  164 us
    ppermute x34, starting transfers between devices, exchange(): return lax.ppermute(block, 'seq', [(i, i ^ flip) for i in range(size)])  46.8 us
    pallas_call x2, Pallas kernels, attend(): pl.pallas_call(functools.partial(attend_kernel, first, row_block), grid=(...  23.3 us
    all_to_all x2, starting transfers between devices, shards(): lax.all_to_all(sent, 'seq', 0, 0, tiled=True)  8.74 us
    all_to_all x1, starting transfers between devices, shards(): lax.all_to_all(hidden_sent, 'seq', 0, 0, tiled=True).reshape(length, cols)  7.39 us
    pallas_call x1, Pallas kernels, pack(): pl.pallas_call(functools.partial(pack_kernel, chunks, per), grid=(images,...  6.1 us
    unnamed x31, local copies, waits for them, and re-layouts  5.79 us
  transfers between devices with their start and end apart: 37, of which 16 were waited for; matrix products, arithmetic and copies ran while one was open for 0% of the time, Pallas kernels for 12%

profile of v4, /device:TPU:0, one launch (start us, length us, event | category | flops | bytes accessed | tf_op | source)
XLA Modules:
  0.0 281.5 jit_solution(6231670618284539589)
XLA Ops:
  0.6 1.5 fusion.4
  2.1 1.2 pad_maximum_fusion
  3.3 7.4 %all-to-all-start.1 = ((bf16[16,64,768]{2,1,0:T(8,128)(2,1)}), bf16[16,64,768]{2,1,0:T(8,128)(2,1)S(1)}, u32[]{:S(2)}, u32[]{:S(2)}) async-start(bf16[16,64,768]{2,1,0:T(8,128)(2,1)} %bitcast.2), calls=%async_computation.1 | async-start | bytes 3145728 | tf_op jit(solution)/shard_map/all_to_all | solution.py:462
  10.8 1.9 copy-done
  12.7 1.3 pieces.1
  16.4 1.7 collective-permute-start.1
  18.1 6.1 %pack.1 = (bf16[16,64,2560]{2,1,0:T(8,128)(2,1)}, bf16[16,64,512]{2,1,0:T(8,128)(2,1)}) custom-call(s32[4]{0:T(128)S(1)} %copy-done.6, bf16[4,64,3072]{2,1,0:T(8,128)(2,1)S(1)} %copy-done.4, bf16[4,64,3072]{2,1,0:T(8,128)(2,1)} %key_ref.1, bf16[4,64,3072]{2,1,0:T(8,128)(2,1)} %value_ref.1, bf16[4,64,3072]{2,1,0:T(8,128)(2,1)} %grad_ref.1), custom_call_target="tpu_custom_call" | custom-call | bytes 12582912 | tf_op jit(solution)/shard_map/pack/pallas_call | solution.py:71
  24.3 6.8 %collective-permute-done.1.refs_2_ = bf16[128,768]{1,0:T(8,128)(2,1)} collective-permute-done((bf16[128,768]{1,0:T(8,128)(2,1)}, bf16[128,768]{1,0:T(8,128)(2,1)}, u32[]{:S(2)}, u32[]{:S(2)}) %collective-permute-start.1) | collective-permute-done | bytes 196640 | tf_op jit(solution)/shard_map/ppermute | solution.py:45
  31.0 5.0 %collective-permute-done.2.refs_3_ = bf16[128,768]{1,0:T(8,128)(2,1)} collective-permute-done((bf16[128,768]{1,0:T(8,128)(2,1)}, bf16[128,768]{1,0:T(8,128)(2,1)}, u32[]{:S(2)}, u32[]{:S(2)}) %collective-permute-start.2) | collective-permute-done | bytes 196640 | tf_op jit(solution)/shard_map/ppermute | solution.py:45
  36.1 1.3 for_images.2
  37.5 14.9 %collective-permute-done.3 = bf16[2,128,768]{2,1,0:T(8,128)(2,1)S(1)} collective-permute-done((bf16[2,128,768]{2,1,0:T(8,128)(2,1)S(1)}, bf16[2,128,768]{2,1,0:T(8,128)(2,1)S(1)}, u32[]{:S(2)}, u32[]{:S(2)}) %collective-permute-start.3) | collective-permute-done | bytes 393248 | tf_op jit(solution)/shard_map/ppermute | solution.py:45
  52.4 2.6 collective-permute-start.4
  55.0 9.0 %collective-permute-done.4 = bf16[1,128,768]{2,1,0:T(8,128)(2,1)S(1)} collective-permute-done((bf16[1,128,768]{2,1,0:T(8,128)(2,1)S(1)}, bf16[1,128,768]{2,1,0:T(8,128)(2,1)S(1)}, u32[]{:S(2)}, u32[]{:S(2)}) %collective-permute-start.4) | collective-permute-done | bytes 196640 | tf_op jit(solution)/shard_map/ppermute | solution.py:45
  64.1 4.9 %all-to-all-start = ((bf16[16,64,2560]{2,1,0:T(8,128)(2,1)}), bf16[16,64,2560]{2,1,0:T(8,128)(2,1)}, u32[]{:S(2)}, u32[]{:S(2)}) async-start(bf16[16,64,2560]{2,1,0:T(8,128)(2,1)} %get-tuple-element.65), calls=%async_computation | async-start | bytes 10485760 | tf_op jit(solution)/shard_map/all_to_all | solution.py:486
  69.4 1.7 collective-permute-start.12
  71.1 34.7 %collective-permute-done.12.refs_2_ = bf16[128,768]{1,0:T(8,128)(2,1)S(1)} collective-permute-done((bf16[128,768]{1,0:T(8,128)(2,1)S(1)}, bf16[128,768]{1,0:T(8,128)(2,1)S(1)}, u32[]{:S(2)}, u32[]{:S(2)}) %collective-permute-start.12) | collective-permute-done | bytes 196640 | tf_op jit(solution)/shard_map/ppermute | solution.py:45
  105.8 3.6 %collective-permute-done.13.refs_3_ = bf16[128,768]{1,0:T(8,128)(2,1)S(1)} collective-permute-done((bf16[128,768]{1,0:T(8,128)(2,1)S(1)}, bf16[128,768]{1,0:T(8,128)(2,1)S(1)}, u32[]{:S(2)}, u32[]{:S(2)}) %collective-permute-start.13) | collective-permute-done | bytes 196640 | tf_op jit(solution)/shard_map/ppermute | solution.py:45
  110.8 8.3 %collective-permute-start.5 = (f32[256,128]{1,0:T(8,128)S(1)}, f32[256,128]{1,0:T(8,128)S(1)}, u32[]{:S(2)}, u32[]{:S(2)}) collective-permute-start(f32[256,128]{1,0:T(8,128)S(1)} %get-tuple-element.104), channel_id=1, source_target_pairs={{0,1},{1,0},{2,3},{3,2},{4,5},{5,4},{6,7},{7,6},{8,9},{9,8},{10,11... | collective-permute-start | bytes 393224 | tf_op jit(solution)/shard_map/ppermute | solution.py:45
  119.1 1.7 collective-permute-start.6
  120.8 42.1 %collective-permute-done.14 = bf16[2,128,768]{2,1,0:T(8,128)(2,1)S(1)} collective-permute-done((bf16[2,128,768]{2,1,0:T(8,128)(2,1)S(1)}, bf16[2,128,768]{2,1,0:T(8,128)(2,1)S(1)}, u32[]{:S(2)}, u32[]{:S(2)}) %collective-permute-start.14) | collective-permute-done | bytes 393248 | tf_op jit(solution)/shard_map/ppermute | solution.py:45
  163.0 4.5 %collective-permute-start.15 = (bf16[1,128,768]{2,1,0:T(8,128)(2,1)S(1)}, bf16[1,128,768]{2,1,0:T(8,128)(2,1)S(1)}, u32[]{:S(2)}, u32[]{:S(2)}) collective-permute-start(bf16[1,128,768]{2,1,0:T(8,128)(2,1)S(1)} %slice_add_fusion), channel_id=1, source_target_pairs={{0,8},{1,9},{2,10},{3,11},{4,12},{5,13},{6,14},{7,15},{8,0},{9,1},... | collective-permute-start | bytes 589832 | tf_op jit(solution)/shard_map/ppermute | solution.py:45
  167.6 1.6 collective-permute-start.9
  169.5 24.4 %collective-permute-done.15 = bf16[1,128,768]{2,1,0:T(8,128)(2,1)S(1)} collective-permute-done((bf16[1,128,768]{2,1,0:T(8,128)(2,1)S(1)}, bf16[1,128,768]{2,1,0:T(8,128)(2,1)S(1)}, u32[]{:S(2)}, u32[]{:S(2)}) %collective-permute-start.15) | collective-permute-done | bytes 196640 | tf_op jit(solution)/shard_map/ppermute | solution.py:45
  194.0 3.9 %all-to-all-start.2 = ((bf16[16,64,512]{2,1,0:T(8,128)(2,1)}), bf16[16,64,512]{2,1,0:T(8,128)(2,1)S(1)}, u32[]{:S(2)}, u32[]{:S(2)}) async-start(bf16[16,64,512]{2,1,0:T(8,128)(2,1)} %get-tuple-element.78), calls=%async_computation.2 | async-start | bytes 2097152 | tf_op jit(solution)/shard_map/all_to_all | solution.py:486
  197.9 19.6 %attend.2 = (f32[1024,128]{1,0:T(8,128)S(1)}, bf16[128,640]{1,0:T(8,128)(2,1)S(1)}) custom-call(bf16[1024,2560]{1,0:T(8,128)(2,1)} %bitcast.4.buf_ref, bf16[1024,128]{1,0:T(8,128)(2,1)S(1)} %pad_maximum_fusion.1.u_ref, bf16[128,768]{1,0:T(8,128)(2,1)S(1)} %fusion.1.bq_ref.bv_ref, bf16[128,768]{1,0:T(8,128)(2,1)S(1)} %fusion.1.bq_ref.bv_ref), custom_call_target="tpu_custom_call" | custom-call | flops 6710886400 | bytes 5242880 | tf_op jit(solution)/shard_map/attend/pallas_call | solution.py:156
  218.4 2.3 all-to-all-done.2
  220.7 1.0 copy-done.14
  221.7 3.7 %attend.3 = (f32[1024,128]{1,0:T(8,128)S(1)}, bf16[128,128]{1,0:T(8,128)(2,1)S(1)}) custom-call(bf16[1024,512]{1,0:T(8,128)(2,1)S(1)} %bitcast.14, bf16[1024,128]{1,0:T(8,128)(2,1)S(1)} %pad_maximum_fusion.1.u_ref, bf16[128,768]{1,0:T(8,128)(2,1)S(1)} %fusion.1.bq_ref.bv_ref, bf16[128,768]{1,0:T(8,128)(2,1)S(1)} %fusion.1.bq_ref.bv_ref, ...), custom_call_target="tpu_custom_call" | custom-call | flops 1342177280 | bytes 1048576 | tf_op jit(solution)/shard_map/attend/pallas_call | solution.py:156
  226.1 1.7 collective-permute-start.19
  228.2 4.7 %collective-permute-start.23 = (bf16[128,768]{1,0:T(8,128)(2,1)S(1)}, bf16[128,768]{1,0:T(8,128)(2,1)S(1)}, u32[]{:S(2)}, u32[]{:S(2)}) collective-permute-start(bf16[128,768]{1,0:T(8,128)(2,1)S(1)} %constant_dynamic-update-slice_fusion.refs_0_), channel_id=1, source_target_pairs={{0,8},{1,9},{2,10},{3,11},{4,12},{5,13},{6,14},{7,15},{8,0},{9,1},... | collective-permute-start | bytes 589832 | tf_op jit(solution)/shard_map/ppermute | solution.py:45
  232.8 1.9 collective-permute-done.18
  234.8 1.5 collective-permute-start.22
  236.9 3.1 %collective-permute-start.16 = (bf16[128,768]{1,0:T(8,128)(2,1)S(1)}, bf16[128,768]{1,0:T(8,128)(2,1)S(1)}, u32[]{:S(2)}, u32[]{:S(2)}) collective-permute-start(bf16[128,768]{1,0:T(8,128)(2,1)S(1)} %constant_dynamic-update-slice_fusion.refs_0_), channel_id=1, source_target_pairs={{0,4},{1,5},{2,6},{3,7},{4,0},{5,1},{6,2},{7,3},{8,12},{9,13},{10,... | collective-permute-start | bytes 589832 | tf_op jit(solution)/shard_map/ppermute | solution.py:45
  240.1 0.8 collective-permute-done.21.refs_2_
  240.9 1.0 slots.1.refs_0_
  242.0 3.1 %collective-permute-start.24 = (bf16[128,768]{1,0:T(8,128)(2,1)S(1)}, bf16[128,768]{1,0:T(8,128)(2,1)S(1)}, u32[]{:S(2)}, u32[]{:S(2)}) collective-permute-start(bf16[128,768]{1,0:T(8,128)(2,1)S(1)} %collective-permute-done.23.refs_2_), channel_id=1, source_target_pairs={{0,4},{1,5},{2,6},{3,7},{4,0},{5,1},{6,2},{7,3},{8,12},{9,13},{10,... | collective-permute-start | bytes 589832 | tf_op jit(solution)/shard_map/ppermute | solution.py:45
  245.1 2.1 collective-permute-start.28
  247.2 2.3 collective-permute-start.26
  249.5 1.7 collective-permute-done.24.refs_3_
  251.3 1.1 owner_sums.2
  252.5 1.2 collective-permute-start.29
  253.7 3.5 %collective-permute-done.28.refs_3_ = bf16[128,768]{1,0:T(8,128)(2,1)S(1)} collective-permute-done((bf16[128,768]{1,0:T(8,128)(2,1)S(1)}, bf16[128,768]{1,0:T(8,128)(2,1)S(1)}, u32[]{:S(2)}, u32[]{:S(2)}) %collective-permute-start.28) | collective-permute-done | bytes 196640 | tf_op jit(solution)/shard_map/ppermute | solution.py:45
  257.2 6.9 %collective-permute-done.27.refs_2_ = bf16[128,768]{1,0:T(8,128)(2,1)S(1)} collective-permute-done((bf16[128,768]{1,0:T(8,128)(2,1)S(1)}, bf16[128,768]{1,0:T(8,128)(2,1)S(1)}, u32[]{:S(2)}, u32[]{:S(2)}) %collective-permute-start.27) | collective-permute-done | bytes 196640 | tf_op jit(solution)/shard_map/ppermute | solution.py:45
  264.1 1.1 owner_sums.3
  265.3 1.7 collective-permute-start.32
  267.8 5.2 %collective-permute-done.32.refs_6_ = bf16[128,768]{1,0:T(8,128)(2,1)S(1)} collective-permute-done((bf16[128,768]{1,0:T(8,128)(2,1)S(1)}, bf16[128,768]{1,0:T(8,128)(2,1)S(1)}, u32[]{:S(2)}, u32[]{:S(2)}) %collective-permute-start.32) | collective-permute-done | bytes 196640 | tf_op jit(solution)/shard_map/ppermute | solution.py:45
  273.1 3.3 %collective-permute-done.33.refs_7_ = bf16[128,768]{1,0:T(8,128)(2,1)S(1)} collective-permute-done((bf16[128,768]{1,0:T(8,128)(2,1)S(1)}, bf16[128,768]{1,0:T(8,128)(2,1)S(1)}, u32[]{:S(2)}, u32[]{:S(2)}) %collective-permute-start.33) | collective-permute-done | bytes 196640 | tf_op jit(solution)/shard_map/ppermute | solution.py:45
  276.4 5.1 %adam.1 = (f32[1,4,64,3072]{3,2,1,0:T(8,128)}, f32[1,4,64,3072]{3,2,1,0:T(8,128)}, f32[1,4,64,3072]{3,2,1,0:T(8,128)}) custom-call(s32[1]{0:T(128)} %bitcast.where_ref, s32[1]{0:T(128)S(6)} %copy.15.count_ref, bf16[128,768]{1,0:T(8,128)(2,1)S(1)} %get-tuple-element.83.refs_0_, bf16[128,768]{1,0:T(8,128)(2,1)S(1)} %collective-permute-done.25.refs_1_, ...), custom_call_target="tpu_custom_call" | custom-call | bytes 18874368 | tf_op jit(solution)/shard_map/adam/pallas_call | solution.py:228
  (82 shorter events, 7.9 us)
Async XLA Ops:
  3.3 60.7 %all-to-all-start.1 = ((bf16[16,64,768]{2,1,0:T(8,128)(2,1)}), bf16[16,64,768]{2,1,0:T(8,128)(2,1)S(1)}, u32[]{:S(2)}, u32[]{:S(2)}) async-start(bf16[16,64,768]{2,1,0:T(8,128)(2,1)} %bitcast.2), calls=%async_computation.1 | async-start | bytes 3145728 | tf_op jit(solution)/shard_map/all_to_all | solution.py:462
  10.8 1.9 copy-start
  12.6 5.4 %copy-start.4 = (bf16[4,64,3072]{2,1,0:T(8,128)(2,1)S(1)}, bf16[4,64,3072]{2,1,0:T(8,128)(2,1)}, u32[]{:S(2)}) copy-start(bf16[4,64,3072]{2,1,0:T(8,128)(2,1)} %query_ref.1) | copy-start | bytes 4718596
  12.6 5.4 %copy-start.6 = (s32[4]{0:T(128)S(1)}, s32[4]{0:T(128)}, u32[]{:S(2)}) copy-start(s32[4]{0:T(128)} %steps_ref.1) | copy-start | bytes 52
  16.0 8.3 %collective-permute-start = (bf16[128,768]{1,0:T(8,128)(2,1)}, bf16[128,768]{1,0:T(8,128)(2,1)}, u32[]{:S(2)}, u32[]{:S(2)}) collective-permute-start(bf16[128,768]{1,0:T(8,128)(2,1)} %get-tuple-element.52), channel_id=1, source_target_pairs={{0,1},{1,0},{2,3},{3,2},{4,5},{5,4},{6,7},{7,6},{8,9},{9,8},{10,11... | collective-permute-start | bytes 589832 | tf_op jit(solution)/shard_map/ppermute | solution.py:45
  16.4 14.6 %collective-permute-start.1 = (bf16[128,768]{1,0:T(8,128)(2,1)}, bf16[128,768]{1,0:T(8,128)(2,1)}, u32[]{:S(2)}, u32[]{:S(2)}) collective-permute-start(bf16[128,768]{1,0:T(8,128)(2,1)} %get-tuple-element.53), channel_id=1, source_target_pairs={{0,2},{1,3},{2,0},{3,1},{4,6},{5,7},{6,4},{7,5},{8,10},{9,11},{10,... | collective-permute-start | bytes 589832 | tf_op jit(solution)/shard_map/ppermute | solution.py:45
  18.1 18.0 %collective-permute-start.2 = (bf16[128,768]{1,0:T(8,128)(2,1)}, bf16[128,768]{1,0:T(8,128)(2,1)}, u32[]{:S(2)}, u32[]{:S(2)}) collective-permute-start(bf16[128,768]{1,0:T(8,128)(2,1)} %get-tuple-element.54), channel_id=1, source_target_pairs={{0,3},{1,2},{2,1},{3,0},{4,7},{5,6},{6,5},{7,4},{8,11},{9,10},{10,... | collective-permute-start | bytes 589832 | tf_op jit(solution)/shard_map/ppermute | solution.py:45
  18.1 18.0 %copy-start.5 = (s32[4]{0:T(128)S(1)}, s32[4]{0:T(128)}, u32[]{:S(2)}) copy-start(s32[4]{0:T(128)} %ids_ref.7) | copy-start | bytes 52
  37.4 15.0 %collective-permute-start.3 = (bf16[2,128,768]{2,1,0:T(8,128)(2,1)S(1)}, bf16[2,128,768]{2,1,0:T(8,128)(2,1)S(1)}, u32[]{:S(2)}, u32[]{:S(2)}) collective-permute-start(bf16[2,128,768]{2,1,0:T(8,128)(2,1)S(1)} %get-tuple-element.64), channel_id=1, source_target_pairs={{0,4},{1,5},{2,6},{3,7},{4,0},{5,1},{6,2},{7,3},{8,12},{9,13},{10,... | collective-permute-start | bytes 1179656 | tf_op jit(solution)/shard_map/ppermute | solution.py:45
  52.4 11.6 %collective-permute-start.4 = (bf16[1,128,768]{2,1,0:T(8,128)(2,1)S(1)}, bf16[1,128,768]{2,1,0:T(8,128)(2,1)S(1)}, u32[]{:S(2)}, u32[]{:S(2)}) collective-permute-start(bf16[1,128,768]{2,1,0:T(8,128)(2,1)S(1)} %slice_add_fusion.2), channel_id=1, source_target_pairs={{0,8},{1,9},{2,10},{3,11},{4,12},{5,13},{6,14},{7,15},{8,0},{9,1},... | collective-permute-start | bytes 589832 | tf_op jit(solution)/shard_map/ppermute | solution.py:45
  64.1 4.9 %copy-start.12 = (bf16[128,768]{1,0:T(8,128)(2,1)S(1)}, bf16[128,768]{1,0:T(8,128)(2,1)}, u32[]{:S(2)}) copy-start(bf16[128,768]{1,0:T(8,128)(2,1)} %copy-done.11) | copy-start | bytes 589828
  64.1 5.4 %copy-start.10 = (bf16[128,768]{1,0:T(8,128)(2,1)S(1)}, bf16[128,768]{1,0:T(8,128)(2,1)}, u32[]{:S(2)}) copy-start(bf16[128,768]{1,0:T(8,128)(2,1)} %copy-done.9) | copy-start | bytes 589828
  64.1 7.0 %copy-start.8 = (bf16[128,768]{1,0:T(8,128)(2,1)S(1)}, bf16[128,768]{1,0:T(8,128)(2,1)}, u32[]{:S(2)}) copy-start(bf16[128,768]{1,0:T(8,128)(2,1)} %copy-done.7) | copy-start | bytes 589828
  64.1 129.9 %all-to-all-start = ((bf16[16,64,2560]{2,1,0:T(8,128)(2,1)}), bf16[16,64,2560]{2,1,0:T(8,128)(2,1)}, u32[]{:S(2)}, u32[]{:S(2)}) async-start(bf16[16,64,2560]{2,1,0:T(8,128)(2,1)} %get-tuple-element.65), calls=%async_computation | async-start | bytes 10485760 | tf_op jit(solution)/shard_map/all_to_all | solution.py:486
  69.0 2.1 collective-permute-start.11
  69.4 36.4 %collective-permute-start.12 = (bf16[128,768]{1,0:T(8,128)(2,1)S(1)}, bf16[128,768]{1,0:T(8,128)(2,1)S(1)}, u32[]{:S(2)}, u32[]{:S(2)}) collective-permute-start(bf16[128,768]{1,0:T(8,128)(2,1)S(1)} %copy-done.10), channel_id=1, source_target_pairs={{0,2},{1,3},{2,0},{3,1},{4,6},{5,7},{6,4},{7,5},{8,10},{9,11},{10,... | collective-permute-start | bytes 589832 | tf_op jit(solution)/shard_map/ppermute | solution.py:45
  71.1 38.3 %collective-permute-start.13 = (bf16[128,768]{1,0:T(8,128)(2,1)S(1)}, bf16[128,768]{1,0:T(8,128)(2,1)S(1)}, u32[]{:S(2)}, u32[]{:S(2)}) collective-permute-start(bf16[128,768]{1,0:T(8,128)(2,1)S(1)} %copy-done.8), channel_id=1, source_target_pairs={{0,3},{1,2},{2,1},{3,0},{4,7},{5,6},{6,5},{7,4},{8,11},{9,10},{10,... | collective-permute-start | bytes 589832 | tf_op jit(solution)/shard_map/ppermute | solution.py:45
  110.1 52.8 %collective-permute-start.14 = (bf16[2,128,768]{2,1,0:T(8,128)(2,1)S(1)}, bf16[2,128,768]{2,1,0:T(8,128)(2,1)S(1)}, u32[]{:S(2)}, u32[]{:S(2)}) collective-permute-start(bf16[2,128,768]{2,1,0:T(8,128)(2,1)S(1)} %get-tuple-element.74), channel_id=1, source_target_pairs={{0,4},{1,5},{2,6},{3,7},{4,0},{5,1},{6,2},{7,3},{8,12},{9,13},{10,... | collective-permute-start | bytes 1179656 | tf_op jit(solution)/shard_map/ppermute | solution.py:45
  110.8 56.7 %collective-permute-start.5 = (f32[256,128]{1,0:T(8,128)S(1)}, f32[256,128]{1,0:T(8,128)S(1)}, u32[]{:S(2)}, u32[]{:S(2)}) collective-permute-start(f32[256,128]{1,0:T(8,128)S(1)} %get-tuple-element.104), channel_id=1, source_target_pairs={{0,1},{1,0},{2,3},{3,2},{4,5},{5,4},{6,7},{7,6},{8,9},{9,8},{10,11... | collective-permute-start | bytes 393224 | tf_op jit(solution)/shard_map/ppermute | solution.py:45
  119.1 48.4 %collective-permute-start.7 = (f32[256,128]{1,0:T(8,128)S(1)}, f32[256,128]{1,0:T(8,128)S(1)}, u32[]{:S(2)}, u32[]{:S(2)}) collective-permute-start(f32[256,128]{1,0:T(8,128)S(1)} %get-tuple-element.105), channel_id=1, source_target_pairs={{0,3},{1,2},{2,1},{3,0},{4,7},{5,6},{6,5},{7,4},{8,11},{9,10},{10,... | collective-permute-start | bytes 393224 | tf_op jit(solution)/shard_map/ppermute | solution.py:45
  119.1 48.4 %collective-permute-start.6 = (f32[256,128]{1,0:T(8,128)S(1)}, f32[256,128]{1,0:T(8,128)S(1)}, u32[]{:S(2)}, u32[]{:S(2)}) collective-permute-start(f32[256,128]{1,0:T(8,128)S(1)} %get-tuple-element.106), channel_id=1, source_target_pairs={{0,2},{1,3},{2,0},{3,1},{4,6},{5,7},{6,4},{7,5},{8,10},{9,11},{10,... | collective-permute-start | bytes 393224 | tf_op jit(solution)/shard_map/ppermute | solution.py:45
  163.0 30.9 %collective-permute-start.15 = (bf16[1,128,768]{2,1,0:T(8,128)(2,1)S(1)}, bf16[1,128,768]{2,1,0:T(8,128)(2,1)S(1)}, u32[]{:S(2)}, u32[]{:S(2)}) collective-permute-start(bf16[1,128,768]{2,1,0:T(8,128)(2,1)S(1)} %slice_add_fusion), channel_id=1, source_target_pairs={{0,8},{1,9},{2,10},{3,11},{4,12},{5,13},{6,14},{7,15},{8,0},{9,1},... | collective-permute-start | bytes 589832 | tf_op jit(solution)/shard_map/ppermute | solution.py:45
  167.6 26.4 %collective-permute-start.10 = (bf16[256,128]{1,0:T(8,128)(2,1)S(1)}, bf16[256,128]{1,0:T(8,128)(2,1)S(1)}, u32[]{:S(2)}, u32[]{:S(2)}) collective-permute-start(bf16[256,128]{1,0:T(8,128)(2,1)S(1)} %add_convert_fusion.1), channel_id=1, source_target_pairs={{0,1},{1,0},{2,3},{3,2},{4,5},{5,4},{6,7},{7,6},{8,9},{9,8},{10,11... | collective-permute-start | bytes 196616 | tf_op jit(solution)/shard_map/ppermute | solution.py:45
  167.6 26.3 %collective-permute-start.9 = (bf16[256,128]{1,0:T(8,128)(2,1)S(1)}, bf16[256,128]{1,0:T(8,128)(2,1)S(1)}, u32[]{:S(2)}, u32[]{:S(2)}) collective-permute-start(bf16[256,128]{1,0:T(8,128)(2,1)S(1)} %add_convert_fusion.1), channel_id=1, source_target_pairs={{0,2},{1,3},{2,0},{3,1},{4,6},{5,7},{6,4},{7,5},{8,10},{9,11},{10,... | collective-permute-start | bytes 196616 | tf_op jit(solution)/shard_map/ppermute | solution.py:45
  169.3 24.7 %collective-permute-start.8 = (bf16[256,128]{1,0:T(8,128)(2,1)S(1)}, bf16[256,128]{1,0:T(8,128)(2,1)S(1)}, u32[]{:S(2)}, u32[]{:S(2)}) collective-permute-start(bf16[256,128]{1,0:T(8,128)(2,1)S(1)} %add_convert_fusion.1), channel_id=1, source_target_pairs={{0,3},{1,2},{2,1},{3,0},{4,7},{5,6},{6,5},{7,4},{8,11},{9,10},{10,... | collective-permute-start | bytes 196616 | tf_op jit(solution)/shard_map/ppermute | solution.py:45
  194.0 26.7 %all-to-all-start.2 = ((bf16[16,64,512]{2,1,0:T(8,128)(2,1)}), bf16[16,64,512]{2,1,0:T(8,128)(2,1)S(1)}, u32[]{:S(2)}, u32[]{:S(2)}) async-start(bf16[16,64,512]{2,1,0:T(8,128)(2,1)} %get-tuple-element.78), calls=%async_computation.2 | async-start | bytes 2097152 | tf_op jit(solution)/shard_map/all_to_all | solution.py:486
  220.7 1.0 copy-start.14
  221.7 54.6 %copy-start.2 = (f32[1,4,64,3072]{3,2,1,0:T(8,128)S(1)}, f32[1,4,64,3072]{3,2,1,0:T(8,128)}, u32[]{:S(2)}) copy-start(f32[1,4,64,3072]{3,2,1,0:T(8,128)} %refs_9_.1) | copy-start | bytes 9437188
  221.7 54.6 %copy-start.3 = (f32[1,4,64,3072]{3,2,1,0:T(8,128)S(1)}, f32[1,4,64,3072]{3,2,1,0:T(8,128)}, u32[]{:S(2)}) copy-start(f32[1,4,64,3072]{3,2,1,0:T(8,128)} %refs_10_.1) | copy-start | bytes 9437188
  225.4 7.4 %collective-permute-start.17 = (f32[256,128]{1,0:T(8,128)S(1)}, f32[256,128]{1,0:T(8,128)S(1)}, u32[]{:S(2)}, u32[]{:S(2)}) collective-permute-start(f32[256,128]{1,0:T(8,128)S(1)} %get-tuple-element.101), channel_id=1, source_target_pairs={{0,1},{1,0},{2,3},{3,2},{4,5},{5,4},{6,7},{7,6},{8,9},{9,8},{10,11... | collective-permute-start | bytes 393224 | tf_op jit(solution)/shard_map/ppermute | solution.py:45
  226.1 6.7 %collective-permute-start.19 = (f32[256,128]{1,0:T(8,128)S(1)}, f32[256,128]{1,0:T(8,128)S(1)}, u32[]{:S(2)}, u32[]{:S(2)}) collective-permute-start(f32[256,128]{1,0:T(8,128)S(1)} %get-tuple-element.102), channel_id=1, source_target_pairs={{0,3},{1,2},{2,1},{3,0},{4,7},{5,6},{6,5},{7,4},{8,11},{9,10},{10,... | collective-permute-start | bytes 393224 | tf_op jit(solution)/shard_map/ppermute | solution.py:45
  227.8 7.0 %collective-permute-start.18 = (f32[256,128]{1,0:T(8,128)S(1)}, f32[256,128]{1,0:T(8,128)S(1)}, u32[]{:S(2)}, u32[]{:S(2)}) collective-permute-start(f32[256,128]{1,0:T(8,128)S(1)} %get-tuple-element.103), channel_id=1, source_target_pairs={{0,2},{1,3},{2,0},{3,1},{4,6},{5,7},{6,4},{7,5},{8,10},{9,11},{10,... | collective-permute-start | bytes 393224 | tf_op jit(solution)/shard_map/ppermute | solution.py:45
  228.2 13.8 %collective-permute-start.23 = (bf16[128,768]{1,0:T(8,128)(2,1)S(1)}, bf16[128,768]{1,0:T(8,128)(2,1)S(1)}, u32[]{:S(2)}, u32[]{:S(2)}) collective-permute-start(bf16[128,768]{1,0:T(8,128)(2,1)S(1)} %constant_dynamic-update-slice_fusion.refs_0_), channel_id=1, source_target_pairs={{0,8},{1,9},{2,10},{3,11},{4,12},{5,13},{6,14},{7,15},{8,0},{9,1},... | collective-permute-start | bytes 589832 | tf_op jit(solution)/shard_map/ppermute | solution.py:45
  234.8 41.6 %copy-start.1 = (f32[1,4,64,3072]{3,2,1,0:T(8,128)S(1)}, f32[1,4,64,3072]{3,2,1,0:T(8,128)}, u32[]{:S(2)}) copy-start(f32[1,4,64,3072]{3,2,1,0:T(8,128)} %refs_8_.1) | copy-start | bytes 9437188
  234.8 5.3 %collective-permute-start.22 = (bf16[256,128]{1,0:T(8,128)(2,1)S(1)}, bf16[256,128]{1,0:T(8,128)(2,1)S(1)}, u32[]{:S(2)}, u32[]{:S(2)}) collective-permute-start(bf16[256,128]{1,0:T(8,128)(2,1)S(1)} %add_convert_fusion.refs_0_), channel_id=1, source_target_pairs={{0,3},{1,2},{2,1},{3,0},{4,7},{5,6},{6,5},{7,4},{8,11},{9,10},{10,... | collective-permute-start | bytes 196616 | tf_op jit(solution)/shard_map/ppermute | solution.py:45
  236.3 4.7 %collective-permute-start.21 = (bf16[256,128]{1,0:T(8,128)(2,1)S(1)}, bf16[256,128]{1,0:T(8,128)(2,1)S(1)}, u32[]{:S(2)}, u32[]{:S(2)}) collective-permute-start(bf16[256,128]{1,0:T(8,128)(2,1)S(1)} %add_convert_fusion.refs_0_), channel_id=1, source_target_pairs={{0,2},{1,3},{2,0},{3,1},{4,6},{5,7},{6,4},{7,5},{8,10},{9,11},{10,... | collective-permute-start | bytes 196616 | tf_op jit(solution)/shard_map/ppermute | solution.py:45
  236.9 4.0 %collective-permute-start.20 = (bf16[256,128]{1,0:T(8,128)(2,1)S(1)}, bf16[256,128]{1,0:T(8,128)(2,1)S(1)}, u32[]{:S(2)}, u32[]{:S(2)}) collective-permute-start(bf16[256,128]{1,0:T(8,128)(2,1)S(1)} %add_convert_fusion.refs_0_), channel_id=1, source_target_pairs={{0,1},{1,0},{2,3},{3,2},{4,5},{5,4},{6,7},{7,6},{8,9},{9,8},{10,11... | collective-permute-start | bytes 196616 | tf_op jit(solution)/shard_map/ppermute | solution.py:45
  236.9 12.6 %collective-permute-start.16 = (bf16[128,768]{1,0:T(8,128)(2,1)S(1)}, bf16[128,768]{1,0:T(8,128)(2,1)S(1)}, u32[]{:S(2)}, u32[]{:S(2)}) collective-permute-start(bf16[128,768]{1,0:T(8,128)(2,1)S(1)} %constant_dynamic-update-slice_fusion.refs_0_), channel_id=1, source_target_pairs={{0,4},{1,5},{2,6},{3,7},{4,0},{5,1},{6,2},{7,3},{8,12},{9,13},{10,... | collective-permute-start | bytes 589832 | tf_op jit(solution)/shard_map/ppermute | solution.py:45
  242.0 9.3 %collective-permute-start.24 = (bf16[128,768]{1,0:T(8,128)(2,1)S(1)}, bf16[128,768]{1,0:T(8,128)(2,1)S(1)}, u32[]{:S(2)}, u32[]{:S(2)}) collective-permute-start(bf16[128,768]{1,0:T(8,128)(2,1)S(1)} %collective-permute-done.23.refs_2_), channel_id=1, source_target_pairs={{0,4},{1,5},{2,6},{3,7},{4,0},{5,1},{6,2},{7,3},{8,12},{9,13},{10,... | collective-permute-start | bytes 589832 | tf_op jit(solution)/shard_map/ppermute | solution.py:45
  245.1 12.1 %collective-permute-start.28 = (bf16[128,768]{1,0:T(8,128)(2,1)S(1)}, bf16[128,768]{1,0:T(8,128)(2,1)S(1)}, u32[]{:S(2)}, u32[]{:S(2)}) collective-permute-start(bf16[128,768]{1,0:T(8,128)(2,1)S(1)} %slots.1.refs_0_), channel_id=1, source_target_pairs={{0,12},{1,13},{2,14},{3,15},{4,8},{5,9},{6,10},{7,11},{8,4},{9,5},... | collective-permute-start | bytes 589832 | tf_op jit(solution)/shard_map/ppermute | solution.py:45
  247.2 16.9 %collective-permute-start.27 = (bf16[128,768]{1,0:T(8,128)(2,1)S(1)}, bf16[128,768]{1,0:T(8,128)(2,1)S(1)}, u32[]{:S(2)}, u32[]{:S(2)}) collective-permute-start(bf16[128,768]{1,0:T(8,128)(2,1)S(1)} %slots.1.refs_0_), channel_id=1, source_target_pairs={{0,8},{1,9},{2,10},{3,11},{4,12},{5,13},{6,14},{7,15},{8,0},{9,1},... | collective-permute-start | bytes 589832 | tf_op jit(solution)/shard_map/ppermute | solution.py:45
  247.2 16.9 %collective-permute-start.26 = (bf16[128,768]{1,0:T(8,128)(2,1)S(1)}, bf16[128,768]{1,0:T(8,128)(2,1)S(1)}, u32[]{:S(2)}, u32[]{:S(2)}) collective-permute-start(bf16[128,768]{1,0:T(8,128)(2,1)S(1)} %slots.1.refs_0_), channel_id=1, source_target_pairs={{0,4},{1,5},{2,6},{3,7},{4,0},{5,1},{6,2},{7,3},{8,12},{9,13},{10,... | collective-permute-start | bytes 589832 | tf_op jit(solution)/shard_map/ppermute | solution.py:45
  252.4 11.7 %collective-permute-start.25 = (bf16[128,768]{1,0:T(8,128)(2,1)S(1)}, bf16[128,768]{1,0:T(8,128)(2,1)S(1)}, u32[]{:S(2)}, u32[]{:S(2)}) collective-permute-start(bf16[128,768]{1,0:T(8,128)(2,1)S(1)} %get-tuple-element.84), channel_id=1, source_target_pairs={{0,1},{1,0},{2,3},{3,2},{4,5},{5,4},{6,7},{7,6},{8,9},{9,8},{10,11... | collective-permute-start | bytes 589832 | tf_op jit(solution)/shard_map/ppermute | solution.py:45
  252.5 15.3 %collective-permute-start.29 = (bf16[128,768]{1,0:T(8,128)(2,1)S(1)}, bf16[128,768]{1,0:T(8,128)(2,1)S(1)}, u32[]{:S(2)}, u32[]{:S(2)}) collective-permute-start(bf16[128,768]{1,0:T(8,128)(2,1)S(1)} %get-tuple-element.87), channel_id=1, source_target_pairs={{0,2},{1,3},{2,0},{3,1},{4,6},{5,7},{6,4},{7,5},{8,10},{9,11},{10,... | collective-permute-start | bytes 589832 | tf_op jit(solution)/shard_map/ppermute | solution.py:45
  257.2 10.6 %collective-permute-start.30 = (bf16[128,768]{1,0:T(8,128)(2,1)S(1)}, bf16[128,768]{1,0:T(8,128)(2,1)S(1)}, u32[]{:S(2)}, u32[]{:S(2)}) collective-permute-start(bf16[128,768]{1,0:T(8,128)(2,1)S(1)} %get-tuple-element.88), channel_id=1, source_target_pairs={{0,3},{1,2},{2,1},{3,0},{4,7},{5,6},{6,5},{7,4},{8,11},{9,10},{10,... | collective-permute-start | bytes 589832 | tf_op jit(solution)/shard_map/ppermute | solution.py:45
  265.2 2.6 collective-permute-start.31
  265.3 7.8 %collective-permute-start.32 = (bf16[128,768]{1,0:T(8,128)(2,1)S(1)}, bf16[128,768]{1,0:T(8,128)(2,1)S(1)}, u32[]{:S(2)}, u32[]{:S(2)}) collective-permute-start(bf16[128,768]{1,0:T(8,128)(2,1)S(1)} %get-tuple-element.95), channel_id=1, source_target_pairs={{0,2},{1,3},{2,0},{3,1},{4,6},{5,7},{6,4},{7,5},{8,10},{9,11},{10,... | collective-permute-start | bytes 589832 | tf_op jit(solution)/shard_map/ppermute | solution.py:45
  267.0 9.4 %collective-permute-start.33 = (bf16[128,768]{1,0:T(8,128)(2,1)S(1)}, bf16[128,768]{1,0:T(8,128)(2,1)S(1)}, u32[]{:S(2)}, u32[]{:S(2)}) collective-permute-start(bf16[128,768]{1,0:T(8,128)(2,1)S(1)} %get-tuple-element.96), channel_id=1, source_target_pairs={{0,3},{1,2},{2,1},{3,0},{4,7},{5,6},{6,5},{7,4},{8,11},{9,10},{10,... | collective-permute-start | bytes 589832 | tf_op jit(solution)/shard_map/ppermute | solution.py:45
  (4 other events, 2.8 us)
